TPU v7x, 32 devices: a whole 2x2x4 slice. The times are simulated.
32 devices in a mesh: dp: 8 (over y, x, core), mp: 4 (over z).
Axes of the slice: x: 2, y: 2, z: 4, core: 2. Of those that a mesh axis runs over, the one named last changes fastest.
Arguments:
- tokens: bfloat16 [2, 16, 512, 768], P(None, 'dp', 'mp'), may hold values from -6 to 6
- prev_logits: bfloat16 [2, 16, 12, 512, 512], P(None, 'dp', 'mp'), may hold values from -6 to 6
- segment_ids: int32 [2, 16, 512], P(None, 'dp'), may hold values from 0 to 3, as said below
- query_weight: bfloat16 [768, 768], P(None, 'mp'), may hold values from -0.21875 to 0.21875
- key_weight: bfloat16 [768, 768], P(None, 'mp'), may hold values from -0.21875 to 0.21875
- value_weight: bfloat16 [768, 768], P(None, 'mp'), may hold values from -0.21875 to 0.21875
- query_bias: float32 [768], P('mp'), may hold values from -1.8 to 1.8
- value_bias: float32 [768], P('mp'), may hold values from -1.8 to 1.8
- output_projection_weight: bfloat16 [768, 768], P('mp'), may hold values from -1.75 to 1.75
- output_bias: float32 [768], replicated, may hold values from -1.8 to 1.8
- first_gain: float32 [768], replicated, may hold values from 0.5 to 1.5
- first_shift: float32 [768], replicated, may hold values from -1.8 to 1.8
- inner_projection_weight: bfloat16 [768, 3072], P(None, 'mp'), may hold values from -0.21875 to 0.21875
- inner_bias: float32 [3072], P('mp'), may hold values from -1.8 to 1.8
- down_projection_weight: bfloat16 [3072, 768], P('mp'), may hold values from -0.21875 to 0.21875
- down_bias: float32 [768], replicated, may hold values from -1.8 to 1.8
- second_gain: float32 [768], replicated, may hold values from 0.5 to 1.5
- second_shift: float32 [768], replicated, may hold values from -1.8 to 1.8
- output_cot: bfloat16 [2, 16, 512, 768], P(None, 'dp', 'mp'), may hold values from -6 to 6
- logit_cot: bfloat16 [2, 16, 12, 512, 512], P(None, 'dp', 'mp'), may hold values from -1.5 to 1.5
Outputs:
- layer_output: bfloat16 [2, 16, 512, 768], P(None, 'dp', 'mp')
- new_logits: bfloat16 [2, 16, 12, 512, 512], P(None, 'dp', 'mp')
- tokens_grad: float32 [2, 16, 512, 768], P(None, 'dp', 'mp')
- prev_grad: float32 [2, 16, 12, 512, 512], P(None, 'dp', 'mp')
- query_weight_grad: float32 [768, 768], P(None, 'mp')
- key_weight_grad: float32 [768, 768], P(None, 'mp')
- value_weight_grad: float32 [768, 768], P(None, 'mp')
- query_bias_grad: float32 [768], P('mp')
- value_bias_grad: float32 [768], P('mp')
- output_weight_grad: float32 [768, 768], P('mp')
- output_bias_grad: float32 [768], replicated
- first_gain_grad: float32 [768], replicated
- first_shift_grad: float32 [768], replicated
- inner_weight_grad: float32 [768, 3072], P(None, 'mp')
- inner_bias_grad: float32 [3072], P('mp')
- down_weight_grad: float32 [3072, 768], P('mp')
- down_bias_grad: float32 [768], replicated
- second_gain_grad: float32 [768], replicated
- second_shift_grad: float32 [768], replicated
Inputs may be any that keep to these rules, and one draw needn't show every extreme that they name: `segment_ids`: segment ids never decrease along a slot; each slot's ids start at 0 and end at 3.
All inputs are finite; a program needn't handle non-finite values.
Results may differ from a plain program's by a relative error of at most 0.017.
Values may be sent and summed in bfloat16 or wider, within the bound.
No kernel may reach another device: no remote copies, remote signals or barrier semaphores. Data moves between devices by JAX's collectives and lax.ppermute only.
A program may use at most 192 MiB of HBM per device.

v0:
```python
import math

import jax
import jax.numpy as jnp
from jax import lax
from jax.sharding import PartitionSpec as P

EPSILON = 1e-12
REAL_NUMBER_TYPE = jnp.float32
BRAIN = jnp.bfloat16


def norm_rows(values_in, gain_vec, shift_vec):
    row_mean = jnp.mean(values_in, -1, keepdims=True)
    centered = values_in - row_mean
    variance = jnp.mean(centered * centered, -1, keepdims=True)
    return centered * lax.rsqrt(variance + EPSILON) * gain_vec + shift_vec


def gelu_exact(value_in):
    return jax.nn.gelu(value_in, approximate=False)


def masked_scores(query_heads, key_heads, previous, segments, score_scale):
    raw_dots = jnp.einsum(
        "sqhe,skhe->shqk", query_heads, key_heads, preferred_element_type=REAL_NUMBER_TYPE
    )
    scores = raw_dots * score_scale + previous.astype(REAL_NUMBER_TYPE)
    same_doc = (segments[:, :, None] == segments[:, None, :])[:, None]
    return (scores, jnp.where(same_doc, scores, -1e30))


def on_device(
    tokens,
    prev_logits,
    segment_ids,
    query_weight,
    key_weight,
    value_weight,
    query_bias,
    value_bias,
    output_projection_weight,
    output_bias,
    first_gain,
    first_shift,
    inner_projection_weight,
    inner_bias,
    down_projection_weight,
    down_bias,
    second_gain,
    second_shift,
    output_cot,
    logit_cot,
):
    micro_count = tokens.shape[0]
    slot_count = tokens.shape[1]
    heads_here = prev_logits.shape[2]
    length = prev_logits.shape[3]
    head_width = query_weight.shape[1]
    head_size = head_width // heads_here
    score_scale = 1.0 / math.sqrt(head_size)
    combined_weight = jnp.concatenate([query_weight, key_weight, value_weight], 1)
    big_total = None
    small_total = None
    layer_list = []
    logit_list = []
    token_grad_list = []
    prev_grad_list = []
    for batch_index in range(micro_count):
        token_rows = tokens[batch_index]
        segments = segment_ids[batch_index]
        previous = prev_logits[batch_index]
        complete_rows = lax.all_gather(token_rows, "mp", axis=1, tiled=True)
        projected = jnp.einsum(
            "kpb,bf->kpf", complete_rows, combined_weight, preferred_element_type=REAL_NUMBER_TYPE
        )
        query_rows = (projected[..., :head_width] + query_bias).astype(BRAIN)
        key_rows = projected[..., head_width : 2 * head_width].astype(BRAIN)
        value_rows = (projected[..., 2 * head_width :] + value_bias).astype(BRAIN)
        query_heads = query_rows.reshape(slot_count, length, heads_here, head_size)
        key_heads = key_rows.reshape(slot_count, length, heads_here, head_size)
        value_heads = value_rows.reshape(slot_count, length, heads_here, head_size)
        scores, masked = masked_scores(query_heads, key_heads, previous, segments, score_scale)
        logit_list.append(scores.astype(BRAIN))
        row_top = jnp.max(masked, -1, keepdims=True)
        exponent = jnp.exp(masked - row_top)
        row_total = jnp.sum(exponent, -1, keepdims=True)
        log_total = row_top + jnp.log(row_total)
        soft_low = (exponent / row_total).astype(BRAIN)
        context_vectors = jnp.einsum(
            "shqk,skhe->sqhe", soft_low, value_heads, preferred_element_type=REAL_NUMBER_TYPE
        )
        context_vectors = context_vectors.astype(BRAIN).reshape(slot_count, length, head_width)
        output_piece = jnp.einsum(
            "xha,ag->xhg",
            context_vectors,
            output_projection_weight,
            preferred_element_type=REAL_NUMBER_TYPE,
        )
        attended = (
            lax.psum_scatter(output_piece, "mp", scatter_dimension=1, tiled=True) + output_bias
        )
        residual = token_rows.astype(REAL_NUMBER_TYPE) + attended
        hidden, first_pull = jax.vjp(norm_rows, residual, first_gain, first_shift)
        hidden_low = hidden.astype(BRAIN)
        hidden_state_rows = lax.all_gather(hidden_low, "mp", axis=1, tiled=True)
        inner_pre = (
            jnp.einsum(
                "tjp,py->tjy",
                hidden_state_rows,
                inner_projection_weight,
                preferred_element_type=REAL_NUMBER_TYPE,
            )
            + inner_bias
        )
        activated, gelu_pull = jax.vjp(gelu_exact, inner_pre)
        activated_reduced = activated.astype(BRAIN)
        down_weight_piece = jnp.einsum(
            "vnr,rm->vnm",
            activated_reduced,
            down_projection_weight,
            preferred_element_type=REAL_NUMBER_TYPE,
        )
        branch = (
            lax.psum_scatter(down_weight_piece, "mp", scatter_dimension=1, tiled=True) + down_bias
        )
        layer_out, second_pull = jax.vjp(norm_rows, hidden + branch, second_gain, second_shift)
        layer_list.append(layer_out.astype(BRAIN))
        d_second, second_gain_part, second_shift_part = second_pull(
            output_cot[batch_index].astype(REAL_NUMBER_TYPE)
        )
        down_bias_part = jnp.sum(d_second, (0, 1))
        residual_branch_rows = lax.all_gather(d_second.astype(BRAIN), "mp", axis=1, tiled=True)
        down_weight_part = jnp.einsum(
            "mpv,mph->vh",
            activated_reduced,
            residual_branch_rows,
            preferred_element_type=REAL_NUMBER_TYPE,
        )
        d_activated = jnp.einsum(
            "ncw,aw->nca",
            residual_branch_rows,
            down_projection_weight,
            preferred_element_type=REAL_NUMBER_TYPE,
        ).astype(BRAIN)
        (d_inner,) = gelu_pull(d_activated.astype(REAL_NUMBER_TYPE))
        inner_bias_part = jnp.sum(d_inner, (0, 1))
        inner_gradient_reduced = d_inner.astype(BRAIN)
        inner_weight_part = jnp.einsum(
            "hcp,hcx->px",
            hidden_state_rows,
            inner_gradient_reduced,
            preferred_element_type=REAL_NUMBER_TYPE,
        )
        back_hidden = jnp.einsum(
            "rnv,ev->rne",
            inner_gradient_reduced,
            inner_projection_weight,
            preferred_element_type=REAL_NUMBER_TYPE,
        )
        d_hidden = d_second + lax.psum_scatter(back_hidden, "mp", scatter_dimension=1, tiled=True)
        d_residual, first_gain_part, first_shift_part = first_pull(d_hidden)
        output_bias_part = jnp.sum(d_residual, (0, 1))
        attention_result_rows = lax.all_gather(d_residual.astype(BRAIN), "mp", axis=1, tiled=True)
        output_weight_part = jnp.einsum(
            "rzw,rzx->wx",
            context_vectors,
            attention_result_rows,
            preferred_element_type=REAL_NUMBER_TYPE,
        )
        d_context = jnp.einsum(
            "fnu,mu->fnm",
            attention_result_rows,
            output_projection_weight,
            preferred_element_type=REAL_NUMBER_TYPE,
        ).astype(BRAIN)
        context_heads = d_context.reshape(slot_count, length, heads_here, head_size)
        scores_again, masked_again = masked_scores(
            query_heads, key_heads, previous, segments, score_scale
        )
        soft_again = jnp.exp(masked_again - log_total)
        d_soft = jnp.einsum(
            "sqhe,skhe->shqk", context_heads, value_heads, preferred_element_type=REAL_NUMBER_TYPE
        )
        d_soft = d_soft.astype(BRAIN).astype(REAL_NUMBER_TYPE)
        row_delta = jnp.sum(soft_again * d_soft, -1, keepdims=True)
        d_scores = soft_again * (d_soft - row_delta) + logit_cot[batch_index].astype(
            REAL_NUMBER_TYPE
        )
        prev_grad_list.append(d_scores)
        d_dots = (d_scores * score_scale).astype(BRAIN)
        d_query = jnp.einsum(
            "shqk,skhe->sqhe", d_dots, key_heads, preferred_element_type=REAL_NUMBER_TYPE
        )
        d_keys = jnp.einsum(
            "shqk,sqhe->skhe", d_dots, query_heads, preferred_element_type=REAL_NUMBER_TYPE
        )
        d_values = jnp.einsum(
            "shqk,sqhe->skhe", soft_low, context_heads, preferred_element_type=REAL_NUMBER_TYPE
        )
        d_query = d_query.astype(BRAIN).reshape(slot_count, length, head_width)
        d_keys = d_keys.astype(BRAIN).reshape(slot_count, length, head_width)
        d_values = d_values.astype(BRAIN).reshape(slot_count, length, head_width)
        combined_gradient = jnp.concatenate([d_query, d_keys, d_values], -1)
        combined_piece = jnp.einsum(
            "irn,irb->nb", complete_rows, combined_gradient, preferred_element_type=REAL_NUMBER_TYPE
        )
        query_bias_part = jnp.sum(d_query.astype(REAL_NUMBER_TYPE), (0, 1))
        value_bias_part = jnp.sum(d_values.astype(REAL_NUMBER_TYPE), (0, 1))
        back_tokens = jnp.einsum(
            "iox,jx->ioj",
            combined_gradient,
            combined_weight,
            preferred_element_type=REAL_NUMBER_TYPE,
        )
        token_grad_list.append(
            d_residual
            + lax.psum_scatter(
                back_tokens.astype(jnp.bfloat16), "mp", scatter_dimension=1, tiled=True
            ).astype(jnp.float32)
        )
        micro_big = (
            combined_piece,
            query_bias_part,
            value_bias_part,
            output_weight_part,
            inner_weight_part,
            inner_bias_part,
            down_weight_part,
        )
        micro_small = (
            output_bias_part,
            first_gain_part,
            first_shift_part,
            down_bias_part,
            second_gain_part,
            second_shift_part,
        )
        if batch_index == 0:
            big_total = micro_big
            small_total = micro_small
        else:
            big_total = jax.tree.map(jnp.add, big_total, micro_big)
            small_total = jax.tree.map(jnp.add, small_total, micro_small)
    small_total = tuple(lax.psum(small_total, "mp"))
    summed = tuple(lax.psum(big_total + small_total, "dp"))
    big_total = summed[:7]
    small_total = summed[7:]
    joined_grad = big_total[0]
    return (
        jnp.stack(layer_list),
        jnp.stack(logit_list),
        jnp.stack(token_grad_list),
        jnp.stack(prev_grad_list),
        joined_grad[:, :head_width],
        joined_grad[:, head_width : 2 * head_width],
        joined_grad[:, 2 * head_width :],
        big_total[1],
        big_total[2],
        big_total[3],
        small_total[0],
        small_total[1],
        small_total[2],
        big_total[4],
        big_total[5],
        big_total[6],
        small_total[3],
        small_total[4],
        small_total[5],
    )


def solution(mesh):
    in_specs = (
        P(None, "dp", "mp", None),
        P(None, "dp", "mp", None, None),
        P(None, "dp", None),
        P(None, "mp"),
        P(None, "mp"),
        P(None, "mp"),
        P("mp"),
        P("mp"),
        P("mp", None),
        P(),
        P(),
        P(),
        P(None, "mp"),
        P("mp"),
        P("mp", None),
        P(),
        P(),
        P(),
        P(None, "dp", "mp", None),
        P(None, "dp", "mp", None, None),
    )
    out_specs = (
        P(None, "dp", "mp", None),
        P(None, "dp", "mp", None, None),
        P(None, "dp", "mp", None),
        P(None, "dp", "mp", None, None),
        P(None, "mp"),
        P(None, "mp"),
        P(None, "mp"),
        P("mp"),
        P("mp"),
        P("mp", None),
        P(),
        P(),
        P(),
        P(None, "mp"),
        P("mp"),
        P("mp", None),
        P(),
        P(),
        P(),
    )
    return jax.shard_map(
        on_device, mesh=mesh, in_specs=in_specs, out_specs=out_specs, check_vma=False
    )
```

profile of v0, /device:TPU:0, one launch (start us, length us, event | category | flops | bytes accessed | tf_op | source)
XLA Modules:
  0.0 945.3 jit_solution(11863445057691197603)
XLA Ops:
  10.2 6.0 fusion.124
  16.2 4.8 copy.70
  21.8 28.2 %all-gather.25.cloned.1.call-done = bf16[1,2,512,768]{3,2,1,0:T(8,128)(2,1)} async-done(((bf16[1,2,128,768]{3,2,1,0:T(8,128)(2,1)}), bf16[1,2,512,768]{3,2,1,0:T(8,128)(2,1)}) %all-gather.25.cloned.1.call-update) | async-done | bytes 1572880 | tf_op jit(solution)/shard_map/all_gather | solution.py:73
  54.0 34.1 %all-gather.23.cloned.1.call-done = bf16[1,2,512,768]{3,2,1,0:T(8,128)(2,1)} async-done(((bf16[1,2,128,768]{3,2,1,0:T(8,128)(2,1)}), bf16[1,2,512,768]{3,2,1,0:T(8,128)(2,1)}) %all-gather.23.cloned.1.call-update) | async-done | bytes 1572880 | tf_op jit(solution)/shard_map/all_gather | solution.py:73
  126.9 38.8 %reduce-scatter.13.cloned.1.call-done = f32[2,128,768]{2,1,0:T(8,128)} async-done(((f32[2,512,768]{2,1,0:T(8,128)}), f32[2,128,768]{2,1,0:T(8,128)}) %reduce-scatter.13.cloned.1.call-update) | async-done | bytes 786448 | tf_op jit(solution)/shard_map/reduce_scatter | solution.py:101
  165.7 62.5 %reduce-scatter.9.cloned.1.call-done = f32[2,128,768]{2,1,0:T(8,128)} async-done(((f32[2,512,768]{2,1,0:T(8,128)}), f32[2,128,768]{2,1,0:T(8,128)}) %reduce-scatter.9.cloned.1.call-update) | async-done | bytes 786448 | tf_op jit(solution)/shard_map/reduce_scatter | solution.py:101
  233.7 36.4 %all-gather.13.cloned.1.call-done = bf16[2,512,768]{2,1,0:T(8,128)(2,1)} async-done(((bf16[2,128,768]{2,1,0:T(8,128)(2,1)}), bf16[2,512,768]{2,1,0:T(8,128)(2,1)}) %all-gather.13.cloned.1.call-update) | async-done | bytes 1572880 | tf_op jit(solution)/shard_map/all_gather | solution.py:106
  274.6 33.5 %all-gather.11.cloned.1.call-done = bf16[2,512,768]{2,1,0:T(8,128)(2,1)} async-done(((bf16[2,128,768]{2,1,0:T(8,128)(2,1)}), bf16[2,512,768]{2,1,0:T(8,128)(2,1)}) %all-gather.11.cloned.1.call-update) | async-done | bytes 1572880 | tf_op jit(solution)/shard_map/all_gather | solution.py:106
  308.1 5.6 fusion.87
  313.8 15.7 %multiply_convert_fusion.3 = (bf16[2,512,768]{2,1,0:T(8,128)(2,1)S(1)}, f32[2,512,768]{2,1,0:T(8,128)}, bf16[2,512,768]{2,1,0:T(8,128)(2,1)}, f32[2,512,768]{2,1,0:T(8,128)}) fusion(f32[2,512,768]{2,1,0:T(8,128)S(1)} %get-tuple-element.148, f32[768]{0:T(1024)S(1)} %copy-done.122, u8[512,768]{1,0:T(8,128)(4,1)S(1)} %get-tuple-element.39, ...), kind=kLoop, calls=%fused_computation.74 | loop fusion | flops 110886912 | bytes 17304576 | tf_op jit(solution)/shard_map/convert_element_type | solution.py:117
  333.7 4.8 fusion.52
  338.6 54.4 %reduce-scatter.11.cloned.1.call-done = f32[2,128,768]{2,1,0:T(8,128)} async-done(((f32[2,512,768]{2,1,0:T(8,128)}), f32[2,128,768]{2,1,0:T(8,128)}) %reduce-scatter.11.cloned.1.call-update) | async-done | bytes 786448 | tf_op jit(solution)/shard_map/reduce_scatter | solution.py:125
  393.0 62.6 %reduce-scatter.15.cloned.1.call-done = f32[2,128,768]{2,1,0:T(8,128)} async-done(((f32[2,512,768]{2,1,0:T(8,128)}), f32[2,128,768]{2,1,0:T(8,128)}) %reduce-scatter.15.cloned.1.call-update) | async-done | bytes 786448 | tf_op jit(solution)/shard_map/reduce_scatter | solution.py:125
  462.8 36.2 %all-gather.19.cloned.1.call-done = bf16[2,512,768]{2,1,0:T(8,128)(2,1)} async-done(((bf16[2,128,768]{2,1,0:T(8,128)(2,1)}), bf16[2,512,768]{2,1,0:T(8,128)(2,1)}) %all-gather.19.cloned.1.call-update) | async-done | bytes 1572880 | tf_op jit(solution)/shard_map/all_gather | solution.py:133
  499.0 6.4 fusion.128
  509.8 27.2 %all-gather.15.cloned.1.call-done = bf16[2,512,768]{2,1,0:T(8,128)(2,1)} async-done(((bf16[2,128,768]{2,1,0:T(8,128)(2,1)}), bf16[2,512,768]{2,1,0:T(8,128)(2,1)}) %all-gather.15.cloned.1.call-update) | async-done | bytes 1572880 | tf_op jit(solution)/shard_map/all_gather | solution.py:133
  537.0 6.4 fusion.127
  547.8 50.6 %reduce-scatter.21.cloned.1.call-done = f32[2,128,768]{2,1,0:T(8,128)} async-done(((f32[2,512,768]{2,1,0:T(8,128)}), f32[2,128,768]{2,1,0:T(8,128)}) %reduce-scatter.21.cloned.1.call-update) | async-done | bytes 786448 | tf_op jit(solution)/shard_map/reduce_scatter | solution.py:161
  601.9 59.0 %reduce-scatter.17.cloned.1.call-done = f32[2,128,768]{2,1,0:T(8,128)} async-done(((f32[2,512,768]{2,1,0:T(8,128)}), f32[2,128,768]{2,1,0:T(8,128)}) %reduce-scatter.17.cloned.1.call-update) | async-done | bytes 786448 | tf_op jit(solution)/shard_map/reduce_scatter | solution.py:161
  666.5 5.8 fusion.123
  672.3 4.7 copy.71
  683.5 20.1 %all-gather.17.cloned.1.call-done = bf16[2,512,768]{2,1,0:T(8,128)(2,1)} async-done(((bf16[2,128,768]{2,1,0:T(8,128)(2,1)}), bf16[2,512,768]{2,1,0:T(8,128)(2,1)}) %all-gather.17.cloned.1.call-update) | async-done | bytes 1572880 | tf_op jit(solution)/shard_map/all_gather | solution.py:164
  712.4 10.8 %fusion.3 = f32[2,3,512,512]{2,3,1,0:T(8,128)S(1)} fusion(bf16[2,3,512,512]{2,3,1,0:T(8,128)(2,1)} %convolution_convert_fusion.1, f32[2,3,512,512]{2,3,1,0:T(8,128)} %copy-done.3, bf16[1,2,3,512,512]{3,4,2,1,0:T(8,128)(2,1)S(1)} %copy-done.41, f32[2,3,512]{2,1,0:T(4,128)S(1)} %log_add_fusion.1, pred[2,512,512]{1,2,0:T(8,128)(4,1)S(1)} %copy-done.17), kind=kOutput, calls=%fused_computation.8 | output fusion | flops 17305088 | bytes 19410944 | tf_op jit(solution)/shard_map/sub | solution.py:187
  729.9 11.7 %all-gather.21.cloned.1.call-done = bf16[2,512,768]{2,1,0:T(8,128)(2,1)} async-done(((bf16[2,128,768]{2,1,0:T(8,128)(2,1)}), bf16[2,512,768]{2,1,0:T(8,128)(2,1)}) %all-gather.21.cloned.1.call-update) | async-done | bytes 1572880 | tf_op jit(solution)/shard_map/all_gather | solution.py:164
  749.7 9.8 %fusion.5 = f32[2,3,512,512]{2,3,1,0:T(8,128)} fusion(bf16[2,3,512,512]{2,3,1,0:T(8,128)(2,1)} %convolution_convert_fusion, f32[2,3,512,512]{2,3,1,0:T(8,128)S(1)} %bitcast.246, bf16[1,2,3,512,512]{3,4,2,1,0:T(8,128)(2,1)S(1)} %copy-done.40, f32[2,3,512]{2,1,0:T(4,128)S(1)} %log_add_fusion, pred[2,512,512]{1,2,0:T(8,128)(4,1)S(1)} %copy-done.15), kind=kOutput, calls=%fused_computation.10 | output fusion | flops 17305088 | bytes 19410944 | tf_op jit(solution)/shard_map/sub | solution.py:187
  787.2 6.1 pad_maximum_fusion.1
  793.5 8.8 copy.55
  803.4 18.1 %all-reduce.2 = (f32[768]{0:T(1024)S(1)}, f32[768]{0:T(1024)S(1)}, f32[768]{0:T(1024)S(1)}, f32[768]{0:T(1024)S(1)}, f32[768]{0:T(1024)S(1)}, /*index=5*/f32[768]{0:T(1024)S(1)}) all-reduce(f32[768]{0:T(1024)S(1)} %add.340, f32[768]{0:T(1024)S(1)} %add.341, f32[768]{0:T(1024)S(1)} %add.342, ...), channel_id=1, replica_groups=mesh['dp'=8,'mp'=4] {'mp'}, use_global_device_ids=true, to_apply=%region_40.41 | all-reduce | flops 4608 | bytes 36864 | tf_op jit(solution)/shard_map/psum | solution.py:245
  821.7 12.0 %pad_maximum_fusion = f32[2,2,3,512,512]{3,4,2,1,0:T(8,128)} fusion(f32[1,2,3,512,512]{3,4,2,1,0:T(8,128)} %bitcast.248, f32[1,2,3,512,512]{3,4,2,1,0:T(8,128)} %bitcast.247), kind=kLoop, calls=%fused_computation.2 | loop fusion | flops 3145728 | bytes 25165824 | tf_op jit(solution)/shard_map/stack | solution.py:254
  833.7 12.9 %copy.56 = f32[2,2,3,512,512]{4,3,2,1,0:T(8,128)} copy(f32[2,2,3,512,512]{3,4,2,1,0:T(8,128)} %pad_maximum_fusion) | data formatting | bytes 25165824
  846.6 23.8 %all-reduce = (f32[192]{0:T(256)}, f32[192]{0:T(256)}, f32[768]{0:T(1024)}, f32[768]{0:T(1024)}, f32[768]{0:T(1024)}, /*index=5*/f32[768]{0:T(1024)}, f32[768]{0:T(1024)}, f32[768]{0:T(1024)}, f32[768]{0:T(1024)}) all-reduce(f32[192]{0:T(256)S(1)} %add.336, f32[192]{0:T(256)S(1)} %add.338, ...), channel_id=1, replica_groups=mesh['dp'=8,'mp'=4] {'dp'}, use_global_device_ids=true, to_apply=%region_33.34 | all-reduce | flops 5760 | bytes 46080 | tf_op jit(solution)/shard_map/psum | solution.py:246
  874.1 57.8 %all-reduce.5.cloned.1.call-done = (f32[768,576]{0,1:T(8,128)}, f32[192,768]{1,0:T(8,128)}, f32[768,768]{1,0:T(8,128)}, f32[768,768]{1,0:T(8,128)}) async-done(((f32[768,576]{0,1:T(8,128)}, f32[192,768]{1,0:T(8,128)}, f32[768,768]{1,0:T(8,128)}, f32[768,768]{1,0:T(8,128)}), (f32[768,576]{0,1:T(8,128)}, f32[192,768]{1,0:T(8,128)}, f32[768,768]{1,0:T(8,128)}, ...) | async-done | bytes 7077904 | tf_op jit(solution)/shard_map/psum | solution.py:246
  (428 shorter events, 153.4 us)
Async XLA Ops:
  7.2 262.9 %copy-start = (bf16[768,768]{1,0:T(8,128)(2,1)S(1)}, bf16[768,768]{1,0:T(8,128)(2,1)}, u32[]{:S(2)}) copy-start(bf16[768,768]{1,0:T(8,128)(2,1)} %param.32) | copy-start | bytes 3538948
  7.2 42.8 %all-gather.25.cloned.1.call-start = ((), (), s32[]{:S(2)}) async-start(), calls=%async_computation.23 | async-start | bytes 1966080 | tf_op jit(solution)/shard_map/all_gather | solution.py:73
  9.4 78.7 %all-gather.23.cloned.1.call-start = ((), (), s32[]{:S(2)}) async-start(), calls=%async_computation.22 | async-start | bytes 1966080 | tf_op jit(solution)/shard_map/all_gather | solution.py:73
  10.2 155.5 %reduce-scatter.13.cloned.1.call-start = ((), (), s32[]{:S(2)}) async-start(), calls=%async_computation.11 | async-start | bytes 3932160 | tf_op jit(solution)/shard_map/reduce_scatter | solution.py:101
  21.7 77.8 %copy-start.14 = (pred[2,512,512]{1,2,0:T(8,128)(4,1)}, pred[2,512,512]{1,2,0:T(8,128)(4,1)S(1)}, u32[]{:S(2)}) copy-start(pred[2,512,512]{1,2,0:T(8,128)(4,1)S(1)} %get-tuple-element.161) | copy-start | bytes 1572868
  21.7 98.2 %copy-start.16 = (pred[2,512,512]{1,2,0:T(8,128)(4,1)}, pred[2,512,512]{1,2,0:T(8,128)(4,1)S(1)}, u32[]{:S(2)}) copy-start(pred[2,512,512]{1,2,0:T(8,128)(4,1)S(1)} %get-tuple-element.162) | copy-start | bytes 1572868
  106.4 121.7 %reduce-scatter.9.cloned.1.call-start = ((), (), s32[]{:S(2)}) async-start(), calls=%async_computation.8 | async-start | bytes 3932160 | tf_op jit(solution)/shard_map/reduce_scatter | solution.py:101
  124.6 103.6 %copy-start.42 = (bf16[2,2,128,768]{3,2,1,0:T(8,128)(2,1)S(1)}, bf16[2,2,128,768]{3,2,1,0:T(8,128)(2,1)}, u32[]{:S(2)}) copy-start(bf16[2,2,128,768]{3,2,1,0:T(8,128)(2,1)} %param.20) | copy-start | bytes 2359300
  126.9 143.2 %all-gather.13.cloned.1.call-start = ((), (), s32[]{:S(2)}) async-start(), calls=%async_computation.12 | async-start | bytes 1966080 | tf_op jit(solution)/shard_map/all_gather | solution.py:106
  232.8 75.3 %all-gather.11.cloned.1.call-start = ((), (), s32[]{:S(2)}) async-start(), calls=%async_computation.9 | async-start | bytes 1966080 | tf_op jit(solution)/shard_map/all_gather | solution.py:106
  233.4 74.7 %copy-start.122 = (f32[768]{0:T(1024)S(1)}, f32[768]{0:T(1024)}, u32[]{:S(2)}) copy-start(f32[768]{0:T(1024)} %param.33) | copy-start | bytes 9220
  233.4 159.6 %reduce-scatter.11.cloned.1.call-start = ((), (), s32[]{:S(2)}) async-start(), calls=%async_computation.10 | async-start | bytes 3932160 | tf_op jit(solution)/shard_map/reduce_scatter | solution.py:125
  333.7 121.9 %reduce-scatter.15.cloned.1.call-start = ((), (), s32[]{:S(2)}) async-start(), calls=%async_computation.13 | async-start | bytes 3932160 | tf_op jit(solution)/shard_map/reduce_scatter | solution.py:125
  338.5 119.1 %copy-start.8 = (bf16[2,2,128,768]{3,2,1,0:T(8,128)(2,1)S(1)}, bf16[2,2,128,768]{3,2,1,0:T(8,128)(2,1)}, u32[]{:S(2)}) copy-start(bf16[2,2,128,768]{3,2,1,0:T(8,128)(2,1)} %param.38) | copy-start | bytes 2359300
  338.5 160.5 %all-gather.19.cloned.1.call-start = ((), (), s32[]{:S(2)}) async-start(), calls=%async_computation.18 | async-start | bytes 1966080 | tf_op jit(solution)/shard_map/all_gather | solution.py:133
  461.7 75.3 %all-gather.15.cloned.1.call-start = ((), (), s32[]{:S(2)}) async-start(), calls=%async_computation.14 | async-start | bytes 1966080 | tf_op jit(solution)/shard_map/all_gather | solution.py:133
  462.3 136.1 %reduce-scatter.21.cloned.1.call-start = ((), (), s32[]{:S(2)}) async-start(), calls=%async_computation.19 | async-start | bytes 3932160 | tf_op jit(solution)/shard_map/reduce_scatter | solution.py:161
  509.7 151.2 %reduce-scatter.17.cloned.1.call-start = ((), (), s32[]{:S(2)}) async-start(), calls=%async_computation.15 | async-start | bytes 3932160 | tf_op jit(solution)/shard_map/reduce_scatter | solution.py:161
  547.6 54.3 %copy-start.114 = (f32[2,128]{1,0:T(2,128)S(1)}, f32[2,128]{1,0:T(2,128)}, u32[]{:S(2)}) copy-start(f32[2,128]{1,0:T(2,128)} %copy-done.113) | copy-start | bytes 3076
  547.7 113.3 %copy-start.11 = (f32[2,128,768]{2,1,0:T(8,128)S(1)}, f32[2,128,768]{2,1,0:T(8,128)}, u32[]{:S(2)}) copy-start(f32[2,128,768]{2,1,0:T(8,128)} %copy-done.10) | copy-start | bytes 2359300
  547.7 113.3 %copy-start.80 = (f32[2,128]{1,0:T(2,128)S(1)}, f32[2,128]{1,0:T(2,128)}, u32[]{:S(2)}) copy-start(f32[2,128]{1,0:T(2,128)} %copy-done.79) | copy-start | bytes 3076
  547.7 113.3 %copy-start.84 = (f32[2,128]{1,0:T(2,128)S(1)}, f32[2,128]{1,0:T(2,128)}, u32[]{:S(2)}) copy-start(f32[2,128]{1,0:T(2,128)} %copy-done.83) | copy-start | bytes 3076
  547.7 113.3 %copy-start.86 = (f32[2,128]{1,0:T(2,128)S(1)}, f32[2,128]{1,0:T(2,128)}, u32[]{:S(2)}) copy-start(f32[2,128]{1,0:T(2,128)} %copy-done.85) | copy-start | bytes 3076
  547.7 113.2 %copy-start.100 = (f32[2,128]{1,0:T(2,128)S(1)}, f32[2,128]{1,0:T(2,128)}, u32[]{:S(2)}) copy-start(f32[2,128]{1,0:T(2,128)} %copy-done.99) | copy-start | bytes 3076
  547.7 113.2 %copy-start.102 = (f32[2,128]{1,0:T(2,128)S(1)}, f32[2,128]{1,0:T(2,128)}, u32[]{:S(2)}) copy-start(f32[2,128]{1,0:T(2,128)} %copy-done.101) | copy-start | bytes 3076
  547.7 113.2 %copy-start.116 = (f32[2,128]{1,0:T(2,128)S(1)}, f32[2,128]{1,0:T(2,128)}, u32[]{:S(2)}) copy-start(f32[2,128]{1,0:T(2,128)} %copy-done.115) | copy-start | bytes 3076
  547.8 115.7 %copy-start.112 = (f32[2,128]{1,0:T(2,128)S(1)}, f32[2,128]{1,0:T(2,128)}, u32[]{:S(2)}) copy-start(f32[2,128]{1,0:T(2,128)} %copy-done.111) | copy-start | bytes 3076
  547.8 155.9 %all-gather.17.cloned.1.call-start = ((), (), s32[]{:S(2)}) async-start(), calls=%async_computation.16 | async-start | bytes 1966080 | tf_op jit(solution)/shard_map/all_gather | solution.py:164
  666.4 75.2 %all-gather.21.cloned.1.call-start = ((), (), s32[]{:S(2)}) async-start(), calls=%async_computation.20 | async-start | bytes 1966080 | tf_op jit(solution)/shard_map/all_gather | solution.py:164
  683.3 187.1 %reduce-scatter.19.cloned.1.call-start = ((), (), s32[]{:S(2)}) async-start(), calls=%async_computation.17 | async-start | bytes 1966080 | tf_op jit(solution)/shard_map/reduce_scatter | solution.py:218
  729.6 142.0 %reduce-scatter.23.cloned.1.call-start = ((), (), s32[]{:S(2)}) async-start(), calls=%async_computation.21 | async-start | bytes 1966080 | tf_op jit(solution)/shard_map/reduce_scatter | solution.py:218
  768.0 163.9 %all-reduce.5.cloned.1.call-start = ((), (), s32[]{:S(2)}) async-start(), calls=%async_computation.24 | async-start | bytes 14155776 | tf_op jit(solution)/shard_map/psum | solution.py:246
  (134 other events, 1678.9 us)
Sparse Core Ops, SparseCore 0:
  10.2 39.7 all-gather.24
  52.1 35.9 all-gather.22
  106.5 59.0 reduce-scatter.12
  167.8 60.2 reduce-scatter.8
  232.9 37.1 all-gather.12
  272.1 35.9 all-gather.10
  333.8 59.1 reduce-scatter.10
  395.3 60.2 reduce-scatter.14
  461.8 37.1 all-gather.18
  501.0 35.9 all-gather.14
  539.3 59.1 reduce-scatter.20
  600.6 60.2 reduce-scatter.16
  666.5 37.0 all-gather.16
  705.7 35.9 all-gather.20
  743.8 34.1 reduce-scatter.18
  780.1 34.6 reduce-scatter.22
  819.0 112.8 all-reduce.4
where the time goes:
time: 953 us; the launch traced here: 945 us
  waiting for transfers between devices  615 us (65%)
  matrix products  98.6 us (10%)
  other arithmetic  88.8 us (9%)
  local copies, waits for them, and re-layouts  82.6 us (9%)
  blocking collectives  41.9 us (4%)
  between operations  16.1 us (2%)
    reduce_scatter x2, waiting for transfers between devices, on_device(): lax.psum_scatter(down_weight_piece, 'mp', scatter_dimension=1, tiled=True)  117 us
    reduce_scatter x2, waiting for transfers between devices, on_device(): lax.psum_scatter(back_hidden, 'mp', scatter_dimension=1, tiled=True)  110 us
    reduce_scatter x2, waiting for transfers between devices, on_device(): lax.psum_scatter(output_piece, 'mp', scatter_dimension=1, tiled=True)  101 us
    all_gather x2, waiting for transfers between devices, on_device(): hidden_state_rows = lax.all_gather(hidden_low, 'mp', axis=1, tiled=True)  69.9 us
    unnamed x307, local copies, waits for them, and re-layouts  64.3 us
    all_gather x2, waiting for transfers between devices, on_device(): lax.all_gather(d_second.astype(BRAIN), 'mp', axis=1, tiled=True)  63.4 us
    all_gather x2, waiting for transfers between devices, on_device(): complete_rows = lax.all_gather(token_rows, 'mp', axis=1, tiled=True)  62.4 us
    psum x1, waiting for transfers between devices, on_device(): summed = tuple(lax.psum(big_total + small_total, 'dp'))  57.8 us
  transfers between devices with their start and end apart: 17, of which 15 were waited for; matrix products, arithmetic and copies ran while one was open for 20% of the time, Pallas kernels for 0%

commit v1 on v0

v1 whole, which is shorter than its diff:
```python
import functools
import math

import jax
import jax.numpy as jnp
from jax import lax
from jax.experimental import pallas as pl
from jax.experimental.pallas import tpu as pltpu
from jax.sharding import PartitionSpec as P

EPSILON = 1e-12
MASKED = -1e30
F32 = jnp.float32
BF16 = jnp.bfloat16
VMEM_LIMIT = 56 * 1024 * 1024
ANY = pl.BlockSpec(memory_space=pl.ANY)
SMEM = pl.BlockSpec(memory_space=pltpu.SMEM)


def mm(a, b, ca, cb):
    return lax.dot_general(a, b, (((ca,), (cb,)), ((), ())), preferred_element_type=F32)


def cost(flops, moved, exps=0):
    return pl.CostEstimate(flops=int(flops), bytes_accessed=int(moved), transcendentals=int(exps))


def params():
    return pltpu.CompilerParams(vmem_limit_bytes=VMEM_LIMIT)


def attend_kernel(chunk, heads, size, tok, w, bias, prev, seg_row, seg_col, *refs):
    logits, probs, qkv, ctx, qs, ks, vs, cs = refs[-8:]
    h = pl.program_id(1)
    length = tok.shape[1]
    width = heads * size

    @pl.when(h == 0)
    def _():
        rows = (mm(tok[0], w[...], 1, 0) + bias[...]).astype(BF16)
        qkv[0] = rows
        for i in range(heads):
            at = i * size
            qs[i] = rows[:, at : at + size] * (1.0 / math.sqrt(size))
            ks[i] = rows[:, width + at : width + at + size]
            vs[i] = rows[:, 2 * width + at : 2 * width + at + size]

    k, v = ks[h], vs[h]
    seg_k = seg_row[0]
    for c in range(length // chunk):
        at = pl.ds(c * chunk, chunk)
        scores = mm(qs[h, at, :], k, 1, 1) + prev[0, 0, 0, at, :].astype(F32)
        logits[0, 0, 0, at, :] = scores.astype(BF16)
        masked = jnp.where(seg_col[0, at, :] == seg_k, scores, MASKED)
        exponent = jnp.exp(masked - jnp.max(masked, -1, keepdims=True))
        p = (exponent * (1.0 / jnp.sum(exponent, -1, keepdims=True))).astype(BF16)
        probs[0, 0, at, :] = p
        cs[h, at, :] = mm(p, v, 1, 0).astype(BF16)

    @pl.when(h == heads - 1)
    def _():
        ctx[0] = jnp.concatenate([cs[i] for i in range(heads)], -1)


def attend(b, complete, w_qkv, bias, prev_logits, seg_row, seg_col, logits_in, chunk=128):
    slots, length, width = complete.shape
    heads = prev_logits.shape[2]
    cols = w_qkv.shape[1]
    size = cols // 3 // heads
    big = pl.BlockSpec((1, 1, 1, length, length), lambda s, h: (b, s, h, 0, 0))

    def whole(*shape):
        return pl.BlockSpec(shape, lambda s, h: (0,) * len(shape))

    def slot(*shape):
        return pl.BlockSpec((1,) + shape, lambda s, h: (s,) + (0,) * len(shape))

    args = [complete, w_qkv, bias, prev_logits, seg_row, seg_col]
    in_specs = [
        slot(length, width), whole(width, cols), whole(1, cols), big, slot(1, length),
        slot(length, 1),
    ]
    alias = {}
    if logits_in is not None:
        alias = {len(args): 0}
        args.append(logits_in)
        in_specs.append(ANY)
    n = slots * heads * length * length
    return pl.pallas_call(
        functools.partial(attend_kernel, chunk, heads, size),
        grid=(slots, heads),
        in_specs=in_specs,
        out_specs=[
            big,
            pl.BlockSpec((1, 1, length, length), lambda s, h: (s, h, 0, 0)),
            slot(length, cols),
            slot(length, cols // 3),
        ],
        out_shape=[
            jax.ShapeDtypeStruct(prev_logits.shape, BF16),
            jax.ShapeDtypeStruct((slots, heads, length, length), BF16),
            jax.ShapeDtypeStruct((slots, length, cols), BF16),
            jax.ShapeDtypeStruct((slots, length, cols // 3), BF16),
        ],
        scratch_shapes=[pltpu.VMEM((heads, length, size), BF16)] * 4,
        input_output_aliases=alias,
        compiler_params=params(),
        cost_estimate=cost(n * 1024 + 2 * slots * length * width * cols, n * 6, n),
        name="attend",
    )(*args)


def attend_back_kernel(chunk, heads, size, n_blocks, place, tok, w, qkv, ctx, probs, cot, *refs):
    blocks = refs[:n_blocks]
    acc_in, bias_in = refs[n_blocks : n_blocks + 2]
    prev_grad, back, acc, bias_acc, qs, ks, vs, os, delta, dqkv = refs[-10:]
    s, h = pl.program_id(0), pl.program_id(1)
    length = tok.shape[1]
    width = heads * size
    local = blocks[0].shape[1]

    @pl.when(h == 0)
    def _():
        for j in range(n_blocks):
            at = pl.ds(pl.multiple_of(place[j] * local, local), local)
            for i in range(heads):
                os[i, at, :] = blocks[j][0, :, i * size : (i + 1) * size]
        rows = qkv[0]
        context = ctx[0]
        for i in range(heads):
            at = i * size
            qs[i] = rows[:, at : at + size]
            ks[i] = rows[:, width + at : width + at + size]
            vs[i] = rows[:, 2 * width + at : 2 * width + at + size]
            o = context[:, at : at + size].astype(F32) * os[i].astype(F32)
            delta[i] = jnp.sum(o, -1, keepdims=True)

    k, v = ks[h], vs[h]
    dk_t = dv_t = None
    for c in range(length // chunk):
        at = pl.ds(c * chunk, chunk)
        d_context = os[h, at, :]
        d_probs = mm(d_context, v, 1, 1)
        p = probs[0, 0, at, :]
        d_scores = p.astype(F32) * (d_probs - delta[h, at, :]) + cot[0, 0, 0, at, :].astype(F32)
        prev_grad[0, 0, 0, at, :] = d_scores
        d_dots = (d_scores * (1.0 / math.sqrt(size))).astype(BF16)
        dqkv[h, at, :size] = mm(d_dots, k, 1, 0).astype(BF16)
        part_k = mm(qs[h, at, :], d_dots, 0, 0)
        part_v = mm(d_context, p, 0, 0)
        dk_t = part_k if c == 0 else dk_t + part_k
        dv_t = part_v if c == 0 else dv_t + part_v
    dqkv[h, :, size : 2 * size] = dk_t.T.astype(BF16)
    dqkv[h, :, 2 * size :] = dv_t.T.astype(BF16)

    @pl.when(h == heads - 1)
    def _():
        parts = [dqkv[i] for i in range(heads)]
        d_qkv = jnp.concatenate(
            [part[:, j * size : (j + 1) * size] for j in range(3) for part in parts], -1
        )
        back[0] = mm(d_qkv, w[...], 1, 1).astype(BF16)
        grad = mm(tok[0], d_qkv, 0, 0)
        sums = jnp.sum(d_qkv.astype(F32), 0, keepdims=True)

        @pl.when(s == 0)
        def _():
            acc[...] = acc_in[...] + grad
            bias_acc[...] = bias_in[...] + sums

        @pl.when(s != 0)
        def _():
            acc[...] += grad
            bias_acc[...] += sums


def attend_back(
    b, place, complete, w_qkv, qkv, ctx, probs, logit_cot, blocks, acc, bias_acc, grad_in, chunk=128
):
    slots, length, width = complete.shape
    heads = logit_cot.shape[2]
    cols = w_qkv.shape[1]
    size = cols // 3 // heads
    local = blocks[0].shape[1]
    big = pl.BlockSpec((1, 1, 1, length, length), lambda s, h: (b, s, h, 0, 0))

    def whole(*shape):
        return pl.BlockSpec(shape, lambda s, h: (0,) * len(shape))

    def slot(*shape):
        return pl.BlockSpec((1,) + shape, lambda s, h: (s,) + (0,) * len(shape))

    args = [place, complete, w_qkv, qkv, ctx, probs, logit_cot, *blocks, acc, bias_acc]
    in_specs = [
        SMEM, slot(length, width), whole(width, cols), slot(length, cols),
        slot(length, cols // 3),
        pl.BlockSpec((1, 1, length, length), lambda s, h: (s, h, 0, 0)), big,
        *[slot(local, cols // 3)] * len(blocks), whole(width, cols), whole(8, cols),
    ]
    alias = {}
    if grad_in is not None:
        alias = {len(args): 0}
        args.append(grad_in)
        in_specs.append(ANY)
    n = slots * heads * length * length
    return pl.pallas_call(
        functools.partial(attend_back_kernel, chunk, heads, size, len(blocks)),
        grid=(slots, heads),
        in_specs=in_specs,
        out_specs=[big, slot(length, width), whole(width, cols), whole(8, cols)],
        out_shape=[
            jax.ShapeDtypeStruct(logit_cot.shape, F32),
            jax.ShapeDtypeStruct((slots, length, width), BF16),
            jax.ShapeDtypeStruct((width, cols), F32),
            jax.ShapeDtypeStruct((8, cols), F32),
        ],
        scratch_shapes=[pltpu.VMEM((heads, length, size), BF16)] * 4
        + [pltpu.VMEM((heads, length, 1), F32), pltpu.VMEM((heads, length, 3 * size), BF16)],
        input_output_aliases=alias,
        compiler_params=params(),
        cost_estimate=cost(n * 2048 + 4 * slots * length * width * cols, n * 8),
        name="attend_back",
    )(*args)


def gelu_and_slope(x):
    bell = jnp.exp(-0.5 * x * x)
    t = 1.0 / (1.0 + (0.3275911 * math.sqrt(0.5)) * jnp.abs(x))
    tail = t * (
        0.5 * 0.254829592
        + t * (
            0.5 * -0.284496736
            + t * (0.5 * 1.421413741 + t * (0.5 * -1.453152027 + t * (0.5 * 1.061405429)))
        )
    ) * bell
    phi = jnp.where(x >= 0, 1.0 - tail, tail)
    return x * phi, phi + x * (bell * (1.0 / math.sqrt(2.0 * math.pi)))


def norm_parts(u):
    centered = u - jnp.mean(u, -1, keepdims=True)
    r = lax.rsqrt(jnp.mean(centered * centered, -1, keepdims=True) + EPSILON)
    return centered * r, r


def norm_back(grad, gain, n, r):
    e = grad * gain
    return r * (e - jnp.mean(e, -1, keepdims=True) - n * jnp.mean(e * n, -1, keepdims=True))


def column_sum(u):
    return jnp.sum(u, 0, keepdims=True)


def feed_forward_kernel(n_ctx, n_in, n_down, chunk, refs_in, refs_out, scratch):
    ctx, refs_in = refs_in[:n_ctx], refs_in[n_ctx:]
    in_parts, refs_in = refs_in[:n_in], refs_in[n_in:]
    down_parts, refs_in = refs_in[:n_down], refs_in[n_down:]
    tok, cot, w_out, b_out, g1, s1, b_in, b_down, g2, s2 = refs_in[:10]
    (out, act, branch, inner, low, att, ctx_all, residual, smalls, unit_sums) = refs_out[:10]
    d_ctx = refs_out[10:]
    w_in, w_down, slope, sem = scratch
    units, width = w_in.shape
    span = units // n_in

    copies = []
    for i in range(n_in):
        copies.append(pltpu.make_async_copy(
            in_parts[i].at[pl.ds(0, span)], w_in.at[pl.ds(i * span, span)], sem.at[0, i]))
        copies[-1].start()
    down_copies = []
    for i in range(n_down):
        down_copies.append(pltpu.make_async_copy(
            down_parts[i].at[pl.ds(0, span)], w_down.at[pl.ds(i * span, span)], sem.at[1, i]))
        down_copies[-1].start()

    attended = b_out[...]
    for k in range(n_ctx):
        attended = attended + mm(ctx[k][...], w_out[k], 1, 0)
    ctx_all[0] = jnp.concatenate([c[...] for c in ctx], -1)
    n1, r1 = norm_parts(tok[0].astype(F32) + attended)
    hidden = n1 * g1[...] + s1[...]
    hidden_low = hidden.astype(BF16)
    low[0] = hidden_low
    second = hidden + b_down[...]
    waited = 0
    for j in range(units // chunk):
        at = pl.ds(j * chunk, chunk)
        while waited < n_in and waited * span < (j + 1) * chunk:
            copies[waited].wait()
            down_copies[waited].wait()
            waited += 1
        pre = mm(hidden_low, w_in[at, :], 1, 1) + b_in[:, at]
        activated, grad = gelu_and_slope(pre)
        activated = activated.astype(BF16)
        act[0, :, at] = activated
        slope[:, at] = grad.astype(BF16)
        second = second + mm(activated, w_down[at, :], 1, 0)

    n2, r2 = norm_parts(second)
    out[0] = (n2 * g2[...] + s2[...]).astype(BF16)
    g = cot[0].astype(F32)
    d_second = norm_back(g, g2[...], n2, r2)
    smalls[3:4, :] = column_sum(d_second)
    smalls[4:5, :] = column_sum(g * n2)
    smalls[5:6, :] = column_sum(g)
    d_branch = d_second.astype(BF16)
    branch[0] = d_branch
    d_hidden = d_second
    for j in range(units // chunk):
        at = pl.ds(j * chunk, chunk)
        d_act = mm(d_branch, w_down[at, :], 1, 1)
        d_inner = d_act * slope[:, at].astype(F32)
        unit_sums[:, at] = jnp.broadcast_to(column_sum(d_inner), (8, chunk))
        d_inner = d_inner.astype(BF16)
        inner[0, :, at] = d_inner
        d_hidden = d_hidden + mm(d_inner, w_in[at, :], 1, 0)
    d_residual = norm_back(d_hidden, g1[...], n1, r1)
    residual[0] = d_residual
    smalls[0:1, :] = column_sum(d_residual)
    smalls[1:2, :] = column_sum(d_hidden * n1)
    smalls[2:3, :] = column_sum(d_hidden)
    smalls[6:8, :] = jnp.zeros((2, width), F32)
    d_att = d_residual.astype(BF16)
    att[0] = d_att
    for k in range(n_ctx):
        d_ctx[k][...] = mm(d_att, w_out[k], 1, 1).astype(BF16)


def feed_forward(b, ctx, in_parts, down_parts, tokens, cot, w_out, vectors, joint, chunk=384):
    micro, rows, width = tokens.shape
    b_out, g1, s1, b_in, b_down, g2, s2 = vectors
    units = b_in.shape[1]
    head_width = ctx[0].shape[1]
    n_ctx, n_in, n_down = len(ctx), len(in_parts), len(down_parts)

    def whole(*shape):
        return pl.BlockSpec(shape, lambda i: (0,) * len(shape))

    def part(cols):
        return pl.BlockSpec((1, rows, cols), lambda i: (b, 0, 0))

    args = [*ctx, *in_parts, *down_parts, tokens, cot, w_out, b_out, g1, s1, b_in, b_down, g2, s2]
    in_specs = (
        [whole(rows, head_width)] * n_ctx
        + [ANY] * (n_in + n_down)
        + [part(width)] * 2
        + [whole(n_ctx, head_width, width)]
        + [whole(1, v.shape[1]) for v in vectors]
    )
    joint_cols = [(width, BF16), (units, BF16), (width, BF16), (units, BF16), (width, BF16),
                  (width, BF16), (width, BF16), (width, F32)]
    alias = {}
    if joint is not None:
        for i, array in enumerate(joint):
            alias[len(args)] = i
            args.append(array)
            in_specs.append(ANY)
    n_args = len(args)
    n_out = len(joint_cols) + 2 + n_ctx

    def kernel(*refs):
        feed_forward_kernel(
            n_ctx, n_in, n_down, chunk, refs[: n_args], refs[n_args : n_args + n_out],
            refs[n_args + n_out :],
        )

    outs = pl.pallas_call(
        kernel,
        grid=(1,),
        in_specs=in_specs,
        out_specs=[part(c) for c, _ in joint_cols]
        + [whole(8, width), whole(8, units)]
        + [whole(rows, head_width)] * n_ctx,
        out_shape=[jax.ShapeDtypeStruct((micro, rows, c), t) for c, t in joint_cols]
        + [jax.ShapeDtypeStruct((8, width), F32), jax.ShapeDtypeStruct((8, units), F32)]
        + [jax.ShapeDtypeStruct((rows, head_width), BF16)] * n_ctx,
        scratch_shapes=[
            pltpu.VMEM((units, width), BF16), pltpu.VMEM((units, width), BF16),
            pltpu.VMEM((rows, units), BF16), pltpu.SemaphoreType.DMA((2, max(n_in, n_down))),
        ],
        input_output_aliases=alias,
        compiler_params=params(),
        cost_estimate=cost(
            2 * rows * width * (4 * units + 2 * width), 4 * units * width + 20 * rows * width,
            rows * units,
        ),
        name="feed_forward",
    )(*args)
    n = len(joint_cols)
    return outs[:n], outs[n], outs[n + 1], outs[n + 2 :]


def shift_pairs(mp, k):
    return [(i, (i + k) % mp) for i in range(mp)]


def flip_pairs(dp, bit):
    return [(i, i ^ bit) for i in range(dp)]


def add_low(a, b):
    return (a.astype(F32) + b.astype(F32)).astype(BF16)


def plane_gather(first, second, dp):
    x, y = flip_pairs(dp, 2), flip_pairs(dp, 4)
    a1 = lax.ppermute(first, "dp", x)
    b2 = lax.ppermute(second, "dp", y)
    a2 = lax.ppermute(first, "dp", y)
    b1 = lax.ppermute(second, "dp", x)
    a3 = lax.ppermute(a1, "dp", y)
    b3 = lax.ppermute(b2, "dp", x)
    return [first, a1, a2, a3], [second, b1, b2, b3]


def plane_reduce(first, second, dp):
    x, y = flip_pairs(dp, 2), flip_pairs(dp, 4)
    a3 = lax.ppermute(first[3], "dp", y)
    b3 = lax.ppermute(second[3], "dp", x)
    a2 = lax.ppermute(first[2], "dp", y)
    b1 = lax.ppermute(second[1], "dp", x)
    a1 = lax.ppermute(add_low(first[1], a3), "dp", x)
    b2 = lax.ppermute(add_low(second[2], b3), "dp", y)
    a = first[0].astype(F32) + a1.astype(F32) + a2.astype(F32)
    b = second[0].astype(F32) + b1.astype(F32) + b2.astype(F32)
    return a.astype(BF16), b.astype(BF16)


def reorder(rows, order):
    pick = (order[:, None] == jnp.arange(rows.shape[0])[None, :]).astype(F32)
    return jnp.dot(pick, rows, precision=lax.Precision.HIGHEST)


def on_device(
    tokens,
    prev_logits,
    segment_ids,
    query_weight,
    key_weight,
    value_weight,
    query_bias,
    value_bias,
    output_projection_weight,
    output_bias,
    first_gain,
    first_shift,
    inner_projection_weight,
    inner_bias,
    down_projection_weight,
    down_bias,
    second_gain,
    second_shift,
    output_cot,
    logit_cot,
):
    dp = lax.axis_size("dp")
    mp = lax.axis_size("mp")
    me = lax.axis_index("dp")
    mine = lax.axis_index("mp")
    micro_count, slots, local, width = tokens.shape
    length = prev_logits.shape[3]
    head_width = query_weight.shape[1]
    units = inner_projection_weight.shape[1]
    rows = slots * local
    small_plane = dp == 8
    chips = dp // 2
    core, chip = me % 2, me // 2
    swap = flip_pairs(dp, 1)
    piece = units // dp
    span = mp * piece
    wo_rows = head_width // chips

    def shifted(array, k):
        return lax.ppermute(array, "mp", shift_pairs(mp, k)) if k else array

    complete = [lax.all_gather(tokens[b], "mp", axis=1, tiled=True) for b in range(micro_count)]

    if small_plane:
        start = (core * chips + chip) * piece
        in_piece = lax.dynamic_slice(inner_projection_weight, (0, start), (width, piece)).T
        wo_piece = lax.dynamic_slice(
            output_projection_weight, (chip * wo_rows, 0), (wo_rows, width)
        )
        first_piece = jnp.concatenate([in_piece, wo_piece], 0)
        second_piece = lax.dynamic_slice(down_projection_weight, (start, 0), (piece, width))
        first_z = [shifted(first_piece, k) for k in range(mp)]
        second_z = [shifted(second_piece, k) for k in range(mp)]
        first = jnp.concatenate([a[:piece] for a in first_z] + [a[piece:] for a in first_z], 0)
        second = jnp.concatenate(second_z, 0)
        in_parts, down_parts = plane_gather(first, second, dp)
        w_out = jnp.zeros((mp, chips, wo_rows, width), BF16)
        for o in range(chips):
            block = in_parts[o][span:].reshape(mp, 1, wo_rows, width)
            w_out = lax.dynamic_update_slice(w_out, block, (0, chip ^ o, 0, 0))
        w_out = w_out.reshape(mp, head_width, width)
        in_parts = in_parts + [lax.ppermute(a, "dp", swap) for a in in_parts]
        down_parts = down_parts + [lax.ppermute(a, "dp", swap) for a in down_parts]
        bias_z = jnp.stack([shifted(inner_bias, k) for k in range(mp)]).reshape(-1, piece)
        c_i, o_i, k_i = jnp.meshgrid(
            jnp.arange(2), jnp.arange(chips), jnp.arange(mp), indexing="ij"
        )
        unit_order = ((k_i * 2 + (core ^ c_i)) * chips + (chip ^ o_i)).reshape(-1)
        bias_units = reorder(bias_z, unit_order).reshape(1, -1)
    else:
        in_parts = [lax.all_gather(inner_projection_weight.T, "mp", axis=0, tiled=True)]
        down_parts = [lax.all_gather(down_projection_weight, "mp", axis=0, tiled=True)]
        wo_all = lax.all_gather(output_projection_weight, "mp")
        w_out = jnp.stack(
            [lax.dynamic_index_in_dim(wo_all, (mine - k) % mp, 0, False) for k in range(mp)]
        )
        bias_units = lax.all_gather(inner_bias, "mp").reshape(1, -1)

    w_qkv = jnp.concatenate([query_weight, key_weight, value_weight], 1)
    bias_row = jnp.concatenate([query_bias, jnp.zeros_like(query_bias), value_bias])[None]
    vectors = [
        output_bias[None], first_gain[None], first_shift[None], bias_units, down_bias[None],
        second_gain[None], second_shift[None],
    ]
    own_tokens = tokens.reshape(micro_count, rows, width)
    own_cot = output_cot.reshape(micro_count, rows, width)
    logits = joint = None
    kept = []
    for b in range(micro_count):
        seg = segment_ids[b]
        logits, probs, qkv, ctx = attend(
            b, complete[b], w_qkv, bias_row, prev_logits, seg[:, None, :], seg[:, :, None], logits
        )
        blocks = []
        for k in range(mp):
            at = ((mine + k) % mp) * local
            block = lax.dynamic_slice(ctx, (0, at, 0), (slots, local, head_width))
            blocks.append(shifted(block, k).reshape(rows, head_width))
        joint, small, unit_sums, d_ctx = feed_forward(
            b, blocks, in_parts, down_parts, own_tokens, own_cot, w_out, vectors, joint
        )
        d_blocks = [
            shifted(block, (mp - k) % mp).reshape(slots, local, head_width)
            for k, block in enumerate(d_ctx)
        ]
        kept.append((probs, qkv, ctx, small, unit_sums, d_blocks))
    layer, act, branch, inner, low, att, ctx_all, residual = joint

    def tall(array):
        return array.reshape(micro_count * rows, -1)

    place = jnp.stack([(mine + k) % mp for k in range(mp)]).astype(jnp.int32)
    prev_grad = None
    acc = jnp.zeros((width, 3 * head_width), F32)
    bias_acc = jnp.zeros((8, 3 * head_width), F32)
    token_grads = []
    for b in range(micro_count):
        probs, qkv, ctx, _, _, d_blocks = kept[b]
        prev_grad, back, acc, bias_acc = attend_back(
            b, place, complete[b], w_qkv, qkv, ctx, probs, logit_cot, d_blocks, acc, bias_acc,
            prev_grad,
        )
        back = lax.psum_scatter(back, "mp", scatter_dimension=1, tiled=True)
        token_grads.append(
            residual[b].reshape(slots, local, width) + back.astype(F32)
        )

    g_down = mm(tall(act), tall(branch), 0, 0)
    g_in = mm(tall(inner), tall(low), 0, 0)
    g_out = mm(tall(ctx_all), tall(att), 0, 0)
    unit_total = sum(each[4][0] for each in kept)
    small = sum(each[3] for each in kept)
    if small_plane:
        g_down, g_in, g_out = (g.astype(BF16) for g in (g_down, g_in, g_out))
        half = units * mp // 2
        g_down = add_low(g_down[:half], lax.ppermute(g_down[half:], "dp", swap))
        g_in = add_low(g_in[:half], lax.ppermute(g_in[half:], "dp", swap))
        g_out = add_low(g_out, lax.ppermute(g_out, "dp", swap))
        g_out = g_out.reshape(mp, chips, wo_rows, width)
        first_list, second_list = [], []
        for o in range(chips):
            block = lax.dynamic_index_in_dim(g_out, chip ^ o, 1, False).reshape(-1, width)
            first_list.append(jnp.concatenate([g_in[o * span : (o + 1) * span], block], 0))
            second_list.append(g_down[o * span : (o + 1) * span])
        first, second = plane_reduce(first_list, second_list, dp)
        in_sum = out_sum = down_sum = 0.0
        for k in range(mp):
            send = jnp.concatenate(
                [
                    first[k * piece : (k + 1) * piece],
                    first[span + k * wo_rows : span + (k + 1) * wo_rows],
                    second[k * piece : (k + 1) * piece],
                ],
                0,
            )
            got = shifted(send, (mp - k) % mp).astype(F32)
            in_sum += got[:piece]
            out_sum += got[piece : piece + wo_rows]
            down_sum += got[piece + wo_rows :]
        firsts, seconds = plane_gather(
            jnp.concatenate([in_sum, out_sum], 0).astype(BF16), down_sum.astype(BF16), dp
        )
        in_grad = jnp.zeros((2, chips, piece, width), BF16)
        down_grad = jnp.zeros((2, chips, piece, width), BF16)
        output_weight_grad = jnp.zeros((chips, wo_rows, width), BF16)
        for o in range(chips):
            for c in range(2):
                a = lax.ppermute(firsts[o], "dp", swap) if c else firsts[o]
                d = lax.ppermute(seconds[o], "dp", swap) if c else seconds[o]
                at = (core ^ c, chip ^ o, 0, 0)
                in_grad = lax.dynamic_update_slice(in_grad, a[None, None, :piece], at)
                down_grad = lax.dynamic_update_slice(down_grad, d[None, None], at)
                if c == 0:
                    output_weight_grad = lax.dynamic_update_slice(
                        output_weight_grad, a[None, piece:], (chip ^ o, 0, 0)
                    )
        inner_weight_grad = in_grad.reshape(units, width).astype(F32).T
        down_weight_grad = down_grad.reshape(units, width).astype(F32)
        output_weight_grad = output_weight_grad.reshape(head_width, width).astype(F32)
        c_j, o_j = jnp.meshgrid(jnp.arange(2), jnp.arange(chips), indexing="ij")
        z_j = jnp.arange(mp)[:, None, None]
        back_order = (((core ^ c_j) * chips + (chip ^ o_j)) * mp + (mine - z_j) % mp).reshape(-1)
        unit_total = reorder(unit_total.reshape(-1, piece), back_order).reshape(-1)
    else:
        g_in = lax.psum_scatter(g_in, "mp", scatter_dimension=0, tiled=True)
        inner_weight_grad = lax.psum(g_in, "dp").T
        g_down = lax.psum_scatter(g_down, "mp", scatter_dimension=0, tiled=True)
        down_weight_grad = lax.psum(g_down, "dp")
        g_out = g_out.reshape(mp, head_width, width)
        out_sum = 0.0
        for k in range(mp):
            out_sum += shifted(g_out[k], (mp - k) % mp)
        output_weight_grad = lax.psum(out_sum, "dp")

    vector = jnp.concatenate([small[:6].reshape(-1), unit_total])
    vector = lax.psum(vector, ("dp", "mp"))
    small = vector[: 6 * width].reshape(6, width)
    inner_bias_grad = lax.dynamic_slice(vector, (6 * width + mine * units,), (units,))
    summed = lax.psum(jnp.concatenate([acc, bias_acc], 0), "dp")
    return (
        layer.reshape(tokens.shape),
        logits,
        jnp.stack(token_grads),
        prev_grad,
        summed[:width, :head_width],
        summed[:width, head_width : 2 * head_width],
        summed[:width, 2 * head_width :],
        summed[width, :head_width],
        summed[width, 2 * head_width :],
        output_weight_grad,
        small[0],
        small[1],
        small[2],
        inner_weight_grad,
        inner_bias_grad,
        down_weight_grad,
        small[3],
        small[4],
        small[5],
    )


def solution(mesh):
    rows = P(None, "dp", "mp", None)
    heads = P(None, "dp", "mp", None, None)
    cols, deep, vec, same = P(None, "mp"), P("mp", None), P("mp"), P()
    in_specs = (
        rows, heads, P(None, "dp", None), cols, cols, cols, vec, vec, deep, same, same, same,
        cols, vec, deep, same, same, same, rows, heads,
    )
    out_specs = (
        rows, heads, rows, heads, cols, cols, cols, vec, vec, deep, same, same, same, cols, vec,
        deep, same, same, same,
    )
    return jax.shard_map(
        on_device, mesh=mesh, in_specs=in_specs, out_specs=out_specs, check_vma=False
    )
```

time: 953 us -> 474 us (0.50)
  waiting for transfers between devices: 615 us -> 125 us
  Pallas kernels: 0 us -> 102 us
  matrix products: 98.6 us -> 9.31 us
  starting transfers between devices: 2.12 us -> 78.2 us
  other arithmetic: 88.8 us -> 34.4 us
  local copies, waits for them, and re-layouts: 82.6 us -> 59.2 us
    reduce_scatter x8 -> x2, waiting for transfers between devices: 328 us -> 9.19 us  [on_device(): back = lax.psum_scatter(back, 'mp', scatter_dimension=1, tiled=True)]
    all_gather x8 -> x2, waiting for transfers between devices: 228 us -> 0.01 us  [on_device(): lax.all_gather(tokens[b], 'mp', axis=1, tiled=True)]
    ppermute x0 -> x61, waiting for transfers between devices: none -> 116 us  [the longest x24 54.5 us: shifted(): return lax.ppermute(array, 'mp', shift_pairs(mp, k)) if k else array]
    pallas_call x0 -> x6, Pallas kernels: none -> 102 us  [the longest x2 36.2 us: feed_forward(): pl.pallas_call(kernel, grid=(1,), in_specs=in_specs, out_specs=[part(c) f...]
    dot_general x36 -> x5, matrix products: 98.6 us -> 9.31 us  [the longest x3 8.27 us: mm(): lax.dot_general(a, b, (((ca,), (cb,)), ((), ())), preferred_element_type=...]
    ppermute x0 -> x61, starting transfers between devices: none -> 77.8 us  [the longest x24 54.2 us: shifted(): return lax.ppermute(array, 'mp', shift_pairs(mp, k)) if k else array]
    psum x1, waiting for transfers between devices: 57.8 us -> 0.01 us  [on_device(): summed = lax.psum(jnp.concatenate([acc, bias_acc], 0), 'dp')]
    unnamed x307 -> x133, local copies, waits for them, and re-layouts: 64.3 us -> 22 us
  transfers between devices with their start and end apart: 17 -> 66, of which waited for: 15 -> 20; matrix products, arithmetic and copies ran while one was open for 20% -> 19% of each run, Pallas kernels for 0% -> 18%
where the time goes in v1:
time: 474 us; the launch traced here: 466 us
  waiting for transfers between devices  125 us (26%)
  Pallas kernels  102 us (22%)
  starting transfers between devices  78.2 us (16%)
  local copies, waits for them, and re-layouts  59.2 us (12%)
  blocking collectives  41.9 us (9%)
  other arithmetic  34.4 us (7%)
  between operations  15.2 us (3%)
  matrix products  9.31 us (2%)
    ppermute x24, waiting for transfers between devices, shifted(): return lax.ppermute(array, 'mp', shift_pairs(mp, k)) if k else array  54.5 us
    ppermute x24, starting transfers between devices, shifted(): return lax.ppermute(array, 'mp', shift_pairs(mp, k)) if k else array  54.2 us
    psum x1, blocking collectives, on_device(): vector = lax.psum(vector, ('dp', 'mp'))  41.9 us
    pallas_call x2, Pallas kernels, feed_forward(): pl.pallas_call(kernel, grid=(1,), in_specs=in_specs, out_specs=[part(c) f...  36.2 us
    pallas_call x2, Pallas kernels, attend_back(): pl.pallas_call(functools.partial(attend_back_kernel, chunk, heads, size,...  36.1 us
    pallas_call x2, Pallas kernels, attend(): pl.pallas_call(functools.partial(attend_kernel, chunk, heads, size), grid...  30 us
    unnamed x133, local copies, waits for them, and re-layouts  22 us
    ppermute x1, waiting for transfers between devices, plane_reduce(): b2 = lax.ppermute(add_low(second[2], b3), 'dp', y)  15.8 us
  transfers between devices with their start and end apart: 66, of which 20 were waited for; matrix products, arithmetic and copies ran while one was open for 19% of the time, Pallas kernels for 18%

profile of v1, /device:TPU:0, one launch (start us, length us, event | category | flops | bytes accessed | tf_op | source)
XLA Modules:
  0.0 465.7 jit_solution(16741506298338508308)
XLA Ops:
  9.9 3.1 collective-permute-start.3
  13.0 2.6 collective-permute-start.4
  21.4 2.5 collective-permute-start.15
  24.5 20.8 %collective-permute-done.4 = bf16[144,768]{1,0:T(8,128)(2,1)S(1)} collective-permute-done((bf16[144,768]{1,0:T(8,128)(2,1)S(1)}, bf16[144,768]{1,0:T(8,128)(2,1)S(1)}, u32[]{:S(2)}, u32[]{:S(2)}) %collective-permute-start.4) | collective-permute-done | bytes 221216 | tf_op jit(solution)/shard_map/ppermute | solution.py:475
  45.3 9.1 %collective-permute-start.23 = (f32[768]{0:T(1024)S(1)}, f32[768]{0:T(1024)S(1)}, u32[]{:S(2)}, u32[]{:S(2)}) collective-permute-start(f32[768]{0:T(1024)S(1)} %copy-done.39), channel_id=1, source_target_pairs={{0,1},{1,2},{2,3},{3,0},{4,5},{5,6},{6,7},{7,4},{8,9},{9,10},{10,1... | collective-permute-start | bytes 9224 | tf_op jit(solution)/shard_map/ppermute | solution.py:475
  60.6 6.9 %collective-permute-start.24 = (f32[768]{0:T(1024)S(1)}, f32[768]{0:T(1024)S(1)}, u32[]{:S(2)}, u32[]{:S(2)}) collective-permute-start(f32[768]{0:T(1024)S(1)} %copy-done.39), channel_id=1, source_target_pairs={{0,2},{1,3},{2,0},{3,1},{4,6},{5,7},{6,4},{7,5},{8,10},{9,11},{10,... | collective-permute-start | bytes 9224 | tf_op jit(solution)/shard_map/ppermute | solution.py:475
  69.6 4.2 collective-permute-start.25
  77.8 12.4 %collective-permute-done.17.refs_14_ = bf16[384,768]{1,0:T(8,128)(2,1)S(1)} collective-permute-done((bf16[384,768]{1,0:T(8,128)(2,1)S(1)}, bf16[384,768]{1,0:T(8,128)(2,1)S(1)}, u32[]{:S(2)}, u32[]{:S(2)}) %collective-permute-start.17) | collective-permute-done | bytes 589856 | tf_op jit(solution)/shard_map/ppermute | solution.py:409
  113.4 10.1 %collective-permute-done.8.refs_7_ = bf16[576,768]{1,0:T(8,128)(2,1)} collective-permute-done((bf16[576,768]{1,0:T(8,128)(2,1)S(1)}, bf16[576,768]{1,0:T(8,128)(2,1)}, u32[]{:S(2)}, u32[]{:S(2)}) %collective-permute-start.8) | collective-permute-done | bytes 884768 | tf_op jit(solution)/shard_map/ppermute | solution.py:412
  126.2 15.0 %attend.2 = (bf16[2,2,3,512,512]{4,3,2,1,0:T(8,128)(2,1)}, bf16[2,3,512,512]{3,2,1,0:T(8,128)(2,1)}, bf16[2,512,576]{2,1,0:T(8,128)(2,1)}, bf16[2,512,192]{2,1,0:T(8,128)(2,1)}) custom-call(bf16[2,512,768]{2,1,0:T(8,128)(2,1)} %bitcast.163, bf16[768,576]{1,0:T(8,128)(2,1)} %pad_maximum_fusion.2.w, f32[1,576]{1,0:T(1,128)} %broadcast_in_dim.116.bias, ...), custom_call_target="tpu_custom_call" | custom-call | flops 2516582400 | bytes 9437184 | tf_op jit(solution)/shard_map/attend/pallas_call | solution.py:89
  143.1 15.0 %attend.3 = (bf16[2,2,3,512,512]{4,3,2,1,0:T(8,128)(2,1)}, bf16[2,3,512,512]{3,2,1,0:T(8,128)(2,1)}, bf16[2,512,576]{2,1,0:T(8,128)(2,1)}, bf16[2,512,192]{2,1,0:T(8,128)(2,1)}) custom-call(bf16[2,512,768]{2,1,0:T(8,128)(2,1)} %bitcast.152, bf16[768,576]{1,0:T(8,128)(2,1)} %pad_maximum_fusion.2.w, ...), custom_call_target="tpu_custom_call", output_to_operand_aliasing={{0}: (6, {})} | custom-call | flops 2516582400 | bytes 9437184 | tf_op jit(solution)/shard_map/attend/pallas_call | solution.py:89
  160.4 2.4 collective-permute-start.28
  167.1 4.8 %collective-permute-done.27 = bf16[2,128,192]{2,1,0:T(8,128)(2,1)S(1)} collective-permute-done((bf16[2,128,192]{2,1,0:T(8,128)(2,1)S(1)}, bf16[2,128,192]{2,1,0:T(8,128)(2,1)S(1)}, u32[]{:S(2)}, u32[]{:S(2)}) %collective-permute-start.27) | collective-permute-done | bytes 98336 | tf_op jit(solution)/shard_map/ppermute | solution.py:475
  172.0 3.8 collective-permute-start.2
  176.4 18.0 %feed_forward.2 = (bf16[2,256,768]{2,1,0:T(8,128)(2,1)}, bf16[2,256,3072]{2,1,0:T(8,128)(2,1)}, bf16[2,256,768]{2,1,0:T(8,128)(2,1)}, bf16[2,256,3072]{2,1,0:T(8...) custom-call(bf16[256,192]{1,0:T(8,128)(2,1)} %bitcast.185, ...), custom_call_target="tpu_custom_call" | custom-call | flops 5435817984 | bytes 13369344 | tf_op jit(solution)/shard_map/feed_forward/pallas_call | solution.py:368
  194.5 5.8 %collective-permute-start.30 = (bf16[256,192]{1,0:T(8,128)(2,1)}, bf16[256,192]{1,0:T(8,128)(2,1)S(1)}, u32[]{:S(2)}, u32[]{:S(2)}) collective-permute-start(bf16[256,192]{1,0:T(8,128)(2,1)} %get-tuple-element.81), channel_id=1, source_target_pairs={{0,2},{1,3},{2,0},{3,1},{4,6},{5,7},{6,4},{7,5},{8,10},{9,11},{10,... | collective-permute-start | bytes 294920 | tf_op jit(solution)/shard_map/ppermute | solution.py:475
  201.2 18.1 %feed_forward.3 = (bf16[2,256,768]{2,1,0:T(8,128)(2,1)}, bf16[2,256,3072]{2,1,0:T(8,128)(2,1)}, bf16[2,256,768]{2,1,0:T(8,128)(2,1)}, bf16[2,256,3072]{2,1,0:T(8...) custom-call(bf16[256,192]{1,0:T(8,128)(2,1)} %bitcast.177, ...), custom_call_target="tpu_custom_call", output_to_operand_aliasing={{0}: (30, {}), {1}: (31, {}), {2}: (32, {}), {3}: (33, {}),... | custom-call | flops 5435817984 | bytes 13369344 | tf_op jit(solution)/shard_map/feed_forward/pallas_call | solution.py:368
  219.4 3.9 collective-permute-start.32
  226.4 18.0 %attend_back.2 = (f32[2,2,3,512,512]{4,3,2,1,0:T(8,128)}, bf16[2,512,768]{2,1,0:T(8,128)(2,1)}, f32[768,576]{1,0:T(8,128)}, f32[8,576]{1,0:T(8,128)}) custom-call(s32[4]{0:T(128)} %pad_add_fusion.place, bf16[2,512,768]{2,1,0:T(8,128)(2,1)} %bitcast.164, bf16[768,576]{1,0:T(8,128)(2,1)} %pad_maximum_fusion.2.w, bf16[2,512,576]{2,1,0:T(8,128)(2,1)} %get-tuple-element.77.qkv, ...), custom_call_target="tpu_custom_call" | custom-call | flops 5033164800 | bytes 12582912 | tf_op jit(solution)/shard_map/attend_back/pallas_call | solution.py:206
  245.2 18.0 %attend_back.3 = (f32[2,2,3,512,512]{4,3,2,1,0:T(8,128)}, bf16[2,512,768]{2,1,0:T(8,128)(2,1)}, f32[768,576]{1,0:T(8,128)}, f32[8,576]{1,0:T(8,128)}) custom-call(s32[4]{0:T(128)} %pad_add_fusion.place, bf16[2,512,768]{2,1,0:T(8,128)(2,1)} %bitcast.153, bf16[768,576]{1,0:T(8,128)(2,1)} %pad_maximum_fusion.2.w, ...), custom_call_target="tpu_custom_call", output_to_operand_aliasing={{0}: (13, {})} | custom-call | flops 5033164800 | bytes 12582912 | tf_op jit(solution)/shard_map/attend_back/pallas_call | solution.py:206
  263.2 3.0 pad_maximum_fusion
  267.3 4.5 bitcast_convert_fusion.1
  277.5 2.9 bitcast_convert_fusion
  285.3 41.9 %psum.15 = f32[7680]{0:T(1024)} all-reduce(f32[7680]{0:T(1024)S(1)} %pad_maximum_fusion.14), channel_id=1, replica_groups=mesh['dp'=8,'mp'=4] {'dp','mp'}, use_global_device_ids=true, to_apply=%region_3.4 | all-reduce | flops 7680 | bytes 61440 | tf_op jit(solution)/shard_map/psum | solution.py:631
  332.2 3.6 add_convert_fusion.1
  345.4 3.3 fusion.24
  350.7 9.6 %collective-permute-done.42 = bf16[384,768]{1,0:T(8,128)(2,1)} collective-permute-done((bf16[384,768]{1,0:T(8,128)(2,1)}, bf16[384,768]{1,0:T(8,128)(2,1)}, u32[]{:S(2)}, u32[]{:S(2)}) %collective-permute-start.42) | collective-permute-done | bytes 589856 | tf_op jit(solution)/shard_map/ppermute | solution.py:420
  375.7 15.8 %collective-permute-done.43 = bf16[384,768]{1,0:T(8,128)(2,1)} collective-permute-done((bf16[384,768]{1,0:T(8,128)(2,1)}, bf16[384,768]{1,0:T(8,128)(2,1)}, u32[]{:S(2)}, u32[]{:S(2)}) %collective-permute-start.43) | collective-permute-done | bytes 589856 | tf_op jit(solution)/shard_map/ppermute | solution.py:424
  398.8 9.2 %reduce-scatter.5.cloned.1.call-done = bf16[2,128,768]{2,1,0:T(8,128)(2,1)} async-done(((bf16[2,512,768]{2,1,0:T(8,128)(2,1)}), bf16[2,128,768]{2,1,0:T(8,128)(2,1)}) %reduce-scatter.5.cloned.1.call-update) | async-done | bytes 393232 | tf_op jit(solution)/shard_map/reduce_scatter | solution.py:558
  410.4 23.4 %collective-permute-done.45 = bf16[240,768]{1,0:T(8,128)(2,1)} collective-permute-done((bf16[240,768]{1,0:T(8,128)(2,1)S(1)}, bf16[240,768]{1,0:T(8,128)(2,1)}, u32[]{:S(2)}, u32[]{:S(2)}) %collective-permute-start.45) | collective-permute-done | bytes 368672 | tf_op jit(solution)/shard_map/ppermute | solution.py:475
  443.9 2.4 collective-permute-done.47
  452.7 2.6 collective-permute-done.49
  (366 shorter events, 133.8 us)
Async XLA Ops:
  7.2 119.0 %all-gather.7.cloned.1.call-start = ((), (), s32[]{:S(2)}) async-start(), calls=%async_computation.6 | async-start | bytes 1966080 | tf_op jit(solution)/shard_map/all_gather | solution.py:477
  9.4 133.6 %all-gather.5.cloned.1.call-start = ((), (), s32[]{:S(2)}) async-start(), calls=%async_computation.5 | async-start | bytes 1966080 | tf_op jit(solution)/shard_map/all_gather | solution.py:477
  13.0 32.3 %collective-permute-start.4 = (bf16[144,768]{1,0:T(8,128)(2,1)S(1)}, bf16[144,768]{1,0:T(8,128)(2,1)S(1)}, u32[]{:S(2)}, u32[]{:S(2)}) collective-permute-start(bf16[144,768]{1,0:T(8,128)(2,1)S(1)} %pad_maximum_fusion.10), channel_id=1, source_target_pairs={{0,2},{1,3},{2,0},{3,1},{4,6},{5,7},{6,4},{7,5},{8,10},{9,11},{10,... | collective-permute-start | bytes 663560 | tf_op jit(solution)/shard_map/ppermute | solution.py:475
  15.5 39.6 %collective-permute-start.5 = (bf16[144,768]{1,0:T(8,128)(2,1)S(1)}, bf16[144,768]{1,0:T(8,128)(2,1)S(1)}, u32[]{:S(2)}, u32[]{:S(2)}) collective-permute-start(bf16[144,768]{1,0:T(8,128)(2,1)S(1)} %pad_maximum_fusion.10), channel_id=1, source_target_pairs={{0,3},{1,0},{2,1},{3,2},{4,7},{5,4},{6,5},{7,6},{8,11},{9,8},{10,9... | collective-permute-start | bytes 663560 | tf_op jit(solution)/shard_map/ppermute | solution.py:475
  17.8 42.8 %collective-permute-start.13 = (bf16[96,768]{1,0:T(8,128)(2,1)S(1)}, bf16[96,768]{1,0:T(8,128)(2,1)S(1)}, u32[]{:S(2)}, u32[]{:S(2)}) collective-permute-start(bf16[96,768]{1,0:T(8,128)(2,1)S(1)} %constant_dynamic-slice_fusion.8), channel_id=1, source_target_pairs={{0,1},{1,2},{2,3},{3,0},{4,5},{5,6},{6,7},{7,4},{8,9},{9,10},{10,1... | collective-permute-start | bytes 442376 | tf_op jit(solution)/shard_map/ppermute | solution.py:475
  18.5 51.1 %collective-permute-start.14 = (bf16[96,768]{1,0:T(8,128)(2,1)S(1)}, bf16[96,768]{1,0:T(8,128)(2,1)S(1)}, u32[]{:S(2)}, u32[]{:S(2)}) collective-permute-start(bf16[96,768]{1,0:T(8,128)(2,1)S(1)} %constant_dynamic-slice_fusion.8), channel_id=1, source_target_pairs={{0,2},{1,3},{2,0},{3,1},{4,6},{5,7},{6,4},{7,5},{8,10},{9,11},{10,... | collective-permute-start | bytes 442376 | tf_op jit(solution)/shard_map/ppermute | solution.py:475
  18.9 326.5 %all-reduce.2.cloned.1.call-start = ((), (), s32[]{:S(2)}) async-start(), calls=%async_computation.4 | async-start | bytes 3973120 | tf_op jit(solution)/shard_map/psum | solution.py:634
  21.4 52.4 %collective-permute-start.15 = (bf16[96,768]{1,0:T(8,128)(2,1)S(1)}, bf16[96,768]{1,0:T(8,128)(2,1)S(1)}, u32[]{:S(2)}, u32[]{:S(2)}) collective-permute-start(bf16[96,768]{1,0:T(8,128)(2,1)S(1)} %constant_dynamic-slice_fusion.8), channel_id=1, source_target_pairs={{0,3},{1,0},{2,1},{3,2},{4,7},{5,4},{6,5},{7,6},{8,11},{9,8},{10,9... | collective-permute-start | bytes 442376 | tf_op jit(solution)/shard_map/ppermute | solution.py:475
  45.3 30.2 %collective-permute-start.23 = (f32[768]{0:T(1024)S(1)}, f32[768]{0:T(1024)S(1)}, u32[]{:S(2)}, u32[]{:S(2)}) collective-permute-start(f32[768]{0:T(1024)S(1)} %copy-done.39), channel_id=1, source_target_pairs={{0,1},{1,2},{2,3},{3,0},{4,5},{5,6},{6,7},{7,4},{8,9},{9,10},{10,1... | collective-permute-start | bytes 9224 | tf_op jit(solution)/shard_map/ppermute | solution.py:475
  58.4 31.8 %collective-permute-start.6 = (bf16[576,768]{1,0:T(8,128)(2,1)}, bf16[576,768]{1,0:T(8,128)(2,1)S(1)}, u32[]{:S(2)}, u32[]{:S(2)}) collective-permute-start(bf16[576,768]{1,0:T(8,128)(2,1)} %get-tuple-element.195.refs_4_), channel_id=1, source_target_pairs={{0,8},{4,12},{8,0},{12,4},{16,24},{20,28},{24,16},{28,20},{1,9},{5... | collective-permute-start | bytes 2654216 | tf_op jit(solution)/shard_map/ppermute | solution.py:408
  75.5 37.1 %collective-permute-start.7 = (bf16[576,768]{1,0:T(8,128)(2,1)}, bf16[576,768]{1,0:T(8,128)(2,1)S(1)}, u32[]{:S(2)}, u32[]{:S(2)}) collective-permute-start(bf16[576,768]{1,0:T(8,128)(2,1)} %get-tuple-element.195.refs_4_), channel_id=1, source_target_pairs={{0,16},{4,20},{8,24},{12,28},{16,0},{20,4},{24,8},{28,12},{1,17},{... | collective-permute-start | bytes 2654216 | tf_op jit(solution)/shard_map/ppermute | solution.py:410
  76.2 33.8 %collective-permute-start.16 = (bf16[384,768]{1,0:T(8,128)(2,1)S(1)}, bf16[384,768]{1,0:T(8,128)(2,1)}, u32[]{:S(2)}, u32[]{:S(2)}) collective-permute-start(bf16[384,768]{1,0:T(8,128)(2,1)S(1)} %pad_maximum_fusion.5.refs_12_), channel_id=1, source_target_pairs={{0,8},{4,12},{8,0},{12,4},{16,24},{20,28},{24,16},{28,20},{1,9},{5... | collective-permute-start | bytes 1769480 | tf_op jit(solution)/shard_map/ppermute | solution.py:411
  77.8 33.7 %collective-permute-start.19 = (bf16[384,768]{1,0:T(8,128)(2,1)S(1)}, bf16[384,768]{1,0:T(8,128)(2,1)}, u32[]{:S(2)}, u32[]{:S(2)}) collective-permute-start(bf16[384,768]{1,0:T(8,128)(2,1)S(1)} %pad_maximum_fusion.5.refs_12_), channel_id=1, source_target_pairs={{0,4},{4,0},{8,12},{12,8},{16,20},{20,16},{24,28},{28,24},{1,5},{5... | collective-permute-start | bytes 1769480 | tf_op jit(solution)/shard_map/ppermute | solution.py:498
  90.2 33.3 %collective-permute-start.8 = (bf16[576,768]{1,0:T(8,128)(2,1)S(1)}, bf16[576,768]{1,0:T(8,128)(2,1)}, u32[]{:S(2)}, u32[]{:S(2)}) collective-permute-start(bf16[576,768]{1,0:T(8,128)(2,1)S(1)} %collective-permute-done.6.refs_5_), channel_id=1, source_target_pairs={{0,16},{4,20},{8,24},{12,28},{16,0},{20,4},{24,8},{28,12},{1,17},{... | collective-permute-start | bytes 2654216 | tf_op jit(solution)/shard_map/ppermute | solution.py:412
  112.7 47.7 %collective-permute-start.10 = (bf16[576,768]{1,0:T(8,128)(2,1)S(1)}, bf16[576,768]{1,0:T(8,128)(2,1)}, u32[]{:S(2)}, u32[]{:S(2)}) collective-permute-start(bf16[576,768]{1,0:T(8,128)(2,1)S(1)} %collective-permute-done.6.refs_5_), channel_id=1, source_target_pairs={{0,4},{4,0},{8,12},{12,8},{16,20},{20,16},{24,28},{28,24},{1,5},{5... | collective-permute-start | bytes 2654216 | tf_op jit(solution)/shard_map/ppermute | solution.py:497
  113.3 51.3 %collective-permute-start.11 = (bf16[576,768]{1,0:T(8,128)(2,1)S(1)}, bf16[576,768]{1,0:T(8,128)(2,1)}, u32[]{:S(2)}, u32[]{:S(2)}) collective-permute-start(bf16[576,768]{1,0:T(8,128)(2,1)S(1)} %collective-permute-done.7.refs_6_), channel_id=1, source_target_pairs={{0,4},{4,0},{8,12},{12,8},{16,20},{20,16},{24,28},{28,24},{1,5},{5... | collective-permute-start | bytes 2654216 | tf_op jit(solution)/shard_map/ppermute | solution.py:497
  123.5 52.2 %collective-permute-start.12 = (bf16[576,768]{1,0:T(8,128)(2,1)}, bf16[576,768]{1,0:T(8,128)(2,1)}, u32[]{:S(2)}, u32[]{:S(2)}) collective-permute-start(bf16[576,768]{1,0:T(8,128)(2,1)} %collective-permute-done.8.refs_7_), channel_id=1, source_target_pairs={{0,4},{4,0},{8,12},{12,8},{16,20},{20,16},{24,28},{28,24},{1,5},{5... | collective-permute-start | bytes 2654216 | tf_op jit(solution)/shard_map/ppermute | solution.py:497
  125.7 32.3 %collective-permute-start.21 = (bf16[384,768]{1,0:T(8,128)(2,1)S(1)}, bf16[384,768]{1,0:T(8,128)(2,1)}, u32[]{:S(2)}, u32[]{:S(2)}) collective-permute-start(bf16[384,768]{1,0:T(8,128)(2,1)S(1)} %copy-done.26), channel_id=1, source_target_pairs={{0,4},{4,0},{8,12},{12,8},{16,20},{20,16},{24,28},{28,24},{1,5},{5... | collective-permute-start | bytes 1769480 | tf_op jit(solution)/shard_map/ppermute | solution.py:498
  125.7 34.6 %collective-permute-start.22 = (bf16[384,768]{1,0:T(8,128)(2,1)}, bf16[384,768]{1,0:T(8,128)(2,1)}, u32[]{:S(2)}, u32[]{:S(2)}) collective-permute-start(bf16[384,768]{1,0:T(8,128)(2,1)} %collective-permute-done.18.refs_15_), channel_id=1, source_target_pairs={{0,4},{4,0},{8,12},{12,8},{16,20},{20,16},{24,28},{28,24},{1,5},{5... | collective-permute-start | bytes 1769480 | tf_op jit(solution)/shard_map/ppermute | solution.py:498
  164.6 35.7 %collective-permute-start = (bf16[2,128,192]{2,1,0:T(8,128)(2,1)S(1)}, bf16[2,128,192]{2,1,0:T(8,128)(2,1)S(1)}, u32[]{:S(2)}, u32[]{:S(2)}) collective-permute-start(bf16[2,128,192]{2,1,0:T(8,128)(2,1)S(1)} %get-tuple-element.188), channel_id=1, source_target_pairs={{0,1},{1,2},{2,3},{3,0},{4,5},{5,6},{6,7},{7,4},{8,9},{9,10},{10,1... | collective-permute-start | bytes 294920 | tf_op jit(solution)/shard_map/ppermute | solution.py:475
  166.3 34.2 %collective-permute-start.1 = (bf16[2,128,192]{2,1,0:T(8,128)(2,1)S(1)}, bf16[2,128,192]{2,1,0:T(8,128)(2,1)S(1)}, u32[]{:S(2)}, u32[]{:S(2)}) collective-permute-start(bf16[2,128,192]{2,1,0:T(8,128)(2,1)S(1)} %get-tuple-element.187), channel_id=1, source_target_pairs={{0,2},{1,3},{2,0},{3,1},{4,6},{5,7},{6,4},{7,5},{8,10},{9,11},{10,... | collective-permute-start | bytes 294920 | tf_op jit(solution)/shard_map/ppermute | solution.py:475
  194.4 28.8 %collective-permute-start.29 = (bf16[256,192]{1,0:T(8,128)(2,1)}, bf16[256,192]{1,0:T(8,128)(2,1)S(1)}, u32[]{:S(2)}, u32[]{:S(2)}) collective-permute-start(bf16[256,192]{1,0:T(8,128)(2,1)} %get-tuple-element.80), channel_id=1, source_target_pairs={{0,3},{1,0},{2,1},{3,2},{4,7},{5,4},{6,5},{7,6},{8,11},{9,8},{10,9... | collective-permute-start | bytes 294920 | tf_op jit(solution)/shard_map/ppermute | solution.py:475
  194.5 29.8 %collective-permute-start.30 = (bf16[256,192]{1,0:T(8,128)(2,1)}, bf16[256,192]{1,0:T(8,128)(2,1)S(1)}, u32[]{:S(2)}, u32[]{:S(2)}) collective-permute-start(bf16[256,192]{1,0:T(8,128)(2,1)} %get-tuple-element.81), channel_id=1, source_target_pairs={{0,2},{1,3},{2,0},{3,1},{4,6},{5,7},{6,4},{7,5},{8,10},{9,11},{10,... | collective-permute-start | bytes 294920 | tf_op jit(solution)/shard_map/ppermute | solution.py:475
  266.2 107.2 %reduce-scatter.3.cloned.1.call-start = ((), (), s32[]{:S(2)}) async-start(), calls=%async_computation.2 | async-start | bytes 1966080 | tf_op jit(solution)/shard_map/reduce_scatter | solution.py:558
  266.8 141.2 %reduce-scatter.5.cloned.1.call-start = ((), (), s32[]{:S(2)}) async-start(), calls=%async_computation.3 | async-start | bytes 1966080 | tf_op jit(solution)/shard_map/reduce_scatter | solution.py:558
  275.0 57.2 %collective-permute-start.35 = (bf16[1536,768]{1,0:T(8,128)(2,1)}, bf16[1536,768]{1,0:T(8,128)(2,1)}, u32[]{:S(2)}, u32[]{:S(2)}) collective-permute-start(bf16[1536,768]{1,0:T(8,128)(2,1)} %slice.338), channel_id=1, source_target_pairs={{0,4},{4,0},{8,12},{12,8},{16,20},{20,16},{24,28},{28,24},{1,5},{5... | collective-permute-start | bytes 7077896 | tf_op jit(solution)/shard_map/ppermute | solution.py:572
  276.0 52.5 %collective-permute-start.36 = (bf16[768,768]{1,0:T(8,128)(2,1)S(1)}, bf16[768,768]{1,0:T(8,128)(2,1)}, u32[]{:S(2)}, u32[]{:S(2)}) collective-permute-start(bf16[768,768]{1,0:T(8,128)(2,1)S(1)} %bitcast_convert_fusion.2), channel_id=1, source_target_pairs={{0,4},{4,0},{8,12},{12,8},{16,20},{20,16},{24,28},{28,24},{1,5},{5... | collective-permute-start | bytes 3538952 | tf_op jit(solution)/shard_map/ppermute | solution.py:573
  283.3 57.0 %collective-permute-start.40 = (bf16[1536,768]{1,0:T(8,128)(2,1)}, bf16[1536,768]{1,0:T(8,128)(2,1)}, u32[]{:S(2)}, u32[]{:S(2)}) collective-permute-start(bf16[1536,768]{1,0:T(8,128)(2,1)} %slice.346), channel_id=1, source_target_pairs={{0,4},{4,0},{8,12},{12,8},{16,20},{20,16},{24,28},{28,24},{1,5},{5... | collective-permute-start | bytes 7077896 | tf_op jit(solution)/shard_map/ppermute | solution.py:571
  349.7 43.3 %collective-permute-start.39 = (bf16[576,768]{1,0:T(8,128)(2,1)}, bf16[576,768]{1,0:T(8,128)(2,1)}, u32[]{:S(2)}, u32[]{:S(2)}) collective-permute-start(bf16[576,768]{1,0:T(8,128)(2,1)} %pad_maximum_fusion.4), channel_id=1, source_target_pairs={{0,16},{4,20},{8,24},{12,28},{16,0},{20,4},{24,8},{28,12},{1,17},{... | collective-permute-start | bytes 2654216 | tf_op jit(solution)/shard_map/ppermute | solution.py:421
  362.3 29.2 %collective-permute-start.43 = (bf16[384,768]{1,0:T(8,128)(2,1)}, bf16[384,768]{1,0:T(8,128)(2,1)}, u32[]{:S(2)}, u32[]{:S(2)}) collective-permute-start(bf16[384,768]{1,0:T(8,128)(2,1)} %add_convert_fusion.6), channel_id=1, source_target_pairs={{0,16},{4,20},{8,24},{12,28},{16,0},{20,4},{24,8},{28,12},{1,17},{... | collective-permute-start | bytes 1769480 | tf_op jit(solution)/shard_map/ppermute | solution.py:424
  396.5 37.2 %collective-permute-start.45 = (bf16[240,768]{1,0:T(8,128)(2,1)S(1)}, bf16[240,768]{1,0:T(8,128)(2,1)}, u32[]{:S(2)}, u32[]{:S(2)}) collective-permute-start(bf16[240,768]{1,0:T(8,128)(2,1)S(1)} %pad_maximum_fusion.7), channel_id=1, source_target_pairs={{0,2},{1,3},{2,0},{3,1},{4,6},{5,7},{6,4},{7,5},{8,10},{9,11},{10,... | collective-permute-start | bytes 1105928 | tf_op jit(solution)/shard_map/ppermute | solution.py:475
  397.4 37.4 %collective-permute-start.46 = (bf16[240,768]{1,0:T(8,128)(2,1)}, bf16[240,768]{1,0:T(8,128)(2,1)S(1)}, u32[]{:S(2)}, u32[]{:S(2)}) collective-permute-start(bf16[240,768]{1,0:T(8,128)(2,1)} %pad_maximum_fusion.8), channel_id=1, source_target_pairs={{0,1},{1,2},{2,3},{3,0},{4,5},{5,6},{6,7},{7,4},{8,9},{9,10},{10,1... | collective-permute-start | bytes 1105928 | tf_op jit(solution)/shard_map/ppermute | solution.py:475
  (93 other events, 1176.3 us)
Sparse Core Ops, SparseCore 0:
  10.2 59.7 all-gather.6
  72.2 39.5 all-gather.4
  266.3 63.0 all-reduce.1
  331.7 34.8 reduce-scatter.2
  368.9 39.0 reduce-scatter.4

commit v2 on v1

v2 whole, which is shorter than its diff:
```python
import functools
import math

import jax
import jax.numpy as jnp
from jax import lax
from jax.experimental import pallas as pl
from jax.experimental.pallas import tpu as pltpu
from jax.sharding import PartitionSpec as P

EPSILON = 1e-12
MASKED = -1e30
F32 = jnp.float32
BF16 = jnp.bfloat16
VMEM_LIMIT = 60 * 1024 * 1024
UNROLL = 2
ANY = pl.BlockSpec(memory_space=pl.ANY)
VMEM = pl.BlockSpec(memory_space=pltpu.VMEM)
SMEM = pl.BlockSpec(memory_space=pltpu.SMEM)


def mm(a, b, ca, cb):
    return lax.dot_general(a, b, (((ca,), (cb,)), ((), ())), preferred_element_type=F32)


def cost(flops, moved, exps=0):
    return pl.CostEstimate(flops=int(flops), bytes_accessed=int(moved), transcendentals=int(exps))


def start(src, dst, sem):
    copy = pltpu.make_async_copy(src, dst, sem)
    copy.start()
    return copy

def attend_kernel(b, slots, heads, size, tok, w, bias, prev, seg, *refs):
    logits, probs, qkv, ctx = refs[-17:-13]
    tok_v, prev_v, logits_v, probs_v, qkv_v, ctx_v, w_v, qs, ks, vs = refs[-13:-3]
    sem_in, sem_out, sem_w = refs[-3:]
    length = tok_v.shape[1]
    width = heads * size
    w_in = start(w, w_v, sem_w)
    tok_in, prev_in = [], []
    for s in range(slots):
        tok_in.append(start(tok.at[s], tok_v.at[s], sem_in.at[s, heads]))
        if s == 0:
            prev_in += [start(prev.at[b, s, h], prev_v.at[s, h], sem_in.at[s, h]) for h in range(heads)]
    w_in.wait()
    for s in range(1, slots):
        prev_in += [start(prev.at[b, s, h], prev_v.at[s, h], sem_in.at[s, h]) for h in range(heads)]
    for copy in tok_in:
        copy.wait()

    def project(s, _):
        rows = (mm(tok_v[s], w_v[...], 1, 0) + bias[...]).astype(BF16)
        qkv_v[s] = rows
        start(qkv_v.at[s], qkv.at[s], sem_out.at[s, 2 * heads])
        for h in range(heads):
            at = h * size
            qs[s, h] = rows[:, at : at + size] * (1.0 / math.sqrt(size))
            ks[s, h] = rows[:, width + at : width + at + size]
            vs[s, h] = rows[:, 2 * width + at : 2 * width + at + size]
        return _

    lax.fori_loop(0, slots, project, 0)

    def one_head(i, _):
        s, h = i // heads, lax.rem(i, heads)
        seg_k = seg[b, pl.ds(s, 1), :]
        seg_q = jnp.broadcast_to(seg_k, (8, length)).T[:, :1]
        pltpu.make_async_copy(prev.at[b, s, h], prev_v.at[s, h], sem_in.at[s, h]).wait()
        q, k, v = qs[s, h], ks[s, h], vs[s, h]
        scores = mm(q, k, 1, 1) + prev_v[s, h].astype(F32)
        logits_v[s, h] = scores.astype(BF16)
        start(logits_v.at[s, h], logits.at[b, s, h], sem_out.at[s, h])
        masked = jnp.where(seg_q == seg_k, scores, MASKED)
        exponent = jnp.exp(masked - jnp.max(masked, -1, keepdims=True))
        p = (exponent * (1.0 / jnp.sum(exponent, -1, keepdims=True))).astype(BF16)
        probs_v[s, h] = p
        start(probs_v.at[s, h], probs.at[s, h], sem_out.at[s, heads + h])
        qs[s, h] = mm(p, v, 1, 0).astype(BF16)
        return _

    lax.fori_loop(0, slots * heads, one_head, 0)
    for s in range(slots):
        ctx_v[s] = jnp.concatenate([qs[s, h] for h in range(heads)], -1)
        start(ctx_v.at[s], ctx.at[s], sem_out.at[s, 2 * heads + 1])
    for s in range(slots):
        for h in range(heads):
            pltpu.make_async_copy(logits_v.at[s, h], logits.at[b, s, h], sem_out.at[s, h]).wait()
            pltpu.make_async_copy(probs_v.at[s, h], probs.at[s, h], sem_out.at[s, heads + h]).wait()
        pltpu.make_async_copy(qkv_v.at[s], qkv.at[s], sem_out.at[s, 2 * heads]).wait()
        pltpu.make_async_copy(ctx_v.at[s], ctx.at[s], sem_out.at[s, 2 * heads + 1]).wait()


def attend(b, complete, w_qkv, bias, prev_logits, seg, logits_in):
    slots, length, width = complete.shape
    heads = prev_logits.shape[2]
    cols = w_qkv.shape[1]
    size = cols // 3 // heads
    args = [complete, w_qkv, bias, prev_logits, seg]
    in_specs = [ANY, ANY, VMEM, ANY, VMEM]
    alias = {}
    if logits_in is not None:
        alias = {len(args): 0}
        args.append(logits_in)
        in_specs.append(ANY)
    n = slots * heads * length * length
    square = pltpu.VMEM((slots, heads, length, length), BF16)
    return pl.pallas_call(
        functools.partial(attend_kernel, b, slots, heads, size),
        in_specs=in_specs,
        out_specs=[ANY] * 4,
        out_shape=[
            jax.ShapeDtypeStruct(prev_logits.shape, BF16),
            jax.ShapeDtypeStruct((slots, heads, length, length), BF16),
            jax.ShapeDtypeStruct((slots, length, cols), BF16),
            jax.ShapeDtypeStruct((slots, length, cols // 3), BF16),
        ],
        scratch_shapes=[
            pltpu.VMEM((slots, length, width), BF16), square, square, square,
            pltpu.VMEM((slots, length, cols), BF16), pltpu.VMEM((slots, length, cols // 3), BF16),
            pltpu.VMEM((width, cols), BF16),
            *[pltpu.VMEM((slots, heads, length, size), BF16)] * 3,
            pltpu.SemaphoreType.DMA((slots, heads + 1)),
            pltpu.SemaphoreType.DMA((slots, 2 * heads + 2)), pltpu.SemaphoreType.DMA,
        ],
        input_output_aliases=alias,
        compiler_params=pltpu.CompilerParams(vmem_limit_bytes=VMEM_LIMIT),
        cost_estimate=cost(n * 1024 + 2 * slots * length * width * cols, n * 6, n),
        name="attend",
    )(*args)


def attend_back_kernel(micro, slots, heads, size, n_blocks, place, *refs):
    tok, qkv, ctx, probs = (refs[i * micro : (i + 1) * micro] for i in range(4))
    w, cot, *blocks = refs[4 * micro : 4 * micro + 2 + n_blocks]
    prev_grad, back, acc, bias_acc = refs[-17:-13]
    tok_v, qkv_v, ctx_v, dctx_v, probs_v, cot_v, grad_v, back_v, w_v, parts, deltas = refs[-13:-2]
    sem_in, sem_out = refs[-2:]
    length = tok_v.shape[1]
    width = heads * size
    local = blocks[0].shape[2]
    total = micro * slots
    first, later = [], []
    for s in range(total):
        b, t = divmod(s, slots)
        first += [
            start(qkv[b].at[t], qkv_v.at[s], sem_in.at[s, 0]),
            start(ctx[b].at[t], ctx_v.at[s], sem_in.at[s, 1]),
        ]
        for j in range(n_blocks):
            at = pl.ds(pl.multiple_of(place[j] * local, local), local)
            first.append(start(blocks[j].at[b, t], dctx_v.at[s, at], sem_in.at[s, 3 + j]))
    for s in range(total):
        b, t = divmod(s, slots)
        for h in range(heads):
            start(probs[b].at[t, h], probs_v.at[s, h], sem_in.at[s, 3 + n_blocks + h])
            start(cot.at[b, t, h], cot_v.at[s, h], sem_in.at[s, 3 + n_blocks + heads + h])
    later.append(start(w, w_v, sem_out.at[0, heads]))
    for s in range(total):
        b, t = divmod(s, slots)
        later.append(start(tok[b].at[t], tok_v.at[s], sem_in.at[s, 2]))
    for copy in first:
        copy.wait()

    def split(s, _):
        rows, d_all = qkv_v[s], dctx_v[s]
        product = d_all.astype(F32) * ctx_v[s].astype(F32)
        for h in range(heads):
            at = h * size
            parts[0, s, h] = rows[:, at : at + size]
            parts[1, s, h] = rows[:, width + at : width + at + size]
            parts[2, s, h] = rows[:, 2 * width + at : 2 * width + at + size]
            parts[3, s, h] = d_all[:, at : at + size]
            deltas[s, h] = jnp.sum(product[:, at : at + size], -1, keepdims=True)
        return _

    lax.fori_loop(0, total, split, 0)

    def leave(s, h):
        return pltpu.make_async_copy(
            grad_v.at[s, h], prev_grad.at[s // slots, lax.rem(s, slots), h], sem_out.at[s, h])

    def leave_back(s):
        return pltpu.make_async_copy(
            back_v.at[s], back.at[s // slots, lax.rem(s, slots)], sem_out.at[s, heads + 1])

    def one_head(i, _):
        s, h = i // heads, lax.rem(i, heads)
        pltpu.make_async_copy(
            probs[0].at[0, h], probs_v.at[s, h], sem_in.at[s, 3 + n_blocks + h]).wait()
        pltpu.make_async_copy(
            cot.at[0, 0, h], cot_v.at[s, h], sem_in.at[s, 3 + n_blocks + heads + h]).wait()
        q, k, v, d_context = (parts[j, s, h] for j in range(4))
        p = probs_v[s, h]
        d_scores = p.astype(F32) * (mm(d_context, v, 1, 1) - deltas[s, h]) + cot_v[s, h].astype(F32)
        grad_v[s, h] = d_scores
        leave(s, h).start()
        d_dots = (d_scores * (1.0 / math.sqrt(size))).astype(BF16)
        parts[0, s, h] = mm(d_dots, k, 1, 0).astype(BF16)
        parts[1, s, h] = mm(q, d_dots, 0, 0).T.astype(BF16)
        parts[2, s, h] = mm(d_context, p, 0, 0).T.astype(BF16)
        return _

    lax.fori_loop(0, total * heads, one_head, 0)
    for copy in later:
        copy.wait()
    acc[...] = jnp.zeros_like(acc)
    bias_acc[...] = jnp.zeros_like(bias_acc)

    def finish(s, _):
        d_qkv = jnp.concatenate([parts[j, s, h] for j in range(3) for h in range(heads)], -1)
        back_v[s] = mm(d_qkv, w_v[...], 1, 1).astype(BF16)
        leave_back(s).start()
        acc[...] += mm(tok_v[s], d_qkv, 0, 0)
        bias_acc[...] += jnp.sum(d_qkv.astype(F32), 0, keepdims=True)
        return _

    lax.fori_loop(0, total, finish, 0)
    for s in range(total):
        for h in range(heads):
            leave(s, h).wait()
        leave_back(s).wait()


def attend_back(place, complete, w_qkv, qkv, ctx, probs, logit_cot, blocks):
    micro, slots, heads, length, _ = logit_cot.shape
    width, cols = w_qkv.shape
    size = cols // 3 // heads
    args = [place, *complete, *qkv, *ctx, *probs, w_qkv, logit_cot, *blocks]
    n = micro * slots * heads * length * length
    total = micro * slots
    square = (total, heads, length, length)
    return pl.pallas_call(
        functools.partial(attend_back_kernel, micro, slots, heads, size, len(blocks)),
        in_specs=[SMEM] + [ANY] * (len(args) - 1),
        out_specs=[ANY, ANY, VMEM, VMEM],
        out_shape=[
            jax.ShapeDtypeStruct(logit_cot.shape, F32),
            jax.ShapeDtypeStruct((micro, slots, length, width), BF16),
            jax.ShapeDtypeStruct((width, cols), F32),
            jax.ShapeDtypeStruct((8, cols), F32),
        ],
        scratch_shapes=[
            pltpu.VMEM((total, length, width), BF16), pltpu.VMEM((total, length, cols), BF16),
            pltpu.VMEM((total, length, cols // 3), BF16),
            pltpu.VMEM((total, length, cols // 3), BF16),
            pltpu.VMEM(square, BF16), pltpu.VMEM(square, BF16), pltpu.VMEM(square, F32),
            pltpu.VMEM((total, length, width), BF16), pltpu.VMEM((width, cols), BF16),
            pltpu.VMEM((4, total, heads, length, size), BF16),
            pltpu.VMEM((total, heads, length, 1), F32),
            pltpu.SemaphoreType.DMA((total, 3 + len(blocks) + 2 * heads)),
            pltpu.SemaphoreType.DMA((total, heads + 2)),
        ],
        compiler_params=pltpu.CompilerParams(vmem_limit_bytes=VMEM_LIMIT),
        cost_estimate=cost(n * 2048 + 4 * total * length * width * cols, n * 8),
        name="attend_back",
    )(*args)


def gelu_and_slope(x):
    bell = jnp.exp(-0.5 * x * x)
    t = 1.0 / (1.0 + (0.3275911 * math.sqrt(0.5)) * jnp.abs(x))
    tail = t * (
        0.5 * 0.254829592
        + t * (
            0.5 * -0.284496736
            + t * (0.5 * 1.421413741 + t * (0.5 * -1.453152027 + t * (0.5 * 1.061405429)))
        )
    ) * bell
    phi = jnp.where(x >= 0, 1.0 - tail, tail)
    return x * phi, phi + x * (bell * (1.0 / math.sqrt(2.0 * math.pi)))


def norm_parts(u):
    centered = u - jnp.mean(u, -1, keepdims=True)
    r = lax.rsqrt(jnp.mean(centered * centered, -1, keepdims=True) + EPSILON)
    return centered * r, r


def norm_back(grad, gain, n, r):
    e = grad * gain
    return r * (e - jnp.mean(e, -1, keepdims=True) - n * jnp.mean(e * n, -1, keepdims=True))


def column_sum(u):
    return jnp.sum(u, 0, keepdims=True)


def feed_forward_kernel(micro, n_ctx, intake, place, refs_in, refs_out, scratch):
    ctx, (tok, cot, vectors, *weights) = refs_in[: micro * n_ctx], refs_in[micro * n_ctx :]
    b_out, g1, s1, b_down, g2, s2 = [vectors[i : i + 1, :] for i in range(6)]
    joint, (smalls, unit_sums), d_ctx = refs_out[:8], refs_out[8:10], refs_out[10:]
    slope, total, *held = scratch
    weights_v, held = held[: -14], held[-14:]
    w_out, b_in = weights_v[-2:]
    ctx_v, tok_v, cot_v, d_ctx_v, *joint_v, sem, io_sem = held
    out_v, act_v, branch_v, inner_v, low_v, att_v, all_v, res_v = joint_v
    units, width = slope.shape[1], total.shape[1]
    chunk = width
    head_width = ctx[0].shape[1]

    def leave(i):
        return pltpu.make_async_copy(joint_v[i], joint[i], io_sem.at[1, i])

    first = [start(tok, tok_v, io_sem.at[0, 0])]
    for i, c in enumerate(ctx):
        b, k = divmod(i, n_ctx)
        rows = pl.ds(b * c.shape[0], c.shape[0])
        first.append(start(c, ctx_v.at[k, rows], io_sem.at[3 + b, k]))
    wait_first, wait_units, weights_of = intake(place, weights, weights_v, sem)
    cot_in = start(cot, cot_v, io_sem.at[0, 1])
    for copy in first:
        copy.wait()
    wait_first()
    attended = b_out
    for k in range(n_ctx):
        attended = attended + mm(ctx_v[k], w_out[k].reshape(-1, width)[:head_width], 1, 0)
    all_v[...] = jnp.concatenate([ctx_v[k] for k in range(n_ctx)], -1)
    n1, r1 = norm_parts(tok_v[...].astype(F32) + attended)
    hidden = n1 * g1 + s1
    low_v[...] = hidden.astype(BF16)
    total[...] = hidden + b_down
    leave(4).start()
    leave(6).start()

    def forward(j, _):
        wait_units(j)
        at = pl.ds(pl.multiple_of(j * chunk, chunk), chunk)
        w_in, w_down = weights_of(j)
        pre = mm(low_v[...], w_in, 1, 1) + b_in[:, at]
        activated, grad = gelu_and_slope(pre)
        activated = activated.astype(BF16)
        act_v[:, at] = activated
        slope[:, at] = grad.astype(BF16)
        total[...] += mm(activated, w_down, 1, 0)
        return _

    lax.fori_loop(0, units // chunk, forward, 0, unroll=UNROLL)
    leave(1).start()
    n2, r2 = norm_parts(total[...])
    out_v[...] = (n2 * g2 + s2).astype(BF16)
    leave(0).start()
    cot_in.wait()
    g = cot_v[...].astype(F32)
    d_second = norm_back(g, g2, n2, r2)
    smalls[3:4, :] = column_sum(d_second)
    smalls[4:5, :] = column_sum(g * n2)
    smalls[5:6, :] = column_sum(g)
    branch_v[...] = d_second.astype(BF16)
    leave(2).start()
    total[...] = d_second

    def backward(j, _):
        at = pl.ds(pl.multiple_of(j * chunk, chunk), chunk)
        w_in, w_down = weights_of(j)
        d_act = mm(branch_v[...], w_down, 1, 1)
        d_inner = d_act * slope[:, at].astype(F32)
        unit_sums[:, at] = jnp.broadcast_to(column_sum(d_inner), (8, chunk))
        d_inner = d_inner.astype(BF16)
        inner_v[:, at] = d_inner
        total[...] += mm(d_inner, w_in, 1, 0)
        return _

    lax.fori_loop(0, units // chunk, backward, 0, unroll=UNROLL)
    leave(3).start()
    d_hidden = total[...]
    d_residual = norm_back(d_hidden, g1, n1, r1)
    d_att = d_residual.astype(BF16)
    for k in range(n_ctx):
        d_ctx_v[k] = mm(d_att, w_out[k].reshape(-1, width)[:head_width], 1, 1).astype(BF16)
        start(d_ctx_v.at[k], d_ctx[k], io_sem.at[2, k])
    att_v[...] = d_att
    res_v[...] = d_residual
    leave(5).start()
    leave(7).start()
    smalls[0:1, :] = column_sum(d_residual)
    smalls[1:2, :] = column_sum(d_hidden * n1)
    smalls[2:3, :] = column_sum(d_hidden)
    smalls[6:8, :] = jnp.zeros((2, width), F32)
    for k in range(n_ctx):
        pltpu.make_async_copy(d_ctx_v.at[k], d_ctx[k], io_sem.at[2, k]).wait()
    for i in range(8):
        leave(i).wait()


def relative_intake(place, weights, held, sem):
    own, *parts = weights
    packed, w_out, b_in = held
    n, mp, rows, width = packed.shape
    stages = [parts[j * n : (j + 1) * n] for j in range(len(parts) // n)]
    piece = b_in.shape[1] // (n * mp)
    pieces = 2 * piece

    def copies(i, at, sources):
        last = [pltpu.make_async_copy(
            own.at[at, pl.ds(pieces, rows - pieces)], packed.at[i, 0, pl.ds(pieces, rows - pieces)],
            sem.at[0, i])]
        main = [pltpu.make_async_copy(
            own.at[at, pl.ds(0, pieces)], packed.at[i, 0, pl.ds(0, pieces)], sem.at[1, i])]
        slot = 1
        for j in range(0, len(sources), 2):
            low, high = sources[j], sources[j + 1]
            slots, cut = pl.ds(slot, low.shape[0]), low.shape[1]
            slot += low.shape[0]
            last.append(pltpu.make_async_copy(
                high.at[:, pl.ds(pieces - cut, rows - pieces)],
                packed.at[i, slots, pl.ds(pieces, rows - pieces)], sem.at[2 + j, i]))
            main += [
                pltpu.make_async_copy(low, packed.at[i, slots, pl.ds(0, cut)], sem.at[3 + j, i]),
                pltpu.make_async_copy(
                    high.at[:, pl.ds(0, pieces - cut)],
                    packed.at[i, slots, pl.ds(cut, pieces - cut)], sem.at[6 + j, i]),
            ]
        return last, main

    for which in range(2):
        for i in range(n):
            for copy in copies(i, place[i], [stage[i] for stage in stages])[which]:
                copy.start()
    some = [stage[0] for stage in stages]

    def wait_first():
        for i in range(n):
            for copy in copies(i, 0, some)[0]:
                copy.wait()
            for s in range(mp):
                for j in range(2):
                    w_out[place[n + s], place[i] + n * j] = (
                        packed[i, s, pieces + 16 * j : pieces + 16 * j + 16]
                    )
                row = packed[i, s, pieces + 32 : pieces + 33, :].astype(F32)
                at = (i * mp + s) * piece
                b_in[:, at : at + piece] = (
                    row[:, :piece] + row[:, 128 : 128 + piece] + row[:, 256 : 256 + piece]
                )

    def wait_units(j):
        for half in range(2):
            for copy in copies(2 * j + half, 0, some)[1]:
                copy.wait()

    def units(j):
        at = pl.ds(2 * j, 2)
        return [packed[at, :, lo : lo + piece].reshape(-1, width) for lo in (0, piece)]

    return wait_first, wait_units, units


def whole_intake(place, weights, held, sem):
    w_in, w_down, w_out, b_in = held
    copies = [start(src, dst, sem.at[0, i]) for i, (src, dst) in enumerate(zip(weights, held))]

    def wait_first():
        for copy in copies:
            copy.wait()

    def units(j):
        return w_in[j], w_down[j]

    return wait_first, lambda j: None, units


def feed_forward(ctx, tokens, cot, vectors, place, weights, intake, block):
    rows, width = tokens.shape
    micro, n_ctx = len(ctx), len(ctx[0])
    head_width = ctx[0][0].shape[1]
    units, held_shapes = block
    args = [place, *[c for blocks in ctx for c in blocks], tokens, cot, vectors, *weights]
    in_specs = [SMEM] + [ANY] * (micro * n_ctx + 2) + [VMEM] + [ANY] * len(weights)
    joint_cols = [(width, BF16), (units, BF16), (width, BF16), (units, BF16), (width, BF16),
                  (width, BF16), (n_ctx * head_width, BF16), (width, F32)]
    n_args = len(args)
    n_out = len(joint_cols) + 2 + n_ctx

    def kernel(place, *refs):
        feed_forward_kernel(
            micro, n_ctx, intake, place, refs[: n_args - 1], refs[n_args - 1 : n_args - 1 + n_out],
            refs[n_args - 1 + n_out :],
        )

    heads_block = pltpu.VMEM((n_ctx, rows, head_width), BF16)
    outs = pl.pallas_call(
        kernel,
        in_specs=in_specs,
        out_specs=[ANY] * len(joint_cols) + [VMEM] * 2 + [ANY] * n_ctx,
        out_shape=[jax.ShapeDtypeStruct((rows, c), t) for c, t in joint_cols]
        + [jax.ShapeDtypeStruct((8, width), F32), jax.ShapeDtypeStruct((8, units), F32)]
        + [jax.ShapeDtypeStruct((rows, head_width), BF16)] * n_ctx,
        scratch_shapes=[
            pltpu.VMEM((rows, units), BF16), pltpu.VMEM((rows, width), F32),
            *[pltpu.VMEM(s, BF16) for s in held_shapes], pltpu.VMEM((1, units), F32),
            heads_block, pltpu.VMEM((rows, width), BF16), pltpu.VMEM((rows, width), BF16),
            heads_block, *[pltpu.VMEM((rows, c), t) for c, t in joint_cols],
            pltpu.SemaphoreType.DMA((9, 8)), pltpu.SemaphoreType.DMA((3 + micro, 8)),
        ],
        compiler_params=pltpu.CompilerParams(vmem_limit_bytes=VMEM_LIMIT),
        cost_estimate=cost(
            2 * rows * width * (4 * units + 2 * width), 4 * units * width + 20 * rows * width,
            rows * units,
        ),
        name="feed_forward",
    )(*args)
    n = len(joint_cols)
    return outs[:n], outs[n], outs[n + 1], outs[n + 2 :]


def weight_grad(half, mp, piece, place, act, branch, inner, low, ctx, att, d_out, got):
    rows, width = branch.shape
    span = mp * piece
    n = act.shape[1] // span // 2
    head_width = ctx.shape[1] // mp
    size = 2 * piece + 32
    cut = size // 2
    order = tuple(reversed(range(n)))

    def kernel(place, act, branch, inner, low, *refs):
        given, outs = refs[:2], refs[2:-7]
        act_v, inner_v, branch_v, low_v, got_v, out_v, sem = refs[-7:]
        moving = [start(low, low_v, sem.at[0, 0]), start(branch, branch_v, sem.at[0, 1])]
        loads, stores = {}, []
        for o in order:
            at = pl.ds((half * n + o) * span, span)
            loads[o] = [
                start(inner.at[:, at], inner_v.at[o], sem.at[1, o]),
                start(act.at[:, at], act_v.at[o], sem.at[2, o]),
            ]
            if not half:
                loads[o].append(start(given[1].at[o], got_v.at[o], sem.at[3, o]))
        if half:
            d_out = outs[1]
            d_out[...] = mm(given[0][...], given[1][...], 0, 0)
        else:
            d_out = given[0]
        for copy in moving:
            copy.wait()
        for o in order:
            for copy in loads[o]:
                copy.wait()
            d_in = mm(inner_v[o], low_v[...], 0, 0)
            d_down = mm(act_v[o], branch_v[...], 0, 0)
            first = place[half * n + o]
            second = jnp.minimum(2 * n + first, head_width // 16 - 1)
            for k in range(mp):
                parts = [d_in[k * piece : (k + 1) * piece], d_down[k * piece : (k + 1) * piece]]
                for p in (first, second):
                    at = place[2 * n + k] * head_width + p * 16
                    at = pl.ds(pl.multiple_of(at, 16), 16)
                    parts.append(d_out[at, :])
                row = 0
                for part in parts:
                    at = slice(row, row + part.shape[0])
                    if not half:
                        part = part.astype(BF16).astype(F32) + got_v[o, k, at].astype(F32)
                    out_v[o, k, at] = part.astype(BF16)
                    row += part.shape[0]
            if half:
                stores.append(start(out_v.at[o], outs[0].at[o], sem.at[4, o]))
            else:
                i = 2 * order.index(o)
                stores += [
                    start(out_v.at[o, :, pl.ds(0, cut)], outs[i], sem.at[4, o]),
                    start(out_v.at[o, :, pl.ds(cut, size - cut)], outs[i + 1], sem.at[5, o]),
                ]
        for copy in stores:
            copy.wait()

    last = (ctx.shape[1], width)
    args = [place, act, branch, inner, low]
    if half:
        args += [ctx, att]
        given_specs = [VMEM, VMEM]
        out_specs = [ANY, VMEM]
        out_shape = [
            jax.ShapeDtypeStruct((n, mp, size, width), BF16), jax.ShapeDtypeStruct(last, F32)
        ]
    else:
        args += [d_out, got]
        given_specs = [VMEM, ANY]
        out_specs = [ANY] * (2 * n)
        out_shape = [
            jax.ShapeDtypeStruct((mp, r, width), BF16) for _ in range(n) for r in (cut, size - cut)
        ]
    wide = pltpu.VMEM((n, rows, span), BF16)
    flat = pltpu.VMEM((rows, width), BF16)
    whole = pltpu.VMEM((n, mp, size, width), BF16)
    return pl.pallas_call(
        kernel,
        in_specs=[SMEM] + [ANY] * 4 + given_specs,
        out_specs=out_specs,
        out_shape=out_shape,
        scratch_shapes=[wide, wide, flat, flat, whole, whole, pltpu.SemaphoreType.DMA((6, n))],
        compiler_params=pltpu.CompilerParams(vmem_limit_bytes=VMEM_LIMIT),
        cost_estimate=cost(2 * rows * width * 5 * width, n * mp * width * 500),
        name="weight_grad",
    )(*args)


def joined(body, shapes, *args, name):
    return pl.pallas_call(
        body,
        out_shape=[jax.ShapeDtypeStruct(s, t) for s, t in shapes],
        compiler_params=pltpu.CompilerParams(vmem_limit_bytes=VMEM_LIMIT),
        name=name,
    )(*args)


def hop_sums(a1, a3, b2, b3):
    def hop_sum(a1, a3, b2, b3, a, b):
        a[...] = (a1[...].astype(F32) + a3[...].astype(F32)).astype(BF16)
        b[...] = (b2[...].astype(F32) + b3[...].astype(F32)).astype(BF16)

    shapes = [(a1.shape, BF16), (b2.shape, BF16)]
    return joined(hop_sum, shapes, a1, a3, b2, b3, name="hop_sum")


def plane_sums(here, a0, a1, a2, b0, b1, b2):
    mp, cut, width = a0.shape
    rows = cut + b0.shape[1]

    def plane_sum(here, a0, a1, a2, b0, b1, b2, out):
        for k in range(mp):
            z = here[k]
            for at, parts in ((slice(0, cut), (a0, a1, a2)), (slice(cut, rows), (b0, b1, b2))):
                out[z, at] = sum(p[k].astype(F32) for p in parts).astype(BF16)

    return pl.pallas_call(
        plane_sum,
        in_specs=[SMEM] + [VMEM] * 6,
        out_shape=jax.ShapeDtypeStruct((mp, rows, width), BF16),
        compiler_params=pltpu.CompilerParams(vmem_limit_bytes=VMEM_LIMIT),
        name="plane_sum",
    )(here, a0, a1, a2, b0, b1, b2)


def plane_gather(first, second, dp, between=lambda *arrays: arrays):
    x, y = flip_pairs(dp, 2), flip_pairs(dp, 4)
    a1, b2 = lax.ppermute(first, "dp", x), lax.ppermute(second, "dp", y)
    a2, b1 = lax.ppermute(first, "dp", y), lax.ppermute(second, "dp", x)
    a1, b2 = between(a1, b2)
    a3, b3 = lax.ppermute(a1, "dp", y), lax.ppermute(b2, "dp", x)
    return [first, a1, a2, a3], [second, b1, b2, b3]


def unpack_grads(packed, piece, head_width):
    n, rows, width = packed.shape

    def kernel(packed, d_in, d_down, d_out, pad, wide):
        for p in range(n):
            whole = packed[p].astype(F32)
            wide[p] = whole[:piece]
            d_down[p] = whole[piece : 2 * piece]
            pad[p] = whole[2 * piece : 2 * piece + 16]
            pad[n + p] = whole[2 * piece + 16 :]
        d_out[...] = pad[: head_width // 16]
        d_in[...] = wide[...].reshape(n * piece, width).T

    shapes = [(width, n * piece), (n, piece, width), (head_width // 16, 16, width)]
    return pl.pallas_call(
        kernel,
        out_shape=[jax.ShapeDtypeStruct(s, F32) for s in shapes],
        scratch_shapes=[pltpu.VMEM((2 * n, 16, width), F32), pltpu.VMEM((n, piece, width), F32)],
        compiler_params=pltpu.CompilerParams(vmem_limit_bytes=VMEM_LIMIT),
        name="unpack_grads",
    )(packed)


def shift_pairs(mp, k):
    return [(i, (i + k) % mp) for i in range(mp)]


def relay(array, mp):
    below, above = [array], [array]
    for hop in range(1, mp):
        pairs = [(i, i + 1) for i in range(hop - 1, mp - 1)]
        below.append(lax.ppermute(below[-1], "mp", pairs))
        above.append(lax.ppermute(above[-1], "mp", [(mp - 1 - i, mp - 1 - j) for i, j in pairs]))
    return below[1:], above[1:]


def flip_pairs(dp, bit):
    return [(i, i ^ bit) for i in range(dp)]


def tie(value, *others):
    return lax.optimization_barrier((value, others))[0]


def halves_of(array, core):
    half = array.shape[0] // 2
    return (
        lax.dynamic_slice_in_dim(array, core * half, half),
        lax.dynamic_slice_in_dim(array, (1 - core) * half, half),
    )


def reorder(rows, order):
    pick = (order[:, None] == jnp.arange(rows.shape[0])[None, :]).astype(F32)
    return jnp.dot(pick, rows, precision=lax.Precision.HIGHEST)


def on_device(
    tokens,
    prev_logits,
    segment_ids,
    query_weight,
    key_weight,
    value_weight,
    query_bias,
    value_bias,
    output_projection_weight,
    output_bias,
    first_gain,
    first_shift,
    inner_projection_weight,
    inner_bias,
    down_projection_weight,
    down_bias,
    second_gain,
    second_shift,
    output_cot,
    logit_cot,
):
    dp = lax.axis_size("dp")
    mp = lax.axis_size("mp")
    me = lax.axis_index("dp")
    mine = lax.axis_index("mp")
    micro_count, slots, local, width = tokens.shape
    length = prev_logits.shape[3]
    head_width = query_weight.shape[1]
    units = inner_projection_weight.shape[1]
    rows = slots * local
    packed = dp == 8 and mp == 4 and micro_count == 2 and units // dp == 96 and head_width == 192
    chips = dp // 2
    swap = flip_pairs(dp, 1)
    piece = units // dp

    def shifted(array, k):
        return lax.ppermute(array, "mp", shift_pairs(mp, k)) if k else array

    if packed:
        own_in = inner_projection_weight.T.reshape(dp, piece, width)
        own_down = down_projection_weight.reshape(dp, piece, width)
        own_out = output_projection_weight.reshape(-1, 16, width)
        high = inner_bias.astype(BF16)
        middle = (inner_bias - high.astype(F32)).astype(BF16)
        lowest = (inner_bias - high.astype(F32) - middle.astype(F32)).astype(BF16)
        own_bias = jnp.concatenate(
            [jnp.pad(v.reshape(dp, 1, piece), ((0, 0), (0, 15), (0, 128 - piece)))
             for v in (high, middle, lowest)]
            + [jnp.zeros((dp, 16, width - 3 * 128), BF16)], 2
        )
        own_out = jnp.concatenate([own_out, own_out[: 2 * dp - own_out.shape[0]]], 0)
        own_pack = jnp.concatenate([own_in, own_down, own_out[:dp], own_out[dp:], own_bias], 1)
        sent = lax.dynamic_index_in_dim(own_pack, me, 0, False)
        below, above = relay(sent, mp)
        first_hop = (below[0], above[0])
        from_z = jnp.stack(
            [jnp.where(mine >= k, below[k - 1], above[mp - k - 1]) for k in range(1, mp)]
        )
        k_of = jnp.arange(mp)
        cut = piece + piece // 3
        ff_place = me ^ (jnp.arange(dp) // chips + jnp.arange(dp) % chips * 2)
        ff_place = jnp.concatenate([ff_place, k_of]).astype(jnp.int32)
        intake = relative_intake
        block = (units * mp, [(dp, mp, 2 * piece + 48, width), (mp, 2 * dp, 16, width)])
    else:
        in_all = lax.all_gather(inner_projection_weight.T, "mp", axis=0, tiled=True)
        down_all = lax.all_gather(down_projection_weight, "mp", axis=0, tiled=True)
        wo_all = lax.all_gather(output_projection_weight, "mp")
        wo_all = jnp.stack(
            [lax.dynamic_index_in_dim(wo_all, (mine - k) % mp, 0, False) for k in range(mp)]
        )
        weights = [
            in_all.reshape(-1, width, width), down_all.reshape(-1, width, width), wo_all[:, None],
            lax.all_gather(inner_bias, "mp").reshape(1, -1),
        ]
        ff_place = jnp.zeros((dp,), jnp.int32)
        intake = whole_intake
        first_hop = ()
        square = (units * mp // width, width, width)
        block = (units * mp, [square, square, (mp, 1, head_width, width)])

    def gather_tokens(b, *after):
        return lax.all_gather(tie(tokens[b], *after), "mp", axis=1, tiled=True)

    complete = [gather_tokens(0, *first_hop)]
    for b in range(1, micro_count):
        complete.append(gather_tokens(b, complete[b - 1]))
    w_qkv = jnp.concatenate([query_weight, key_weight, value_weight], 1)
    bias_row = jnp.concatenate([query_bias, jnp.zeros_like(query_bias), value_bias])[None]
    vectors = jnp.stack(
        [output_bias, first_gain, first_shift, down_bias, second_gain, second_shift]
        + [jnp.zeros_like(down_bias)] * 2
    )
    own_tokens = tokens.reshape(-1, width)
    own_cot = output_cot.reshape(-1, width)
    place = jnp.stack([(mine + k) % mp for k in range(mp)]).astype(jnp.int32)
    logits = None

    def attend_fully(b, logits):
        logits, probs, qkv, ctx = attend(
            b, complete[b], w_qkv, bias_row, prev_logits, segment_ids, logits
        )
        blocks = []
        for k in range(mp):
            at = ((mine + k) % mp) * local
            part = lax.dynamic_slice(ctx, (0, at, 0), (slots, local, head_width))
            blocks.append(shifted(part, k).reshape(rows, head_width))
        return logits, (probs, qkv, ctx), blocks

    def to_heads(d_ctx):
        return [
            shifted(part, (mp - k) % mp).reshape(micro_count, slots, local, head_width)
            for k, part in enumerate(d_ctx)
        ]

    kept, blocks = [], []
    for b in range(micro_count):
        logits, each, ctx_blocks = attend_fully(b, logits)
        kept.append(each)
        blocks.append(ctx_blocks)
        if packed and b == 0:
            firsts, seconds = plane_gather(
                from_z[:, :cut], from_z[:, cut:], dp, lambda *arrays: tie(arrays, each[2])
            )
            firsts, seconds, blocks[0], complete[1] = lax.optimization_barrier(
                (firsts, seconds, blocks[0], complete[1])
            )
            weights = [own_pack]
            for group in (firsts, seconds):
                weights += group + [lax.ppermute(a, "dp", swap) for a in group]
    blocks = lax.optimization_barrier(blocks)
    joint, small, unit_sums, d_ctx = feed_forward(
        blocks, own_tokens, own_cot, vectors, ff_place, weights, intake, block
    )
    d_blocks = to_heads(d_ctx)
    layer, act, branch, inner, low, att, ctx_all, residual = joint

    def back_through(*after):
        d_blocks[0] = tie(d_blocks[0], *after)
        probs, qkv, ctx = zip(*kept)
        return attend_back(place, complete, w_qkv, qkv, ctx, probs, logit_cot, d_blocks)

    unit_total = unit_sums[0]
    if packed:
        z, i = jnp.meshgrid(jnp.arange(mp), jnp.arange(dp), indexing="ij")
        at = me ^ i
        at = ((at % 2 * chips + at // 2) * mp + k_of[(mine - z) % mp]).reshape(-1)
        unit_total = reorder(unit_total.reshape(-1, piece), at).reshape(-1)
    vector = jnp.concatenate([small[:6].reshape(-1), unit_total])
    cols = 3 * head_width
    vector = jnp.pad(vector, (0, -vector.shape[0] % (24 * cols))).reshape(-1, cols)
    at = width + 8
    def joint_grads(*after):
        return tie(jnp.concatenate([acc, bias_acc, vector], 0), *after)

    if packed:
        pairs = [act, branch, inner, low, ctx_all, att]
        other, d_out = weight_grad(1, mp, piece, ff_place, *pairs, None, None)
        got = lax.ppermute(other, "dp", swap)
        prev_grad, back, acc, bias_acc = back_through(d_out)
        got, prev_grad = lax.optimization_barrier((got, prev_grad))
        sums = weight_grad(0, mp, piece, ff_place, *pairs, d_out, got)
        cut = 2 * piece + 32 >> 1
        x, y = flip_pairs(dp, 2), flip_pairs(dp, 4)
        a3, b3, a2, b2, a1, b1, a0, b0 = sums
        a3, b3 = lax.ppermute(a3, "dp", y), lax.ppermute(b3, "dp", x)
        a2, b1 = lax.ppermute(a2, "dp", y), lax.ppermute(b1, "dp", x)
        a1, b2 = hop_sums(a1, a3, b2, b3)
        a1, b2 = lax.ppermute(a1, "dp", x), lax.ppermute(b2, "dp", y)
        back = lax.psum_scatter(back, "mp", scatter_dimension=2, tiled=True)
        a0, back = lax.optimization_barrier((a0, back))
        total = plane_sums(((mine - k_of) % mp).astype(jnp.int32), a0, a1, a2, b0, b1, b2)
        scattered = lax.psum_scatter(total, "mp", scatter_dimension=0)
        keep, send = halves_of(joint_grads(total), me % 2)
        keep = keep + lax.ppermute(send, "dp", swap)
        quarter = keep.shape[0] // 2
        top, low_part = keep[:quarter], keep[quarter:]
        top, low_part = (
            top + lax.ppermute(top, "dp", x), low_part + lax.ppermute(low_part, "dp", y)
        )
        top, low_part = (
            top + lax.ppermute(top, "dp", y), low_part + lax.ppermute(low_part, "dp", x)
        )
        keep = jnp.concatenate([top, low_part], 0)
        scattered, keep = lax.optimization_barrier((scattered, keep))
        gathered = lax.all_gather(scattered, "dp")
        other = lax.ppermute(keep, "dp", swap)
        summed = jnp.where(
            me % 2 == 0, jnp.concatenate([keep, other], 0), jnp.concatenate([other, keep], 0)
        )
        vector = summed[at:]
        for bit in (1, 2):
            vector += lax.ppermute(vector, "mp", flip_pairs(mp, bit))
        d_in, d_down, d_out = unpack_grads(gathered, piece, head_width)
        inner_weight_grad = d_in
        down_weight_grad = d_down.reshape(units, width)
        output_weight_grad = d_out.reshape(head_width, width)
    else:
        g_down = mm(act, branch, 0, 0)
        g_in = mm(inner, low, 0, 0)
        g_out = mm(ctx_all, att, 0, 0)
        vector = lax.psum(vector, "mp")
        prev_grad, back, acc, bias_acc = back_through()
        summed = lax.psum(joint_grads(), "dp")
        vector = summed[at:]
        back = lax.psum_scatter(back, "mp", scatter_dimension=2, tiled=True)
        g_in = lax.psum_scatter(g_in, "mp", scatter_dimension=0, tiled=True)
        inner_weight_grad = lax.psum(g_in, "dp").T
        g_down = lax.psum_scatter(g_down, "mp", scatter_dimension=0, tiled=True)
        down_weight_grad = lax.psum(g_down, "dp")
        g_out = g_out.reshape(mp, head_width, width)
        out_sum = 0.0
        for k in range(mp):
            out_sum += shifted(g_out[k], (mp - k) % mp)
        output_weight_grad = lax.psum(out_sum, "dp")
    token_grads = residual.reshape(tokens.shape) + back.astype(F32)
    vector = vector.reshape(-1)
    small = vector[: 6 * width].reshape(6, width)
    unit_total = vector[6 * width : 6 * width + units * mp]
    inner_bias_grad = lax.dynamic_index_in_dim(unit_total.reshape(mp, units), mine, 0, False)
    return (
        layer.reshape(tokens.shape),
        logits,
        token_grads,
        prev_grad,
        summed[:width, :head_width],
        summed[:width, head_width : 2 * head_width],
        summed[:width, 2 * head_width :],
        summed[width, :head_width],
        summed[width, 2 * head_width :],
        output_weight_grad,
        small[0],
        small[1],
        small[2],
        inner_weight_grad,
        inner_bias_grad,
        down_weight_grad,
        small[3],
        small[4],
        small[5],
    )


def solution(mesh):
    rows = P(None, "dp", "mp", None)
    heads = P(None, "dp", "mp", None, None)
    cols, deep, vec, same = P(None, "mp"), P("mp", None), P("mp"), P()
    in_specs = (
        rows, heads, P(None, "dp", None), cols, cols, cols, vec, vec, deep, same, same, same,
        cols, vec, deep, same, same, same, rows, heads,
    )
    out_specs = (
        rows, heads, rows, heads, cols, cols, cols, vec, vec, deep, same, same, same, cols, vec,
        deep, same, same, same,
    )
    return jax.shard_map(
        on_device, mesh=mesh, in_specs=in_specs, out_specs=out_specs, check_vma=False
    )
```

time: 474 us -> 382 us (0.81); the launches traced: 466 us -> 381 us
  waiting for transfers between devices: 125 us -> 169 us
  blocking collectives: 41.9 us -> 0 us
  local copies, waits for them, and re-layouts: 59.2 us -> 25.3 us
  starting transfers between devices: 78.2 us -> 52.7 us
  other arithmetic: 34.4 us -> 10.9 us
  matrix products: 9.31 us -> 0.19 us
  Pallas kernels: 102 us -> 108 us
    all_gather x2 -> x3, waiting for transfers between devices: 0.01 us -> 49.9 us  [the longest x2 34.7 us: gather_tokens(): return lax.all_gather(tie(tokens[b], *after), 'mp', axis=1, tiled=True)]
    psum x1 -> x0, blocking collectives: 41.9 us -> none  [on_device(): vector = lax.psum(vector, ('dp', 'mp'))]
    ppermute x24 -> x9, starting transfers between devices: 54.2 us -> 20.2 us  [shifted(): return lax.ppermute(array, 'mp', shift_pairs(mp, k)) if k else array]
    ppermute x24 -> x9, waiting for transfers between devices: 54.5 us -> 26 us  [shifted(): return lax.ppermute(array, 'mp', shift_pairs(mp, k)) if k else array]
    convert_element_type x12 -> x1, other arithmetic: 18.6 us -> 0.77 us  [on_device(): high = inner_bias.astype(BF16)]
    reduce_scatter x2, waiting for transfers between devices: 9.19 us -> 22 us  [the longest x1 21.6 us: on_device(): back = lax.psum_scatter(back, 'mp', scatter_dimension=2, tiled=True)]
    unnamed x133 -> x87, local copies, waits for them, and re-layouts: 22 us -> 10.1 us
    ppermute x37 -> x35, waiting for transfers between devices: 61 us -> 71.1 us  [the longest x3 15 us: relay(): lax.ppermute(above[-1], 'mp', [(mp - 1 - i, mp - 1 - j) for i, j in pairs])]
  transfers between devices with their start and end apart: 66 -> 49, of which waited for: 20 -> 25; matrix products, arithmetic and copies ran while one was open for 19% -> 6% of each run, Pallas kernels for 18% -> 19%
where the time goes in v2:
time: 382 us; the launch traced here: 381 us
  waiting for transfers between devices  169 us (44%)
  Pallas kernels  108 us (28%)
  starting transfers between devices  52.7 us (14%)
  local copies, waits for them, and re-layouts  25.3 us (7%)
  between operations  14.7 us (4%)
  other arithmetic  10.9 us (3%)
    all_gather x2, waiting for transfers between devices, gather_tokens(): return lax.all_gather(tie(tokens[b], *after), 'mp', axis=1, tiled=True)  34.7 us
    pallas_call x1, Pallas kernels, feed_forward(): pl.pallas_call(kernel, in_specs=in_specs, out_specs=[ANY] * len(joint_col...  29.1 us
    ppermute x9, waiting for transfers between devices, shifted(): return lax.ppermute(array, 'mp', shift_pairs(mp, k)) if k else array  26 us
    pallas_call x2, Pallas kernels, attend(): pl.pallas_call(functools.partial(attend_kernel, b, slots, heads, size), i...  25.8 us
    pallas_call x1, Pallas kernels, attend_back(): pl.pallas_call(functools.partial(attend_back_kernel, micro, slots, heads,...  23.5 us
    reduce_scatter x1, waiting for transfers between devices, on_device(): back = lax.psum_scatter(back, 'mp', scatter_dimension=2, tiled=True)  21.6 us
    ppermute x9, starting transfers between devices, shifted(): return lax.ppermute(array, 'mp', shift_pairs(mp, k)) if k else array  20.2 us
    pallas_call x2, Pallas kernels, weight_grad(): pl.pallas_call(kernel, in_specs=[SMEM] + [ANY] * 4 + given_specs, out_spe...  18.5 us
  transfers between devices with their start and end apart: 49, of which 25 were waited for; matrix products, arithmetic and copies ran while one was open for 6% of the time, Pallas kernels for 19%

profile of v2, /device:TPU:0, one launch (start us, length us, event | category | flops | bytes accessed | tf_op | source)
XLA Modules:
  0.0 380.8 jit_solution(6831296611049021369)
XLA Ops:
  16.2 5.0 %collective-permute-start = (bf16[240,768]{1,0:T(8,128)(2,1)S(1)}, bf16[240,768]{1,0:T(8,128)(2,1)S(1)}, u32[]{:S(2)}, u32[]{:S(2)}) collective-permute-start(bf16[240,768]{1,0:T(8,128)(2,1)S(1)} %dynamic-slice_bitcast_fusion), channel_id=1, source_target_pairs={{0,1},{1,2},{2,3},{4,5},{5,6},{6,7},{8,9},{9,10},{10,11},{12,13},{... | collective-permute-start | bytes 1105928 | tf_op jit(solution)/shard_map/ppermute | solution.py:676
  23.4 5.6 %collective-permute-done = bf16[240,768]{1,0:T(8,128)(2,1)S(1)} collective-permute-done((bf16[240,768]{1,0:T(8,128)(2,1)S(1)}, bf16[240,768]{1,0:T(8,128)(2,1)S(1)}, u32[]{:S(2)}, u32[]{:S(2)}) %collective-permute-start) | collective-permute-done | bytes 368672 | tf_op jit(solution)/shard_map/ppermute | solution.py:676
  28.9 4.1 %collective-permute-done.1 = bf16[240,768]{1,0:T(8,128)(2,1)S(1)} collective-permute-done((bf16[240,768]{1,0:T(8,128)(2,1)S(1)}, bf16[240,768]{1,0:T(8,128)(2,1)S(1)}, u32[]{:S(2)}, u32[]{:S(2)}) %collective-permute-start.1) | collective-permute-done | bytes 368672 | tf_op jit(solution)/shard_map/ppermute | solution.py:677
  35.1 34.7 %all-gather.5.cloned.1.call-done.tok.refs_0_ = bf16[2,512,768]{2,1,0:T(8,128)(2,1)} async-done(((bf16[2,128,768]{2,1,0:T(8,128)(2,1)}), bf16[2,512,768]{2,1,0:T(8,128)(2,1)}) %all-gather.5.cloned.1.call-update) | async-done | bytes 1572880 | tf_op jit(solution)/shard_map/all_gather | solution.py:785
  72.0 10.9 %collective-permute-done.3 = bf16[240,768]{1,0:T(8,128)(2,1)S(1)} collective-permute-done((bf16[240,768]{1,0:T(8,128)(2,1)S(1)}, bf16[240,768]{1,0:T(8,128)(2,1)S(1)}, u32[]{:S(2)}, u32[]{:S(2)}) %collective-permute-start.3) | collective-permute-done | bytes 368672 | tf_op jit(solution)/shard_map/ppermute | solution.py:677
  90.1 12.9 %attend.2 = (bf16[2,2,3,512,512]{4,3,2,1,0:T(8,128)(2,1)}, bf16[2,3,512,512]{3,2,1,0:T(8,128)(2,1)}, bf16[2,512,576]{2,1,0:T(8,128)(2,1)}, bf16[2,512,192]{2,1,0:T(8,128)(2,1)}) custom-call(bf16[2,512,768]{2,1,0:T(8,128)(2,1)} %all-gather.5.cloned.1.call-done.tok.refs_0_, bf16[768,576]{1,0:T(8,128)(2,1)} %pad_maximum_fusion.3.w.refs_8_, ...), custom_call_target="tpu_custom_call" | custom-call | flops 2516582400 | bytes 9437184 | tf_op jit(solution)/shard_map/attend/pallas_call | solution.py:109
  107.8 2.8 collective-permute-done.10.refs_21_
  110.7 6.9 %collective-permute-start.13 = (bf16[2,128,192]{2,1,0:T(8,128)(2,1)S(1)}, bf16[2,128,192]{2,1,0:T(8,128)(2,1)S(1)}, u32[]{:S(2)}, u32[]{:S(2)}) collective-permute-start(bf16[2,128,192]{2,1,0:T(8,128)(2,1)S(1)} %get-tuple-element.227), channel_id=1, source_target_pairs={{0,2},{1,3},{2,0},{3,1},{4,6},{5,7},{6,4},{7,5},{8,10},{9,11},{10,... | collective-permute-start | bytes 294920 | tf_op jit(solution)/shard_map/ppermute | solution.py:739
  117.6 3.4 collective-permute-start.14
  124.6 12.9 %attend.3 = (bf16[2,2,3,512,512]{4,3,2,1,0:T(8,128)(2,1)}, bf16[2,3,512,512]{3,2,1,0:T(8,128)(2,1)}, bf16[2,512,576]{2,1,0:T(8,128)(2,1)}, bf16[2,512,192]{2,1,0:T(8,128)(2,1)}) custom-call(bf16[2,512,768]{2,1,0:T(8,128)(2,1)} %all-gather.7.cloned.1.call-done.tok.refs_1_, ...), custom_call_target="tpu_custom_call", output_to_operand_aliasing={{0}: (5, {})} | custom-call | flops 2516582400 | bytes 9437184 | tf_op jit(solution)/shard_map/attend/pallas_call | solution.py:109
  140.3 4.2 %collective-permute-start.16 = (bf16[2,128,192]{2,1,0:T(8,128)(2,1)S(1)}, bf16[2,128,192]{2,1,0:T(8,128)(2,1)S(1)}, u32[]{:S(2)}, u32[]{:S(2)}) collective-permute-start(bf16[2,128,192]{2,1,0:T(8,128)(2,1)S(1)} %get-tuple-element.223), channel_id=1, source_target_pairs={{0,2},{1,3},{2,0},{3,1},{4,6},{5,7},{6,4},{7,5},{8,10},{9,11},{10,... | collective-permute-start | bytes 294920 | tf_op jit(solution)/shard_map/ppermute | solution.py:739
  144.6 3.9 %collective-permute-done.15 = bf16[2,128,192]{2,1,0:T(8,128)(2,1)S(1)} collective-permute-done((bf16[2,128,192]{2,1,0:T(8,128)(2,1)S(1)}, bf16[2,128,192]{2,1,0:T(8,128)(2,1)S(1)}, u32[]{:S(2)}, u32[]{:S(2)}) %collective-permute-start.15) | collective-permute-done | bytes 98336 | tf_op jit(solution)/shard_map/ppermute | solution.py:739
  150.3 3.5 collective-permute-done.16
  153.8 2.3 collective-permute-done.17
  161.5 29.1 %feed_forward.1 = (bf16[512,768]{1,0:T(8,128)(2,1)}, bf16[512,3072]{1,0:T(8,128)(2,1)}, bf16[512,768]{1,0:T(8,128)(2,1)}, bf16[512,3072]{1,0:T(8,128)(2,1)}, bf1...) custom-call(s32[12]{0:T(128)} %pad_add_fusion.place, ...), custom_call_target="tpu_custom_call" | custom-call | flops 10871635968 | bytes 17301504 | tf_op jit(solution)/shard_map/feed_forward/pallas_call | solution.py:483
  190.7 2.2 collective-permute-start.27
  193.5 9.1 %weight_grad.2 = (bf16[4,4,224,768]{3,2,1,0:T(8,128)(2,1)}, f32[768,768]{1,0:T(8,128)}) custom-call(s32[12]{0:T(128)} %pad_add_fusion.place, bf16[512,3072]{1,0:T(8,128)(2,1)} %get-tuple-element.124.act, bf16[512,768]{1,0:T(8,128)(2,1)} %get-tuple-element.125.branch, bf16[512,3072]{1,0:T(8,128)(2,1)} %get-tuple-element.126.inner, ...), custom_call_target="tpu_custom_call" | custom-call | flops 3019898880 | bytes 6144000 | tf_op jit(solution)/shard_map/weight_grad/pallas_call | solution.py:587
  203.3 13.4 %collective-permute-done.28 = bf16[512,192]{1,0:T(8,128)(2,1)S(1)} collective-permute-done((bf16[512,192]{1,0:T(8,128)(2,1)}, bf16[512,192]{1,0:T(8,128)(2,1)S(1)}, u32[]{:S(2)}, u32[]{:S(2)}) %collective-permute-start.28) | collective-permute-done | bytes 196640 | tf_op jit(solution)/shard_map/ppermute | solution.py:739
  217.5 23.5 %attend_back.1 = (f32[2,2,3,512,512]{4,3,2,1,0:T(8,128)}, bf16[2,2,512,768]{3,2,1,0:T(8,128)(2,1)}, f32[768,576]{1,0:T(8,128)}, f32[8,576]{1,0:T(8,128)}) custom-call(s32[4]{0:T(128)} %pad_add_fusion.1.place, bf16[2,512,768]{2,1,0:T(8,128)(2,1)} %all-gather.5.cloned.1.call-done.tok.refs_0_, bf16[2,512,768]{2,1,0:T(8,128)(2,1)} %all-gather.7.cloned.1.call-done.tok.refs_1_, ...), custom_call_target="tpu_custom_call" | custom-call | flops 10066329600 | bytes 25165824 | tf_op jit(solution)/shard_map/attend_back/pallas_call | solution.py:234
  241.2 9.4 %weight_grad.3 = (bf16[4,112,768]{2,1,0:T(8,128)(2,1)}, bf16[4,112,768]{2,1,0:T(8,128)(2,1)}, bf16[4,112,768]{2,1,0:T(8,128)(2,1)}, bf16[4,112,768]{2,1,0:T(8,12...) custom-call(s32[12]{0:T(128)} %pad_add_fusion.place, ...), custom_call_target="tpu_custom_call" | custom-call | flops 3019898880 | bytes 6144000 | tf_op jit(solution)/shard_map/weight_grad/pallas_call | solution.py:587
  254.2 2.0 collective-permute-start.34
  256.3 13.0 %collective-permute-done.30.a3 = bf16[4,112,768]{2,1,0:T(8,128)(2,1)S(1)} collective-permute-done((bf16[4,112,768]{2,1,0:T(8,128)(2,1)}, bf16[4,112,768]{2,1,0:T(8,128)(2,1)S(1)}, u32[]{:S(2)}, u32[]{:S(2)}) %collective-permute-start.30) | collective-permute-done | bytes 688160 | tf_op jit(solution)/shard_map/ppermute | solution.py:868
  271.6 3.0 hop_sum.1
  278.2 21.6 %reduce-scatter.3.cloned.1.call-done = bf16[2,2,128,768]{3,2,1,0:T(8,128)(2,1)} async-done(((bf16[2,2,512,768]{3,2,1,0:T(8,128)(2,1)}), bf16[2,2,128,768]{3,2,1,0:T(8,128)(2,1)}) %reduce-scatter.3.cloned.1.call-update) | async-done | bytes 786448 | tf_op jit(solution)/shard_map/reduce_scatter | solution.py:872
  300.9 3.7 plane_sum.1
  306.0 2.5 collective-permute-done.36
  311.7 10.8 %collective-permute-done.37 = f32[200,576]{1,0:T(8,128)S(1)} collective-permute-done((f32[200,576]{1,0:T(8,128)S(1)}, f32[200,576]{1,0:T(8,128)S(1)}, u32[]{:S(2)}, u32[]{:S(2)}) %collective-permute-start.37) | collective-permute-done | bytes 460832 | tf_op jit(solution)/shard_map/ppermute | solution.py:881
  326.0 10.7 %collective-permute-done.38 = f32[200,576]{1,0:T(8,128)S(1)} collective-permute-done((f32[200,576]{1,0:T(8,128)S(1)}, f32[200,576]{1,0:T(8,128)S(1)}, u32[]{:S(2)}, u32[]{:S(2)}) %collective-permute-start.38) | collective-permute-done | bytes 460832 | tf_op jit(solution)/shard_map/ppermute | solution.py:884
  343.9 3.2 collective-permute-done.42
  347.1 2.2 collective-permute-start.43
  354.6 15.1 %all-gather.9.cloned.1.call-done = bf16[1792,768]{1,0:T(8,128)(2,1)} async-done(((bf16[224,768]{1,0:T(8,128)(2,1)}), bf16[1792,768]{1,0:T(8,128)(2,1)}) %all-gather.9.cloned.1.call-update) | async-done | bytes 2752528 | tf_op jit(solution)/shard_map/all_gather | solution.py:888
  369.7 4.5 %unpack_grads.1 = (f32[768,768]{1,0:T(8,128)}, f32[8,96,768]{2,1,0:T(8,128)}, f32[12,16,768]{2,1,0:T(8,128)}) custom-call(bf16[8,224,768]{2,1,0:T(8,128)(2,1)} %bitcast.49), custom_call_target="tpu_custom_call" | custom-call | tf_op jit(solution)/shard_map/unpack_grads/pallas_call | solution.py:659
  (249 shorter events, 73.9 us)
Async XLA Ops:
  7.2 62.7 %all-gather.5.cloned.1.call-start = ((), (), s32[]{:S(2)}) async-start(), calls=%async_computation.2 | async-start | bytes 1966080 | tf_op jit(solution)/shard_map/all_gather | solution.py:785
  16.2 12.8 %collective-permute-start = (bf16[240,768]{1,0:T(8,128)(2,1)S(1)}, bf16[240,768]{1,0:T(8,128)(2,1)S(1)}, u32[]{:S(2)}, u32[]{:S(2)}) collective-permute-start(bf16[240,768]{1,0:T(8,128)(2,1)S(1)} %dynamic-slice_bitcast_fusion), channel_id=1, source_target_pairs={{0,1},{1,2},{2,3},{4,5},{5,6},{6,7},{8,9},{9,10},{10,11},{12,13},{... | collective-permute-start | bytes 1105928 | tf_op jit(solution)/shard_map/ppermute | solution.py:676
  33.1 90.8 %all-gather.7.cloned.1.call-start = ((), (), s32[]{:S(2)}) async-start(), calls=%async_computation.3 | async-start | bytes 1966080 | tf_op jit(solution)/shard_map/all_gather | solution.py:785
  33.1 36.8 %collective-permute-start.2 = (bf16[240,768]{1,0:T(8,128)(2,1)S(1)}, bf16[240,768]{1,0:T(8,128)(2,1)S(1)}, u32[]{:S(2)}, u32[]{:S(2)}) collective-permute-start(bf16[240,768]{1,0:T(8,128)(2,1)S(1)} %collective-permute-done.1), channel_id=1, source_target_pairs={{2,1},{1,0},{6,5},{5,4},{10,9},{9,8},{14,13},{13,12},{18,17},{17,1... | collective-permute-start | bytes 1105928 | tf_op jit(solution)/shard_map/ppermute | solution.py:677
  34.4 36.8 %collective-permute-start.4 = (bf16[240,768]{1,0:T(8,128)(2,1)S(1)}, bf16[240,768]{1,0:T(8,128)(2,1)S(1)}, u32[]{:S(2)}, u32[]{:S(2)}) collective-permute-start(bf16[240,768]{1,0:T(8,128)(2,1)S(1)} %collective-permute-done), channel_id=1, source_target_pairs={{1,2},{2,3},{5,6},{6,7},{9,10},{10,11},{13,14},{14,15},{17,18},{18... | collective-permute-start | bytes 1105928 | tf_op jit(solution)/shard_map/ppermute | solution.py:676
  69.9 229.9 %reduce-scatter.3.cloned.1.call-start = ((), (), s32[]{:S(2)}) async-start(), calls=%async_computation.4 | async-start | bytes 3932160 | tf_op jit(solution)/shard_map/reduce_scatter | solution.py:872
  69.9 13.0 %collective-permute-start.3 = (bf16[240,768]{1,0:T(8,128)(2,1)S(1)}, bf16[240,768]{1,0:T(8,128)(2,1)S(1)}, u32[]{:S(2)}, u32[]{:S(2)}) collective-permute-start(bf16[240,768]{1,0:T(8,128)(2,1)S(1)} %collective-permute-done.2), channel_id=1, source_target_pairs={{1,0},{5,4},{9,8},{13,12},{17,16},{21,20},{25,24},{29,28}} | collective-permute-start | bytes 1105928 | tf_op jit(solution)/shard_map/ppermute | solution.py:677
  83.3 19.7 %collective-permute-start.6 = (bf16[3,128,768]{2,1,0:T(8,128)(2,1)S(1)}, bf16[3,128,768]{2,1,0:T(8,128)(2,1)S(1)}, u32[]{:S(2)}, u32[]{:S(2)}) collective-permute-start(bf16[3,128,768]{2,1,0:T(8,128)(2,1)S(1)} %slice.115.refs_12_), channel_id=1, source_target_pairs={{0,8},{4,12},{8,0},{12,4},{16,24},{20,28},{24,16},{28,20},{1,9},{5... | collective-permute-start | bytes 1769480 | tf_op jit(solution)/shard_map/ppermute | solution.py:638
  84.9 18.1 %collective-permute-start.7 = (bf16[3,112,768]{2,1,0:T(8,128)(2,1)S(1)}, bf16[3,112,768]{2,1,0:T(8,128)(2,1)}, u32[]{:S(2)}, u32[]{:S(2)}) collective-permute-start(bf16[3,112,768]{2,1,0:T(8,128)(2,1)S(1)} %pad_maximum_fusion.4.refs_20_), channel_id=1, source_target_pairs={{0,16},{4,20},{8,24},{12,28},{16,0},{20,4},{24,8},{28,12},{1,17},{... | collective-permute-start | bytes 1548296 | tf_op jit(solution)/shard_map/ppermute | solution.py:638
  89.0 21.6 %collective-permute-start.10 = (bf16[3,112,768]{2,1,0:T(8,128)(2,1)S(1)}, bf16[3,112,768]{2,1,0:T(8,128)(2,1)S(1)}, u32[]{:S(2)}, u32[]{:S(2)}) collective-permute-start(bf16[3,112,768]{2,1,0:T(8,128)(2,1)S(1)} %pad_maximum_fusion.4.refs_20_), channel_id=1, source_target_pairs={{0,8},{4,12},{8,0},{12,4},{16,24},{20,28},{24,16},{28,20},{1,9},{5... | collective-permute-start | bytes 1548296 | tf_op jit(solution)/shard_map/ppermute | solution.py:639
  89.6 28.0 %collective-permute-start.8 = (bf16[3,128,768]{2,1,0:T(8,128)(2,1)S(1)}, bf16[3,128,768]{2,1,0:T(8,128)(2,1)S(1)}, u32[]{:S(2)}, u32[]{:S(2)}) collective-permute-start(bf16[3,128,768]{2,1,0:T(8,128)(2,1)S(1)} %slice.115.refs_12_), channel_id=1, source_target_pairs={{0,16},{4,20},{8,24},{12,28},{16,0},{20,4},{24,8},{28,12},{1,17},{... | collective-permute-start | bytes 1769480 | tf_op jit(solution)/shard_map/ppermute | solution.py:639
  103.0 20.9 %collective-permute-start.9 = (bf16[3,128,768]{2,1,0:T(8,128)(2,1)S(1)}, bf16[3,128,768]{2,1,0:T(8,128)(2,1)}, u32[]{:S(2)}, u32[]{:S(2)}) collective-permute-start(bf16[3,128,768]{2,1,0:T(8,128)(2,1)S(1)} %collective-permute-done.6.refs_13_), channel_id=1, source_target_pairs={{0,16},{4,20},{8,24},{12,28},{16,0},{20,4},{24,8},{28,12},{1,17},{... | collective-permute-start | bytes 1769480 | tf_op jit(solution)/shard_map/ppermute | solution.py:641
  104.6 19.3 %collective-permute-start.11 = (bf16[3,112,768]{2,1,0:T(8,128)(2,1)}, bf16[3,112,768]{2,1,0:T(8,128)(2,1)}, u32[]{:S(2)}, u32[]{:S(2)}) collective-permute-start(bf16[3,112,768]{2,1,0:T(8,128)(2,1)} %collective-permute-done.7.refs_22_), channel_id=1, source_target_pairs={{0,8},{4,12},{8,0},{12,4},{16,24},{20,28},{24,16},{28,20},{1,9},{5... | collective-permute-start | bytes 1548296 | tf_op jit(solution)/shard_map/ppermute | solution.py:641
  107.8 13.2 %collective-permute-start.12 = (bf16[2,128,192]{2,1,0:T(8,128)(2,1)S(1)}, bf16[2,128,192]{2,1,0:T(8,128)(2,1)S(1)}, u32[]{:S(2)}, u32[]{:S(2)}) collective-permute-start(bf16[2,128,192]{2,1,0:T(8,128)(2,1)S(1)} %get-tuple-element.228), channel_id=1, source_target_pairs={{0,1},{1,2},{2,3},{3,0},{4,5},{5,6},{6,7},{7,4},{8,9},{9,10},{10,1... | collective-permute-start | bytes 294920 | tf_op jit(solution)/shard_map/ppermute | solution.py:739
  123.9 32.2 %collective-permute-start.22 = (bf16[3,112,768]{2,1,0:T(8,128)(2,1)S(1)}, bf16[3,112,768]{2,1,0:T(8,128)(2,1)S(1)}, u32[]{:S(2)}, u32[]{:S(2)}) collective-permute-start(bf16[3,112,768]{2,1,0:T(8,128)(2,1)S(1)} %pad_maximum_fusion.4.refs_20_), channel_id=1, source_target_pairs={{0,4},{4,0},{8,12},{12,8},{16,20},{20,16},{24,28},{28,24},{1,5},{5... | collective-permute-start | bytes 1548296 | tf_op jit(solution)/shard_map/ppermute | solution.py:832
  124.0 32.7 %collective-permute-start.23 = (bf16[3,112,768]{2,1,0:T(8,128)(2,1)S(1)}, bf16[3,112,768]{2,1,0:T(8,128)(2,1)}, u32[]{:S(2)}, u32[]{:S(2)}) collective-permute-start(bf16[3,112,768]{2,1,0:T(8,128)(2,1)S(1)} %collective-permute-done.10.refs_21_), channel_id=1, source_target_pairs={{0,4},{4,0},{8,12},{12,8},{16,20},{20,16},{24,28},{28,24},{1,5},{5... | collective-permute-start | bytes 1548296 | tf_op jit(solution)/shard_map/ppermute | solution.py:832
  124.5 32.3 %collective-permute-start.24 = (bf16[3,112,768]{2,1,0:T(8,128)(2,1)}, bf16[3,112,768]{2,1,0:T(8,128)(2,1)}, u32[]{:S(2)}, u32[]{:S(2)}) collective-permute-start(bf16[3,112,768]{2,1,0:T(8,128)(2,1)} %collective-permute-done.7.refs_22_), channel_id=1, source_target_pairs={{0,4},{4,0},{8,12},{12,8},{16,20},{20,16},{24,28},{28,24},{1,5},{5... | collective-permute-start | bytes 1548296 | tf_op jit(solution)/shard_map/ppermute | solution.py:832
  140.3 13.5 %collective-permute-start.16 = (bf16[2,128,192]{2,1,0:T(8,128)(2,1)S(1)}, bf16[2,128,192]{2,1,0:T(8,128)(2,1)S(1)}, u32[]{:S(2)}, u32[]{:S(2)}) collective-permute-start(bf16[2,128,192]{2,1,0:T(8,128)(2,1)S(1)} %get-tuple-element.223), channel_id=1, source_target_pairs={{0,2},{1,3},{2,0},{3,1},{4,6},{5,7},{6,4},{7,5},{8,10},{9,11},{10,... | collective-permute-start | bytes 294920 | tf_op jit(solution)/shard_map/ppermute | solution.py:739
  192.9 23.8 %collective-permute-start.28 = (bf16[512,192]{1,0:T(8,128)(2,1)}, bf16[512,192]{1,0:T(8,128)(2,1)S(1)}, u32[]{:S(2)}, u32[]{:S(2)}) collective-permute-start(bf16[512,192]{1,0:T(8,128)(2,1)} %get-tuple-element.139), channel_id=1, source_target_pairs={{0,2},{1,3},{2,0},{3,1},{4,6},{5,7},{6,4},{7,5},{8,10},{9,11},{10,... | collective-permute-start | bytes 589832 | tf_op jit(solution)/shard_map/ppermute | solution.py:739
  193.2 23.5 %collective-permute-start.29 = (bf16[512,192]{1,0:T(8,128)(2,1)}, bf16[512,192]{1,0:T(8,128)(2,1)S(1)}, u32[]{:S(2)}, u32[]{:S(2)}) collective-permute-start(bf16[512,192]{1,0:T(8,128)(2,1)} %get-tuple-element.140), channel_id=1, source_target_pairs={{0,1},{1,2},{2,3},{3,0},{4,5},{5,6},{6,7},{7,4},{8,9},{9,10},{10,1... | collective-permute-start | bytes 589832 | tf_op jit(solution)/shard_map/ppermute | solution.py:739
  202.7 38.6 %collective-permute-start.26 = (bf16[4,4,224,768]{3,2,1,0:T(8,128)(2,1)}, bf16[4,4,224,768]{3,2,1,0:T(8,128)(2,1)}, u32[]{:S(2)}, u32[]{:S(2)}) collective-permute-start(bf16[4,4,224,768]{3,2,1,0:T(8,128)(2,1)} %get-tuple-element.131), channel_id=1, source_target_pairs={{0,4},{4,0},{8,12},{12,8},{16,20},{20,16},{24,28},{28,24},{1,5},{5... | collective-permute-start | bytes 16515080 | tf_op jit(solution)/shard_map/ppermute | solution.py:861
  241.0 97.2 %reduce-scatter.5.cloned.1.call-start = ((), (), s32[]{:S(2)}) async-start(), calls=%async_computation.5 | async-start | bytes 1720320 | tf_op jit(solution)/shard_map/reduce_scatter | solution.py:875
  250.6 18.6 %collective-permute-start.30 = (bf16[4,112,768]{2,1,0:T(8,128)(2,1)}, bf16[4,112,768]{2,1,0:T(8,128)(2,1)S(1)}, u32[]{:S(2)}, u32[]{:S(2)}) collective-permute-start(bf16[4,112,768]{2,1,0:T(8,128)(2,1)} %get-tuple-element.149), channel_id=1, source_target_pairs={{0,16},{4,20},{8,24},{12,28},{16,0},{20,4},{24,8},{28,12},{1,17},{... | collective-permute-start | bytes 2064392 | tf_op jit(solution)/shard_map/ppermute | solution.py:868
  252.1 18.6 %collective-permute-start.31 = (bf16[4,112,768]{2,1,0:T(8,128)(2,1)}, bf16[4,112,768]{2,1,0:T(8,128)(2,1)S(1)}, u32[]{:S(2)}, u32[]{:S(2)}) collective-permute-start(bf16[4,112,768]{2,1,0:T(8,128)(2,1)} %get-tuple-element.151), channel_id=1, source_target_pairs={{0,8},{4,12},{8,0},{12,4},{16,24},{20,28},{24,16},{28,20},{1,9},{5... | collective-permute-start | bytes 2064392 | tf_op jit(solution)/shard_map/ppermute | solution.py:868
  253.6 46.2 %collective-permute-start.33 = (bf16[4,112,768]{2,1,0:T(8,128)(2,1)}, bf16[4,112,768]{2,1,0:T(8,128)(2,1)S(1)}, u32[]{:S(2)}, u32[]{:S(2)}) collective-permute-start(bf16[4,112,768]{2,1,0:T(8,128)(2,1)} %get-tuple-element.153), channel_id=1, source_target_pairs={{0,16},{4,20},{8,24},{12,28},{16,0},{20,4},{24,8},{28,12},{1,17},{... | collective-permute-start | bytes 2064392 | tf_op jit(solution)/shard_map/ppermute | solution.py:869
  254.2 45.6 %collective-permute-start.34 = (bf16[4,112,768]{2,1,0:T(8,128)(2,1)}, bf16[4,112,768]{2,1,0:T(8,128)(2,1)S(1)}, u32[]{:S(2)}, u32[]{:S(2)}) collective-permute-start(bf16[4,112,768]{2,1,0:T(8,128)(2,1)} %get-tuple-element.155), channel_id=1, source_target_pairs={{0,8},{4,12},{8,0},{12,4},{16,24},{20,28},{24,16},{28,20},{1,9},{5... | collective-permute-start | bytes 2064392 | tf_op jit(solution)/shard_map/ppermute | solution.py:869
  274.5 25.3 %collective-permute-start.32 = (bf16[4,112,768]{2,1,0:T(8,128)(2,1)}, bf16[4,112,768]{2,1,0:T(8,128)(2,1)}, u32[]{:S(2)}, u32[]{:S(2)}) collective-permute-start(bf16[4,112,768]{2,1,0:T(8,128)(2,1)} %get-tuple-element.152), channel_id=1, source_target_pairs={{0,8},{4,12},{8,0},{12,4},{16,24},{20,28},{24,16},{28,20},{1,9},{5... | collective-permute-start | bytes 2064392 | tf_op jit(solution)/shard_map/ppermute | solution.py:871
  274.5 25.3 %collective-permute-start.35 = (bf16[4,112,768]{2,1,0:T(8,128)(2,1)}, bf16[4,112,768]{2,1,0:T(8,128)(2,1)}, u32[]{:S(2)}, u32[]{:S(2)}) collective-permute-start(bf16[4,112,768]{2,1,0:T(8,128)(2,1)} %get-tuple-element.156), channel_id=1, source_target_pairs={{0,16},{4,20},{8,24},{12,28},{16,0},{20,4},{24,8},{28,12},{1,17},{... | collective-permute-start | bytes 2064392 | tf_op jit(solution)/shard_map/ppermute | solution.py:871
  305.7 64.0 %all-gather.9.cloned.1.call-start = ((), (), s32[]{:S(2)}) async-start(), calls=%async_computation.6 | async-start | bytes 3096576 | tf_op jit(solution)/shard_map/all_gather | solution.py:888
  308.7 13.8 %collective-permute-start.37 = (f32[200,576]{1,0:T(8,128)S(1)}, f32[200,576]{1,0:T(8,128)S(1)}, u32[]{:S(2)}, u32[]{:S(2)}) collective-permute-start(f32[200,576]{1,0:T(8,128)S(1)} %get-tuple-element.218), channel_id=1, source_target_pairs={{0,8},{4,12},{8,0},{12,4},{16,24},{20,28},{24,16},{28,20},{1,9},{5... | collective-permute-start | bytes 1382408 | tf_op jit(solution)/shard_map/ppermute | solution.py:881
  310.2 13.4 %collective-permute-start.39 = (f32[200,576]{1,0:T(8,128)S(1)}, f32[200,576]{1,0:T(8,128)S(1)}, u32[]{:S(2)}, u32[]{:S(2)}) collective-permute-start(f32[200,576]{1,0:T(8,128)S(1)} %get-tuple-element.219), channel_id=1, source_target_pairs={{0,16},{4,20},{8,24},{12,28},{16,0},{20,4},{24,8},{28,12},{1,17},{... | collective-permute-start | bytes 1382408 | tf_op jit(solution)/shard_map/ppermute | solution.py:881
  323.9 12.7 %collective-permute-start.38 = (f32[200,576]{1,0:T(8,128)S(1)}, f32[200,576]{1,0:T(8,128)S(1)}, u32[]{:S(2)}, u32[]{:S(2)}) collective-permute-start(f32[200,576]{1,0:T(8,128)S(1)} %get-tuple-element.216), channel_id=1, source_target_pairs={{0,16},{4,20},{8,24},{12,28},{16,0},{20,4},{24,8},{28,12},{1,17},{... | collective-permute-start | bytes 1382408 | tf_op jit(solution)/shard_map/ppermute | solution.py:884
  (57 other events, 726.1 us)
Sparse Core Ops, SparseCore 0:
  33.2 36.5 all-gather.4
  72.0 40.3 all-gather.6
  241.2 58.5 reduce-scatter.2
  305.8 32.4 reduce-scatter.4
  340.2 29.4 all-gather.8

commit v3 on v2

--- a/solution.py
+++ b/solution.py
@@ -134,7 +134,7 @@
 def attend_back_kernel(micro, slots, heads, size, n_blocks, place, *refs):
     tok, qkv, ctx, probs = (refs[i * micro : (i + 1) * micro] for i in range(4))
     w, cot, *blocks = refs[4 * micro : 4 * micro + 2 + n_blocks]
-    prev_grad, back, acc, bias_acc = refs[-17:-13]
+    prev_grad, acc, bias_acc, *backs = refs[-16 - micro : -13]
     tok_v, qkv_v, ctx_v, dctx_v, probs_v, cot_v, grad_v, back_v, w_v, parts, deltas = refs[-13:-2]
     sem_in, sem_out = refs[-2:]
     length = tok_v.shape[1]
@@ -181,9 +181,9 @@
         return pltpu.make_async_copy(
             grad_v.at[s, h], prev_grad.at[s // slots, lax.rem(s, slots), h], sem_out.at[s, h])
 
-    def leave_back(s):
+    def leave_back(s, b):
         return pltpu.make_async_copy(
-            back_v.at[s], back.at[s // slots, lax.rem(s, slots)], sem_out.at[s, heads + 1])
+            back_v.at[s], backs[b].at[lax.rem(s, slots)], sem_out.at[s, heads + 1])
 
     def one_head(i, _):
         s, h = i // heads, lax.rem(i, heads)
@@ -211,7 +211,8 @@
     def finish(s, _):
         d_qkv = jnp.concatenate([parts[j, s, h] for j in range(3) for h in range(heads)], -1)
         back_v[s] = mm(d_qkv, w_v[...], 1, 1).astype(BF16)
-        leave_back(s).start()
+        for b in range(micro):
+            pl.when(s // slots == b)(leave_back(s, b).start)
         acc[...] += mm(tok_v[s], d_qkv, 0, 0)
         bias_acc[...] += jnp.sum(d_qkv.astype(F32), 0, keepdims=True)
         return _
@@ -220,7 +221,7 @@
     for s in range(total):
         for h in range(heads):
             leave(s, h).wait()
-        leave_back(s).wait()
+        leave_back(s, 0).wait()
 
 
 def attend_back(place, complete, w_qkv, qkv, ctx, probs, logit_cot, blocks):
@@ -234,13 +235,13 @@
     return pl.pallas_call(
         functools.partial(attend_back_kernel, micro, slots, heads, size, len(blocks)),
         in_specs=[SMEM] + [ANY] * (len(args) - 1),
-        out_specs=[ANY, ANY, VMEM, VMEM],
+        out_specs=[ANY, VMEM, VMEM] + [ANY] * micro,
         out_shape=[
             jax.ShapeDtypeStruct(logit_cot.shape, F32),
-            jax.ShapeDtypeStruct((micro, slots, length, width), BF16),
             jax.ShapeDtypeStruct((width, cols), F32),
             jax.ShapeDtypeStruct((8, cols), F32),
-        ],
+        ]
+        + [jax.ShapeDtypeStruct((slots, length, width), BF16)] * micro,
         scratch_shapes=[
             pltpu.VMEM((total, length, width), BF16), pltpu.VMEM((total, length, cols), BF16),
             pltpu.VMEM((total, length, cols // 3), BF16),
@@ -642,12 +643,17 @@
     return [first, a1, a2, a3], [second, b1, b2, b3]
 
 
-def unpack_grads(packed, piece, head_width):
-    n, rows, width = packed.shape
-
-    def kernel(packed, d_in, d_down, d_out, pad, wide):
-        for p in range(n):
-            whole = packed[p].astype(F32)
+def gather_grads(place, units, piece, head_width, firsts, seconds):
+    n = len(firsts)
+    cut, width = firsts[0].shape
+    rows = cut + seconds[0].shape[0]
+
+    def kernel(place, *refs):
+        parts, (d_in, d_down, d_out) = refs[: 2 * n], refs[2 * n : 2 * n + 3]
+        pad, wide = refs[-2:]
+        for i in range(n):
+            p = place[i]
+            whole = jnp.concatenate([parts[i][...], parts[n + i][...]], 0).astype(F32)
             wide[p] = whole[:piece]
             d_down[p] = whole[piece : 2 * piece]
             pad[p] = whole[2 * piece : 2 * piece + 16]
@@ -655,14 +661,16 @@
         d_out[...] = pad[: head_width // 16]
         d_in[...] = wide[...].reshape(n * piece, width).T
 
+    vmem = [VMEM] * (2 * n)
     shapes = [(width, n * piece), (n, piece, width), (head_width // 16, 16, width)]
     return pl.pallas_call(
         kernel,
+        in_specs=[SMEM] + vmem,
         out_shape=[jax.ShapeDtypeStruct(s, F32) for s in shapes],
         scratch_shapes=[pltpu.VMEM((2 * n, 16, width), F32), pltpu.VMEM((n, piece, width), F32)],
         compiler_params=pltpu.CompilerParams(vmem_limit_bytes=VMEM_LIMIT),
-        name="unpack_grads",
-    )(packed)
+        name="gather_grads",
+    )(place, *firsts, *seconds)
 
 
 def shift_pairs(mp, k):
@@ -754,7 +762,7 @@
         own_pack = jnp.concatenate([own_in, own_down, own_out[:dp], own_out[dp:], own_bias], 1)
         sent = lax.dynamic_index_in_dim(own_pack, me, 0, False)
         below, above = relay(sent, mp)
-        first_hop = (below[0], above[0])
+        second_hop = (below[1], above[1])
         from_z = jnp.stack(
             [jnp.where(mine >= k, below[k - 1], above[mp - k - 1]) for k in range(1, mp)]
         )
@@ -777,16 +785,16 @@
         ]
         ff_place = jnp.zeros((dp,), jnp.int32)
         intake = whole_intake
-        first_hop = ()
+        second_hop = ()
         square = (units * mp // width, width, width)
         block = (units * mp, [square, square, (mp, 1, head_width, width)])
 
     def gather_tokens(b, *after):
         return lax.all_gather(tie(tokens[b], *after), "mp", axis=1, tiled=True)
 
-    complete = [gather_tokens(0, *first_hop)]
+    complete = [gather_tokens(0)]
     for b in range(1, micro_count):
-        complete.append(gather_tokens(b, complete[b - 1]))
+        complete.append(gather_tokens(b, *second_hop))
     w_qkv = jnp.concatenate([query_weight, key_weight, value_weight], 1)
     bias_row = jnp.concatenate([query_bias, jnp.zeros_like(query_bias), value_bias])[None]
     vectors = jnp.stack(
@@ -824,8 +832,8 @@
             firsts, seconds = plane_gather(
                 from_z[:, :cut], from_z[:, cut:], dp, lambda *arrays: tie(arrays, each[2])
             )
-            firsts, seconds, blocks[0], complete[1] = lax.optimization_barrier(
-                (firsts, seconds, blocks[0], complete[1])
+            firsts[-1], seconds[-1], blocks[0] = lax.optimization_barrier(
+                (firsts[-1], seconds[-1], blocks[0])
             )
             weights = [own_pack]
             for group in (firsts, seconds):
@@ -852,6 +860,9 @@
     cols = 3 * head_width
     vector = jnp.pad(vector, (0, -vector.shape[0] % (24 * cols))).reshape(-1, cols)
     at = width + 8
+    def scatter_tokens(back):
+        return lax.psum_scatter(back, "mp", scatter_dimension=1, tiled=True)
+
     def joint_grads(*after):
         return tie(jnp.concatenate([acc, bias_acc, vector], 0), *after)
 
@@ -859,20 +870,22 @@
         pairs = [act, branch, inner, low, ctx_all, att]
         other, d_out = weight_grad(1, mp, piece, ff_place, *pairs, None, None)
         got = lax.ppermute(other, "dp", swap)
-        prev_grad, back, acc, bias_acc = back_through(d_out)
-        got, prev_grad = lax.optimization_barrier((got, prev_grad))
         sums = weight_grad(0, mp, piece, ff_place, *pairs, d_out, got)
+        prev_grad, acc, bias_acc, *backs = back_through(sums)
         cut = 2 * piece + 32 >> 1
         x, y = flip_pairs(dp, 2), flip_pairs(dp, 4)
         a3, b3, a2, b2, a1, b1, a0, b0 = sums
         a3, b3 = lax.ppermute(a3, "dp", y), lax.ppermute(b3, "dp", x)
         a2, b1 = lax.ppermute(a2, "dp", y), lax.ppermute(b1, "dp", x)
+        a1, a2, b1, prev_grad = lax.optimization_barrier((a1, a2, b1, prev_grad))
         a1, b2 = hop_sums(a1, a3, b2, b3)
+        backs[0] = tie(backs[0], a1)
         a1, b2 = lax.ppermute(a1, "dp", x), lax.ppermute(b2, "dp", y)
-        back = lax.psum_scatter(back, "mp", scatter_dimension=2, tiled=True)
-        a0, back = lax.optimization_barrier((a0, back))
         total = plane_sums(((mine - k_of) % mp).astype(jnp.int32), a0, a1, a2, b0, b1, b2)
+        backs[0] = scatter_tokens(backs[0])
+        backs[0], total = lax.optimization_barrier((backs[0], total))
         scattered = lax.psum_scatter(total, "mp", scatter_dimension=0)
+        backs[1:] = [scatter_tokens(tie(back, scattered)) for back in backs[1:]]
         keep, send = halves_of(joint_grads(total), me % 2)
         keep = keep + lax.ppermute(send, "dp", swap)
         quarter = keep.shape[0] // 2
@@ -884,8 +897,9 @@
             top + lax.ppermute(top, "dp", y), low_part + lax.ppermute(low_part, "dp", x)
         )
         keep = jnp.concatenate([top, low_part], 0)
-        scattered, keep = lax.optimization_barrier((scattered, keep))
-        gathered = lax.all_gather(scattered, "dp")
+        firsts, seconds = plane_gather(scattered[:cut], scattered[cut:], dp)
+        firsts += [lax.ppermute(a, "dp", swap) for a in firsts]
+        seconds += [lax.ppermute(a, "dp", swap) for a in seconds]
         other = lax.ppermute(keep, "dp", swap)
         summed = jnp.where(
             me % 2 == 0, jnp.concatenate([keep, other], 0), jnp.concatenate([other, keep], 0)
@@ -893,7 +907,9 @@
         vector = summed[at:]
         for bit in (1, 2):
             vector += lax.ppermute(vector, "mp", flip_pairs(mp, bit))
-        d_in, d_down, d_out = unpack_grads(gathered, piece, head_width)
+        firsts[-1], vector = lax.optimization_barrier((firsts[-1], vector))
+        d_in, d_down, d_out = gather_grads(ff_place, units, piece, head_width, firsts, seconds)
+        backs[-1] = tie(backs[-1], d_in)
         inner_weight_grad = d_in
         down_weight_grad = d_down.reshape(units, width)
         output_weight_grad = d_out.reshape(head_width, width)
@@ -902,10 +918,10 @@
         g_in = mm(inner, low, 0, 0)
         g_out = mm(ctx_all, att, 0, 0)
         vector = lax.psum(vector, "mp")
-        prev_grad, back, acc, bias_acc = back_through()
+        prev_grad, acc, bias_acc, *backs = back_through()
         summed = lax.psum(joint_grads(), "dp")
         vector = summed[at:]
-        back = lax.psum_scatter(back, "mp", scatter_dimension=2, tiled=True)
+        backs = [scatter_tokens(back) for back in backs]
         g_in = lax.psum_scatter(g_in, "mp", scatter_dimension=0, tiled=True)
         inner_weight_grad = lax.psum(g_in, "dp").T
         g_down = lax.psum_scatter(g_down, "mp", scatter_dimension=0, tiled=True)
@@ -915,7 +931,7 @@
         for k in range(mp):
             out_sum += shifted(g_out[k], (mp - k) % mp)
         output_weight_grad = lax.psum(out_sum, "dp")
-    token_grads = residual.reshape(tokens.shape) + back.astype(F32)
+    token_grads = residual.reshape(tokens.shape) + jnp.stack(backs).astype(F32)
     vector = vector.reshape(-1)
     small = vector[: 6 * width].reshape(6, width)
     unit_total = vector[6 * width : 6 * width + units * mp]

time: 382 us -> 372 us (0.974); the launches traced: 381 us -> 365 us
  waiting for transfers between devices: 169 us -> 151 us
    all_gather x2, waiting for transfers between devices: 34.7 us -> 0.01 us  [gather_tokens(): return lax.all_gather(tie(tokens[b], *after), 'mp', axis=1, tiled=True)]
    ppermute x3, waiting for transfers between devices: 15 us -> 48.5 us  [relay(): lax.ppermute(above[-1], 'mp', [(mp - 1 - i, mp - 1 - j) for i, j in pairs])]
    ppermute x2, waiting for transfers between devices: 0.01 us -> 15.5 us  [on_device(): a1, b2 = (lax.ppermute(a1, 'dp', x), lax.ppermute(b2, 'dp', y))]
    all_gather x1 -> x0, waiting for transfers between devices: 15.1 us -> none  [on_device(): gathered = lax.all_gather(scattered, 'dp')]
    ppermute x2, waiting for transfers between devices: 14.4 us -> 0.01 us  [on_device(): a3, b3 = (lax.ppermute(a3, 'dp', y), lax.ppermute(b3, 'dp', x))]
    reduce_scatter x1 -> x2, waiting for transfers between devices: 21.6 us -> 9.91 us  [scatter_tokens(): return lax.psum_scatter(back, 'mp', scatter_dimension=1, tiled=True)]
    ppermute x2, waiting for transfers between devices: 3.24 us -> 11.7 us  [on_device(): vector += lax.ppermute(vector, 'mp', flip_pairs(mp, bit))]
    ppermute x9, starting transfers between devices: 20.2 us -> 11.7 us  [shifted(): return lax.ppermute(array, 'mp', shift_pairs(mp, k)) if k else array]
  transfers between devices with their start and end apart: 49 -> 63, of which waited for: 25 -> 27; matrix products, arithmetic and copies ran while one was open for 6% -> 7% of each run, Pallas kernels for 19% -> 18%
where the time goes in v3:
time: 372 us; the launch traced here: 365 us
  waiting for transfers between devices  151 us (41%)
  Pallas kernels  108 us (29%)
  starting transfers between devices  51.5 us (14%)
  local copies, waits for them, and re-layouts  28.6 us (8%)
  between operations  15.2 us (4%)
  other arithmetic  11.1 us (3%)
    ppermute x3, waiting for transfers between devices, relay(): lax.ppermute(above[-1], 'mp', [(mp - 1 - i, mp - 1 - j) for i, j in pairs])  48.5 us
    pallas_call x1, Pallas kernels, feed_forward(): pl.pallas_call(kernel, in_specs=in_specs, out_specs=[ANY] * len(joint_col...  29.4 us
    ppermute x9, waiting for transfers between devices, shifted(): return lax.ppermute(array, 'mp', shift_pairs(mp, k)) if k else array  26.1 us
    pallas_call x2, Pallas kernels, attend(): pl.pallas_call(functools.partial(attend_kernel, b, slots, heads, size), i...  25.8 us
    pallas_call x1, Pallas kernels, attend_back(): pl.pallas_call(functools.partial(attend_back_kernel, micro, slots, heads,...  23.5 us
    pallas_call x2, Pallas kernels, weight_grad(): pl.pallas_call(kernel, in_specs=[SMEM] + [ANY] * 4 + given_specs, out_spe...  17.6 us
    ppermute x2, waiting for transfers between devices, on_device(): a1, b2 = (lax.ppermute(a1, 'dp', x), lax.ppermute(b2, 'dp', y))  15.5 us
    unnamed x117, local copies, waits for them, and re-layouts  12.9 us
  transfers between devices with their start and end apart: 63, of which 27 were waited for; matrix products, arithmetic and copies ran while one was open for 7% of the time, Pallas kernels for 18%

profile of v3, /device:TPU:0, one launch (start us, length us, event | category | flops | bytes accessed | tf_op | source)
XLA Modules:
  0.0 365.4 jit_solution(1290595443838156014)
XLA Ops:
  7.3 2.1 slice_bitcast_fusion
  15.2 5.6 %collective-permute-start = (bf16[240,768]{1,0:T(8,128)(2,1)S(1)}, bf16[240,768]{1,0:T(8,128)(2,1)S(1)}, u32[]{:S(2)}, u32[]{:S(2)}) collective-permute-start(bf16[240,768]{1,0:T(8,128)(2,1)S(1)} %dynamic-slice_bitcast_fusion), channel_id=1, source_target_pairs={{0,1},{1,2},{2,3},{4,5},{5,6},{6,7},{8,9},{9,10},{10,11},{12,13},{... | collective-permute-start | bytes 1105928 | tf_op jit(solution)/shard_map/ppermute | solution.py:684
  20.8 16.1 %collective-permute-done.1 = bf16[240,768]{1,0:T(8,128)(2,1)S(1)} collective-permute-done((bf16[240,768]{1,0:T(8,128)(2,1)S(1)}, bf16[240,768]{1,0:T(8,128)(2,1)S(1)}, u32[]{:S(2)}, u32[]{:S(2)}) %collective-permute-start.1) | collective-permute-done | bytes 368672 | tf_op jit(solution)/shard_map/ppermute | solution.py:685
  38.9 21.7 %collective-permute-done.2 = bf16[240,768]{1,0:T(8,128)(2,1)S(1)} collective-permute-done((bf16[240,768]{1,0:T(8,128)(2,1)S(1)}, bf16[240,768]{1,0:T(8,128)(2,1)S(1)}, u32[]{:S(2)}, u32[]{:S(2)}) %collective-permute-start.2) | collective-permute-done | bytes 368672 | tf_op jit(solution)/shard_map/ppermute | solution.py:685
  62.7 10.7 %collective-permute-done.3 = bf16[240,768]{1,0:T(8,128)(2,1)S(1)} collective-permute-done((bf16[240,768]{1,0:T(8,128)(2,1)S(1)}, bf16[240,768]{1,0:T(8,128)(2,1)S(1)}, u32[]{:S(2)}, u32[]{:S(2)}) %collective-permute-start.3) | collective-permute-done | bytes 368672 | tf_op jit(solution)/shard_map/ppermute | solution.py:685
  80.5 12.8 %attend.2 = (bf16[2,2,3,512,512]{4,3,2,1,0:T(8,128)(2,1)}, bf16[2,3,512,512]{3,2,1,0:T(8,128)(2,1)}, bf16[2,512,576]{2,1,0:T(8,128)(2,1)}, bf16[2,512,192]{2,1,0:T(8,128)(2,1)}) custom-call(bf16[2,512,768]{2,1,0:T(8,128)(2,1)} %all-gather.3.cloned.1.call-done.tok.refs_0_, bf16[768,576]{1,0:T(8,128)(2,1)} %pad_maximum_fusion.3.w.refs_8_, ...), custom_call_target="tpu_custom_call" | custom-call | flops 2516582400 | bytes 9437184 | tf_op jit(solution)/shard_map/attend/pallas_call | solution.py:109
  97.3 2.1 collective-permute-done.21.refs_21_
  100.9 2.0 collective-permute-done.16.refs_14_
  102.8 12.7 %collective-permute-done.10 = bf16[2,128,192]{2,1,0:T(8,128)(2,1)S(1)} collective-permute-done((bf16[2,128,192]{2,1,0:T(8,128)(2,1)S(1)}, bf16[2,128,192]{2,1,0:T(8,128)(2,1)S(1)}, u32[]{:S(2)}, u32[]{:S(2)}) %collective-permute-start.10) | collective-permute-done | bytes 98336 | tf_op jit(solution)/shard_map/ppermute | solution.py:747
  115.6 12.9 %attend.3 = (bf16[2,2,3,512,512]{4,3,2,1,0:T(8,128)(2,1)}, bf16[2,3,512,512]{3,2,1,0:T(8,128)(2,1)}, bf16[2,512,576]{2,1,0:T(8,128)(2,1)}, bf16[2,512,192]{2,1,0:T(8,128)(2,1)}) custom-call(bf16[2,512,768]{2,1,0:T(8,128)(2,1)} %all-gather.5.cloned.1.call-done.tok.refs_1_, ...), custom_call_target="tpu_custom_call", output_to_operand_aliasing={{0}: (5, {})} | custom-call | flops 2516582400 | bytes 9437184 | tf_op jit(solution)/shard_map/attend/pallas_call | solution.py:109
  133.8 2.0 collective-permute-start.13
  141.8 3.6 collective-permute-done.14
  148.5 29.4 %feed_forward.1 = (bf16[512,768]{1,0:T(8,128)(2,1)}, bf16[512,3072]{1,0:T(8,128)(2,1)}, bf16[512,768]{1,0:T(8,128)(2,1)}, bf16[512,3072]{1,0:T(8,128)(2,1)}, bf1...) custom-call(s32[12]{0:T(128)} %pad_add_fusion.place, ...), custom_call_target="tpu_custom_call" | custom-call | flops 10871635968 | bytes 17301504 | tf_op jit(solution)/shard_map/feed_forward/pallas_call | solution.py:484
  177.9 9.2 %weight_grad.2 = (bf16[4,4,224,768]{3,2,1,0:T(8,128)(2,1)}, f32[768,768]{1,0:T(8,128)}) custom-call(s32[12]{0:T(128)} %pad_add_fusion.place, bf16[512,3072]{1,0:T(8,128)(2,1)} %get-tuple-element.118.act, bf16[512,768]{1,0:T(8,128)(2,1)} %get-tuple-element.119.branch, bf16[512,3072]{1,0:T(8,128)(2,1)} %get-tuple-element.120.inner, ...), custom_call_target="tpu_custom_call" | custom-call | flops 3019898880 | bytes 6144000 | tf_op jit(solution)/shard_map/weight_grad/pallas_call | solution.py:588
  188.1 3.6 collective-permute-start.27
  192.3 4.3 %collective-permute-done.26.refs_1_ = bf16[4,4,224,768]{3,2,1,0:T(8,128)(2,1)} collective-permute-done((bf16[4,4,224,768]{3,2,1,0:T(8,128)(2,1)}, bf16[4,4,224,768]{3,2,1,0:T(8,128)(2,1)}, u32[]{:S(2)}, u32[]{:S(2)}) %collective-permute-start.26) | collective-permute-done | bytes 5505056 | tf_op jit(solution)/shard_map/ppermute | solution.py:872
  196.6 8.4 %weight_grad.3 = (bf16[4,112,768]{2,1,0:T(8,128)(2,1)}, bf16[4,112,768]{2,1,0:T(8,128)(2,1)}, bf16[4,112,768]{2,1,0:T(8,128)(2,1)}, bf16[4,112,768]{2,1,0:T(8,12...) custom-call(s32[12]{0:T(128)} %pad_add_fusion.place, ...), custom_call_target="tpu_custom_call" | custom-call | flops 3019898880 | bytes 6144000 | tf_op jit(solution)/shard_map/weight_grad/pallas_call | solution.py:588
  208.6 6.4 %collective-permute-done.28 = bf16[512,192]{1,0:T(8,128)(2,1)S(1)} collective-permute-done((bf16[512,192]{1,0:T(8,128)(2,1)S(1)}, bf16[512,192]{1,0:T(8,128)(2,1)S(1)}, u32[]{:S(2)}, u32[]{:S(2)}) %collective-permute-start.28) | collective-permute-done | bytes 196640 | tf_op jit(solution)/shard_map/ppermute | solution.py:747
  217.3 23.5 %attend_back.1 = (f32[2,2,3,512,512]{4,3,2,1,0:T(8,128)}, f32[768,576]{1,0:T(8,128)}, f32[8,576]{1,0:T(8,128)}, bf16[2,512,768]{2,1,0:T(8,128)(2,1)}, bf16[2,512,768]{2,1,0:T(8,128)(2,1)}) custom-call(s32[4]{0:T(128)} %pad_add_fusion.1.place, bf16[2,512,768]{2,1,0:T(8,128)(2,1)} %all-gather.3.cloned.1.call-done.tok.refs_0_, ...), custom_call_target="tpu_custom_call" | custom-call | flops 10066329600 | bytes 25165824 | tf_op jit(solution)/shard_map/attend_back/pallas_call | solution.py:235
  242.6 3.0 hop_sum.1
  247.8 15.3 %collective-permute-done.34.a1 = bf16[4,112,768]{2,1,0:T(8,128)(2,1)S(1)} collective-permute-done((bf16[4,112,768]{2,1,0:T(8,128)(2,1)}, bf16[4,112,768]{2,1,0:T(8,128)(2,1)S(1)}, u32[]{:S(2)}, u32[]{:S(2)}) %collective-permute-start.34) | collective-permute-done | bytes 688160 | tf_op jit(solution)/shard_map/ppermute | solution.py:883
  264.7 3.8 %plane_sum.1 = bf16[4,224,768]{2,1,0:T(8,128)(2,1)} custom-call(s32[4]{0:T(128)} %fusion.19.here, bf16[4,112,768]{2,1,0:T(8,128)(2,1)} %get-tuple-element.132.a0, bf16[4,112,768]{2,1,0:T(8,128)(2,1)} %copy-done.12, bf16[4,112,768]{2,1,0:T(8,128)(2,1)} %copy-done.10, bf16[4,112,768]{2,1,0:T(8,128)(2,1)} %get-tuple-element.133.b0, ...), custom_call_target="tpu_custom_call" | custom-call | tf_op jit(solution)/shard_map/plane_sum/pallas_call | solution.py:628
  268.5 9.9 %reduce-scatter.4.cloned.1.call-done = bf16[2,128,768]{2,1,0:T(8,128)(2,1)} async-done(((bf16[2,512,768]{2,1,0:T(8,128)(2,1)}), bf16[2,128,768]{2,1,0:T(8,128)(2,1)}) %reduce-scatter.4.cloned.1.call-update) | async-done | bytes 393232 | tf_op jit(solution)/shard_map/reduce_scatter | solution.py:864
  282.7 2.7 collective-permute-done.43
  290.0 10.7 %collective-permute-done.44 = f32[200,576]{1,0:T(8,128)S(1)} collective-permute-done((f32[200,576]{1,0:T(8,128)S(1)}, f32[200,576]{1,0:T(8,128)S(1)}, u32[]{:S(2)}, u32[]{:S(2)}) %collective-permute-start.44) | collective-permute-done | bytes 460832 | tf_op jit(solution)/shard_map/ppermute | solution.py:894
  304.1 10.6 %collective-permute-done.45 = f32[200,576]{1,0:T(8,128)S(1)} collective-permute-done((f32[200,576]{1,0:T(8,128)S(1)}, f32[200,576]{1,0:T(8,128)S(1)}, u32[]{:S(2)}, u32[]{:S(2)}) %collective-permute-start.45) | collective-permute-done | bytes 460832 | tf_op jit(solution)/shard_map/ppermute | solution.py:897
  324.7 3.2 collective-permute-done.49
  329.2 8.6 %collective-permute-done.50 = f32[24,576]{1,0:T(8,128)S(1)} collective-permute-done((f32[24,576]{1,0:T(8,128)S(1)}, f32[24,576]{1,0:T(8,128)S(1)}, u32[]{:S(2)}, u32[]{:S(2)}) %collective-permute-start.50) | collective-permute-done | bytes 55328 | tf_op jit(solution)/shard_map/ppermute | solution.py:909
  340.8 2.2 copy.54
  342.9 2.2 copy.55
  349.6 5.2 %gather_grads.1 = (f32[768,768]{1,0:T(8,128)}, f32[8,96,768]{2,1,0:T(8,128)}, f32[12,16,768]{2,1,0:T(8,128)}) custom-call(s32[12]{0:T(128)} %pad_add_fusion.place, bf16[112,768]{1,0:T(8,128)(2,1)} %copy-done.9, bf16[112,768]{1,0:T(8,128)(2,1)} %collective-permute-done.36.refs_1_, bf16[112,768]{1,0:T(8,128)(2,1)} %copy-done.21, ...), custom_call_target="tpu_custom_call" | custom-call | tf_op jit(solution)/shard_map/gather_grads/pallas_call | solution.py:666
  356.1 2.3 convert_add_fusion
  (308 shorter events, 81.4 us)
Async XLA Ops:
  7.2 73.3 %all-gather.3.cloned.1.call-start = ((), (), s32[]{:S(2)}) async-start(), calls=%async_computation.3 | async-start | bytes 1966080 | tf_op jit(solution)/shard_map/all_gather | solution.py:793
  9.4 106.1 %all-gather.5.cloned.1.call-start = ((), (), s32[]{:S(2)}) async-start(), calls=%async_computation.4 | async-start | bytes 1966080 | tf_op jit(solution)/shard_map/all_gather | solution.py:793
  13.9 23.0 %collective-permute-start.1 = (bf16[240,768]{1,0:T(8,128)(2,1)S(1)}, bf16[240,768]{1,0:T(8,128)(2,1)S(1)}, u32[]{:S(2)}, u32[]{:S(2)}) collective-permute-start(bf16[240,768]{1,0:T(8,128)(2,1)S(1)} %dynamic-slice_bitcast_fusion), channel_id=1, source_target_pairs={{3,2},{2,1},{1,0},{7,6},{6,5},{5,4},{11,10},{10,9},{9,8},{15,14},{... | collective-permute-start | bytes 1105928 | tf_op jit(solution)/shard_map/ppermute | solution.py:685
  15.2 23.0 %collective-permute-start = (bf16[240,768]{1,0:T(8,128)(2,1)S(1)}, bf16[240,768]{1,0:T(8,128)(2,1)S(1)}, u32[]{:S(2)}, u32[]{:S(2)}) collective-permute-start(bf16[240,768]{1,0:T(8,128)(2,1)S(1)} %dynamic-slice_bitcast_fusion), channel_id=1, source_target_pairs={{0,1},{1,2},{2,3},{4,5},{5,6},{6,7},{8,9},{9,10},{10,11},{12,13},{... | collective-permute-start | bytes 1105928 | tf_op jit(solution)/shard_map/ppermute | solution.py:684
  36.9 23.7 %collective-permute-start.2 = (bf16[240,768]{1,0:T(8,128)(2,1)S(1)}, bf16[240,768]{1,0:T(8,128)(2,1)S(1)}, u32[]{:S(2)}, u32[]{:S(2)}) collective-permute-start(bf16[240,768]{1,0:T(8,128)(2,1)S(1)} %collective-permute-done.1), channel_id=1, source_target_pairs={{2,1},{1,0},{6,5},{5,4},{10,9},{9,8},{14,13},{13,12},{18,17},{17,1... | collective-permute-start | bytes 1105928 | tf_op jit(solution)/shard_map/ppermute | solution.py:685
  38.2 22.4 %collective-permute-start.4 = (bf16[240,768]{1,0:T(8,128)(2,1)S(1)}, bf16[240,768]{1,0:T(8,128)(2,1)S(1)}, u32[]{:S(2)}, u32[]{:S(2)}) collective-permute-start(bf16[240,768]{1,0:T(8,128)(2,1)S(1)} %collective-permute-done), channel_id=1, source_target_pairs={{1,2},{2,3},{5,6},{6,7},{9,10},{10,11},{13,14},{14,15},{17,18},{18... | collective-permute-start | bytes 1105928 | tf_op jit(solution)/shard_map/ppermute | solution.py:684
  60.6 217.8 %reduce-scatter.4.cloned.1.call-start = ((), (), s32[]{:S(2)}) async-start(), calls=%async_computation.5 | async-start | bytes 1966080 | tf_op jit(solution)/shard_map/reduce_scatter | solution.py:864
  73.8 20.3 %collective-permute-start.6 = (bf16[3,128,768]{2,1,0:T(8,128)(2,1)S(1)}, bf16[3,128,768]{2,1,0:T(8,128)(2,1)S(1)}, u32[]{:S(2)}, u32[]{:S(2)}) collective-permute-start(bf16[3,128,768]{2,1,0:T(8,128)(2,1)S(1)} %slice.131.refs_12_), channel_id=1, source_target_pairs={{0,8},{4,12},{8,0},{12,4},{16,24},{20,28},{24,16},{28,20},{1,9},{5... | collective-permute-start | bytes 1769480 | tf_op jit(solution)/shard_map/ppermute | solution.py:639
  75.3 18.1 %collective-permute-start.7 = (bf16[3,112,768]{2,1,0:T(8,128)(2,1)S(1)}, bf16[3,112,768]{2,1,0:T(8,128)(2,1)}, u32[]{:S(2)}, u32[]{:S(2)}) collective-permute-start(bf16[3,112,768]{2,1,0:T(8,128)(2,1)S(1)} %pad_maximum_fusion.4.refs_20_), channel_id=1, source_target_pairs={{0,16},{4,20},{8,24},{12,28},{16,0},{20,4},{24,8},{28,12},{1,17},{... | collective-permute-start | bytes 1548296 | tf_op jit(solution)/shard_map/ppermute | solution.py:639
  76.9 22.5 %collective-permute-start.21 = (bf16[3,112,768]{2,1,0:T(8,128)(2,1)S(1)}, bf16[3,112,768]{2,1,0:T(8,128)(2,1)}, u32[]{:S(2)}, u32[]{:S(2)}) collective-permute-start(bf16[3,112,768]{2,1,0:T(8,128)(2,1)S(1)} %pad_maximum_fusion.4.refs_20_), channel_id=1, source_target_pairs={{0,8},{4,12},{8,0},{12,4},{16,24},{20,28},{24,16},{28,20},{1,9},{5... | collective-permute-start | bytes 1548296 | tf_op jit(solution)/shard_map/ppermute | solution.py:640
  77.5 25.4 %collective-permute-start.16 = (bf16[3,128,768]{2,1,0:T(8,128)(2,1)S(1)}, bf16[3,128,768]{2,1,0:T(8,128)(2,1)}, u32[]{:S(2)}, u32[]{:S(2)}) collective-permute-start(bf16[3,128,768]{2,1,0:T(8,128)(2,1)S(1)} %slice.131.refs_12_), channel_id=1, source_target_pairs={{0,16},{4,20},{8,24},{12,28},{16,0},{20,4},{24,8},{28,12},{1,17},{... | collective-permute-start | bytes 1769480 | tf_op jit(solution)/shard_map/ppermute | solution.py:640
  79.2 20.2 %collective-permute-start.22 = (bf16[3,112,768]{2,1,0:T(8,128)(2,1)S(1)}, bf16[3,112,768]{2,1,0:T(8,128)(2,1)}, u32[]{:S(2)}, u32[]{:S(2)}) collective-permute-start(bf16[3,112,768]{2,1,0:T(8,128)(2,1)S(1)} %pad_maximum_fusion.4.refs_20_), channel_id=1, source_target_pairs={{0,4},{4,0},{8,12},{12,8},{16,20},{20,16},{24,28},{28,24},{1,5},{5... | collective-permute-start | bytes 1548296 | tf_op jit(solution)/shard_map/ppermute | solution.py:840
  93.4 46.1 %collective-permute-start.17 = (bf16[3,128,768]{2,1,0:T(8,128)(2,1)S(1)}, bf16[3,128,768]{2,1,0:T(8,128)(2,1)S(1)}, u32[]{:S(2)}, u32[]{:S(2)}) collective-permute-start(bf16[3,128,768]{2,1,0:T(8,128)(2,1)S(1)} %slice.131.refs_12_), channel_id=1, source_target_pairs={{0,4},{4,0},{8,12},{12,8},{16,20},{20,16},{24,28},{28,24},{1,5},{5... | collective-permute-start | bytes 1769480 | tf_op jit(solution)/shard_map/ppermute | solution.py:840
  94.0 43.7 %collective-permute-start.8 = (bf16[3,128,768]{2,1,0:T(8,128)(2,1)S(1)}, bf16[3,128,768]{2,1,0:T(8,128)(2,1)}, u32[]{:S(2)}, u32[]{:S(2)}) collective-permute-start(bf16[3,128,768]{2,1,0:T(8,128)(2,1)S(1)} %collective-permute-done.6.refs_13_), channel_id=1, source_target_pairs={{0,16},{4,20},{8,24},{12,28},{16,0},{20,4},{24,8},{28,12},{1,17},{... | collective-permute-start | bytes 1769480 | tf_op jit(solution)/shard_map/ppermute | solution.py:642
  99.4 16.1 %collective-permute-start.10 = (bf16[2,128,192]{2,1,0:T(8,128)(2,1)S(1)}, bf16[2,128,192]{2,1,0:T(8,128)(2,1)S(1)}, u32[]{:S(2)}, u32[]{:S(2)}) collective-permute-start(bf16[2,128,192]{2,1,0:T(8,128)(2,1)S(1)} %get-tuple-element.222), channel_id=1, source_target_pairs={{0,1},{1,2},{2,3},{3,0},{4,5},{5,6},{6,7},{7,4},{8,9},{9,10},{10,1... | collective-permute-start | bytes 294920 | tf_op jit(solution)/shard_map/ppermute | solution.py:747
  99.4 36.4 %collective-permute-start.9 = (bf16[3,112,768]{2,1,0:T(8,128)(2,1)}, bf16[3,112,768]{2,1,0:T(8,128)(2,1)S(1)}, u32[]{:S(2)}, u32[]{:S(2)}) collective-permute-start(bf16[3,112,768]{2,1,0:T(8,128)(2,1)} %collective-permute-done.7.refs_22_), channel_id=1, source_target_pairs={{0,8},{4,12},{8,0},{12,4},{16,24},{20,28},{24,16},{28,20},{1,9},{5... | collective-permute-start | bytes 1548296 | tf_op jit(solution)/shard_map/ppermute | solution.py:642
  102.8 36.7 %collective-permute-start.23 = (bf16[3,112,768]{2,1,0:T(8,128)(2,1)}, bf16[3,112,768]{2,1,0:T(8,128)(2,1)}, u32[]{:S(2)}, u32[]{:S(2)}) collective-permute-start(bf16[3,112,768]{2,1,0:T(8,128)(2,1)} %collective-permute-done.21.refs_21_), channel_id=1, source_target_pairs={{0,4},{4,0},{8,12},{12,8},{16,20},{20,16},{24,28},{28,24},{1,5},{5... | collective-permute-start | bytes 1548296 | tf_op jit(solution)/shard_map/ppermute | solution.py:840
  188.1 19.0 %collective-permute-start.27 = (bf16[512,192]{1,0:T(8,128)(2,1)S(1)}, bf16[512,192]{1,0:T(8,128)(2,1)S(1)}, u32[]{:S(2)}, u32[]{:S(2)}) collective-permute-start(bf16[512,192]{1,0:T(8,128)(2,1)S(1)} %copy-done.44), channel_id=1, source_target_pairs={{0,3},{1,0},{2,1},{3,2},{4,7},{5,4},{6,5},{7,6},{8,11},{9,8},{10,9... | collective-permute-start | bytes 589832 | tf_op jit(solution)/shard_map/ppermute | solution.py:747
  191.6 23.4 %collective-permute-start.28 = (bf16[512,192]{1,0:T(8,128)(2,1)S(1)}, bf16[512,192]{1,0:T(8,128)(2,1)S(1)}, u32[]{:S(2)}, u32[]{:S(2)}) collective-permute-start(bf16[512,192]{1,0:T(8,128)(2,1)S(1)} %copy-done.43), channel_id=1, source_target_pairs={{0,2},{1,3},{2,0},{3,1},{4,6},{5,7},{6,4},{7,5},{8,10},{9,11},{10,... | collective-permute-start | bytes 589832 | tf_op jit(solution)/shard_map/ppermute | solution.py:747
  191.6 24.9 %collective-permute-start.29 = (bf16[512,192]{1,0:T(8,128)(2,1)S(1)}, bf16[512,192]{1,0:T(8,128)(2,1)S(1)}, u32[]{:S(2)}, u32[]{:S(2)}) collective-permute-start(bf16[512,192]{1,0:T(8,128)(2,1)S(1)} %copy-done.42), channel_id=1, source_target_pairs={{0,1},{1,2},{2,3},{3,0},{4,5},{5,6},{6,7},{7,4},{8,9},{9,10},{10,1... | collective-permute-start | bytes 589832 | tf_op jit(solution)/shard_map/ppermute | solution.py:747
  205.0 35.8 %collective-permute-start.30 = (bf16[4,112,768]{2,1,0:T(8,128)(2,1)}, bf16[4,112,768]{2,1,0:T(8,128)(2,1)S(1)}, u32[]{:S(2)}, u32[]{:S(2)}) collective-permute-start(bf16[4,112,768]{2,1,0:T(8,128)(2,1)} %get-tuple-element.128), channel_id=1, source_target_pairs={{0,16},{4,20},{8,24},{12,28},{16,0},{20,4},{24,8},{28,12},{1,17},{... | collective-permute-start | bytes 2064392 | tf_op jit(solution)/shard_map/ppermute | solution.py:879
  205.6 35.3 %collective-permute-start.31 = (bf16[4,112,768]{2,1,0:T(8,128)(2,1)}, bf16[4,112,768]{2,1,0:T(8,128)(2,1)S(1)}, u32[]{:S(2)}, u32[]{:S(2)}) collective-permute-start(bf16[4,112,768]{2,1,0:T(8,128)(2,1)} %get-tuple-element.131), channel_id=1, source_target_pairs={{0,8},{4,12},{8,0},{12,4},{16,24},{20,28},{24,16},{28,20},{1,9},{5... | collective-permute-start | bytes 2064392 | tf_op jit(solution)/shard_map/ppermute | solution.py:879
  207.0 33.8 %collective-permute-start.32 = (bf16[4,112,768]{2,1,0:T(8,128)(2,1)}, bf16[4,112,768]{2,1,0:T(8,128)(2,1)S(1)}, u32[]{:S(2)}, u32[]{:S(2)}) collective-permute-start(bf16[4,112,768]{2,1,0:T(8,128)(2,1)} %get-tuple-element.126), channel_id=1, source_target_pairs={{0,16},{4,20},{8,24},{12,28},{16,0},{20,4},{24,8},{28,12},{1,17},{... | collective-permute-start | bytes 2064392 | tf_op jit(solution)/shard_map/ppermute | solution.py:878
  215.1 25.8 %collective-permute-start.33 = (bf16[4,112,768]{2,1,0:T(8,128)(2,1)}, bf16[4,112,768]{2,1,0:T(8,128)(2,1)S(1)}, u32[]{:S(2)}, u32[]{:S(2)}) collective-permute-start(bf16[4,112,768]{2,1,0:T(8,128)(2,1)} %get-tuple-element.127), channel_id=1, source_target_pairs={{0,8},{4,12},{8,0},{12,4},{16,24},{20,28},{24,16},{28,20},{1,9},{5... | collective-permute-start | bytes 2064392 | tf_op jit(solution)/shard_map/ppermute | solution.py:878
  245.6 70.5 %reduce-scatter.8.cloned.1.call-start = ((), (), s32[]{:S(2)}) async-start(), calls=%async_computation.7 | async-start | bytes 1720320 | tf_op jit(solution)/shard_map/reduce_scatter | solution.py:887
  246.0 17.1 %collective-permute-start.34 = (bf16[4,112,768]{2,1,0:T(8,128)(2,1)}, bf16[4,112,768]{2,1,0:T(8,128)(2,1)S(1)}, u32[]{:S(2)}, u32[]{:S(2)}) collective-permute-start(bf16[4,112,768]{2,1,0:T(8,128)(2,1)} %get-tuple-element.141), channel_id=1, source_target_pairs={{0,8},{4,12},{8,0},{12,4},{16,24},{20,28},{24,16},{28,20},{1,9},{5... | collective-permute-start | bytes 2064392 | tf_op jit(solution)/shard_map/ppermute | solution.py:883
  246.5 16.7 %collective-permute-start.35 = (bf16[4,112,768]{2,1,0:T(8,128)(2,1)}, bf16[4,112,768]{2,1,0:T(8,128)(2,1)S(1)}, u32[]{:S(2)}, u32[]{:S(2)}) collective-permute-start(bf16[4,112,768]{2,1,0:T(8,128)(2,1)} %get-tuple-element.145), channel_id=1, source_target_pairs={{0,16},{4,20},{8,24},{12,28},{16,0},{20,4},{24,8},{28,12},{1,17},{... | collective-permute-start | bytes 2064392 | tf_op jit(solution)/shard_map/ppermute | solution.py:883
  278.5 76.3 %reduce-scatter.6.cloned.1.call-start = ((), (), s32[]{:S(2)}) async-start(), calls=%async_computation.6 | async-start | bytes 1966080 | tf_op jit(solution)/shard_map/reduce_scatter | solution.py:864
  321.0 17.2 %collective-permute-start.37 = (bf16[112,768]{1,0:T(8,128)(2,1)S(1)}, bf16[112,768]{1,0:T(8,128)(2,1)S(1)}, u32[]{:S(2)}, u32[]{:S(2)}) collective-permute-start(bf16[112,768]{1,0:T(8,128)(2,1)S(1)} %get-tuple-element.225.refs_0_), channel_id=1, source_target_pairs={{0,16},{4,20},{8,24},{12,28},{16,0},{20,4},{24,8},{28,12},{1,17},{... | collective-permute-start | bytes 516104 | tf_op jit(solution)/shard_map/ppermute | solution.py:640
  321.6 16.3 %collective-permute-start.52 = (bf16[112,768]{1,0:T(8,128)(2,1)S(1)}, bf16[112,768]{1,0:T(8,128)(2,1)}, u32[]{:S(2)}, u32[]{:S(2)}) collective-permute-start(bf16[112,768]{1,0:T(8,128)(2,1)S(1)} %get-tuple-element.224.refs_8_), channel_id=1, source_target_pairs={{0,16},{4,20},{8,24},{12,28},{16,0},{20,4},{24,8},{28,12},{1,17},{... | collective-permute-start | bytes 516104 | tf_op jit(solution)/shard_map/ppermute | solution.py:639
  324.1 15.1 %collective-permute-start.38 = (bf16[112,768]{1,0:T(8,128)(2,1)}, bf16[112,768]{1,0:T(8,128)(2,1)}, u32[]{:S(2)}, u32[]{:S(2)}) collective-permute-start(bf16[112,768]{1,0:T(8,128)(2,1)} %collective-permute-done.36.refs_1_), channel_id=1, source_target_pairs={{0,16},{4,20},{8,24},{12,28},{16,0},{20,4},{24,8},{28,12},{1,17},{... | collective-permute-start | bytes 516104 | tf_op jit(solution)/shard_map/ppermute | solution.py:642
  328.0 18.2 %collective-permute-start.51 = (bf16[112,768]{1,0:T(8,128)(2,1)S(1)}, bf16[112,768]{1,0:T(8,128)(2,1)}, u32[]{:S(2)}, u32[]{:S(2)}) collective-permute-start(bf16[112,768]{1,0:T(8,128)(2,1)S(1)} %get-tuple-element.224.refs_8_), channel_id=1, source_target_pairs={{0,8},{4,12},{8,0},{12,4},{16,24},{20,28},{24,16},{28,20},{1,9},{5... | collective-permute-start | bytes 516104 | tf_op jit(solution)/shard_map/ppermute | solution.py:640
  (86 other events, 787.0 us)
Sparse Core Ops, SparseCore 0:
  10.2 50.6 all-gather.2
  63.0 38.1 all-gather.4
  245.8 32.6 reduce-scatter.3
  280.6 31.1 reduce-scatter.7
  314.1 36.7 reduce-scatter.5

commit v4 on v3

--- a/solution.py
+++ b/solution.py
@@ -291,7 +291,10 @@
 def feed_forward_kernel(micro, n_ctx, intake, place, refs_in, refs_out, scratch):
     ctx, (tok, cot, vectors, *weights) = refs_in[: micro * n_ctx], refs_in[micro * n_ctx :]
     b_out, g1, s1, b_down, g2, s2 = [vectors[i : i + 1, :] for i in range(6)]
-    joint, (smalls, unit_sums), d_ctx = refs_out[:8], refs_out[8:10], refs_out[10:]
+    joint, (smalls, unit_sums) = refs_out[:8], refs_out[8:10]
+    d_ctx, other = refs_out[10 : 10 + n_ctx], refs_out[10 + n_ctx :] or None
+    if other:
+        scratch, other_scratch = scratch[:-2], scratch[-2:]
     slope, total, *held = scratch
     weights_v, held = held[: -14], held[-14:]
     w_out, b_in = weights_v[-2:]
@@ -379,6 +382,23 @@
     smalls[1:2, :] = column_sum(d_hidden * n1)
     smalls[2:3, :] = column_sum(d_hidden)
     smalls[6:8, :] = jnp.zeros((2, width), F32)
+    if other is not None:
+        grads, d_out = other
+        other_v, other_sem = other_scratch
+        n, mp, size, _ = other_v.shape
+        piece = (size - 32) // 2
+        span = mp * piece
+        d_out[...] = mm(all_v[...], att_v[...], 0, 0)
+        for o in reversed(range(n)):
+            at = slice((n + o) * span, (n + o + 1) * span)
+            fill_block(
+                other_v, o, mm(inner_v[:, at], low_v[...], 0, 0),
+                mm(act_v[:, at], branch_v[...], 0, 0), d_out, piece, place[n + o],
+                2 * n + place[n + o], lambda k: place[2 * n + k],
+            )
+            start(other_v.at[o], grads.at[o], other_sem.at[o])
+        for o in range(n):
+            pltpu.make_async_copy(other_v.at[o], grads.at[o], other_sem.at[o]).wait()
     for k in range(n_ctx):
         pltpu.make_async_copy(d_ctx_v.at[k], d_ctx[k], io_sem.at[2, k]).wait()
     for i in range(8):
@@ -462,7 +482,7 @@
     return wait_first, lambda j: None, units
 
 
-def feed_forward(ctx, tokens, cot, vectors, place, weights, intake, block):
+def feed_forward(ctx, tokens, cot, vectors, place, weights, intake, block, grads):
     rows, width = tokens.shape
     micro, n_ctx = len(ctx), len(ctx[0])
     head_width = ctx[0][0].shape[1]
@@ -472,7 +492,8 @@
     joint_cols = [(width, BF16), (units, BF16), (width, BF16), (units, BF16), (width, BF16),
                   (width, BF16), (n_ctx * head_width, BF16), (width, F32)]
     n_args = len(args)
-    n_out = len(joint_cols) + 2 + n_ctx
+    n_out = len(joint_cols) + 2 + n_ctx + 2 * len(grads)
+    context = n_ctx * head_width
 
     def kernel(place, *refs):
         feed_forward_kernel(
@@ -484,17 +505,19 @@
     outs = pl.pallas_call(
         kernel,
         in_specs=in_specs,
-        out_specs=[ANY] * len(joint_cols) + [VMEM] * 2 + [ANY] * n_ctx,
+        out_specs=[ANY] * len(joint_cols) + [VMEM] * 2 + [ANY] * n_ctx + [ANY, VMEM] * len(grads),
         out_shape=[jax.ShapeDtypeStruct((rows, c), t) for c, t in joint_cols]
         + [jax.ShapeDtypeStruct((8, width), F32), jax.ShapeDtypeStruct((8, units), F32)]
-        + [jax.ShapeDtypeStruct((rows, head_width), BF16)] * n_ctx,
+        + [jax.ShapeDtypeStruct((rows, head_width), BF16)] * n_ctx
+        + [jax.ShapeDtypeStruct(s, t) for g in grads for s, t in ((g, BF16), ((context, width), F32))],
         scratch_shapes=[
             pltpu.VMEM((rows, units), BF16), pltpu.VMEM((rows, width), F32),
             *[pltpu.VMEM(s, BF16) for s in held_shapes], pltpu.VMEM((1, units), F32),
             heads_block, pltpu.VMEM((rows, width), BF16), pltpu.VMEM((rows, width), BF16),
             heads_block, *[pltpu.VMEM((rows, c), t) for c, t in joint_cols],
             pltpu.SemaphoreType.DMA((9, 8)), pltpu.SemaphoreType.DMA((3 + micro, 8)),
-        ],
+        ]
+        + [s for g in grads for s in (pltpu.VMEM(g, BF16), pltpu.SemaphoreType.DMA((g[0],)))],
         compiler_params=pltpu.CompilerParams(vmem_limit_bytes=VMEM_LIMIT),
         cost_estimate=cost(
             2 * rows * width * (4 * units + 2 * width), 4 * units * width + 20 * rows * width,
@@ -503,98 +526,76 @@
         name="feed_forward",
     )(*args)
     n = len(joint_cols)
-    return outs[:n], outs[n], outs[n + 1], outs[n + 2 :]
-
-
-def weight_grad(half, mp, piece, place, act, branch, inner, low, ctx, att, d_out, got):
+    return outs[:n], outs[n], outs[n + 1], outs[n + 2 : n + 2 + n_ctx], outs[n + 2 + n_ctx :]
+
+
+def fill_block(out, o, d_in, d_down, d_out, piece, first, spare, place_of, got=None):
+    mp = out.shape[1]
+    head_width = d_out.shape[0] // mp
+    for k in range(mp):
+        parts = [d_in[k * piece : (k + 1) * piece], d_down[k * piece : (k + 1) * piece]]
+        for p in (first, jnp.minimum(spare, head_width // 16 - 1)):
+            at = pl.ds(pl.multiple_of(place_of(k) * head_width + p * 16, 16), 16)
+            parts.append(d_out[at, :])
+        row = 0
+        for part in parts:
+            at = slice(row, row + part.shape[0])
+            if got is not None:
+                part = part.astype(BF16).astype(F32) + got[o, k, at].astype(F32)
+            out[o, k, at] = part.astype(BF16)
+            row += part.shape[0]
+
+
+def weight_grad(mp, piece, place, act, branch, inner, low, d_out, got):
     rows, width = branch.shape
     span = mp * piece
     n = act.shape[1] // span // 2
-    head_width = ctx.shape[1] // mp
     size = 2 * piece + 32
     cut = size // 2
     order = tuple(reversed(range(n)))
 
-    def kernel(place, act, branch, inner, low, *refs):
-        given, outs = refs[:2], refs[2:-7]
-        act_v, inner_v, branch_v, low_v, got_v, out_v, sem = refs[-7:]
+    def kernel(place, act, branch, inner, low, d_out, got, *refs):
+        outs, (act_v, inner_v, branch_v, low_v, got_v, out_v, sem) = refs[:-7], refs[-7:]
         moving = [start(low, low_v, sem.at[0, 0]), start(branch, branch_v, sem.at[0, 1])]
         loads, stores = {}, []
         for o in order:
-            at = pl.ds((half * n + o) * span, span)
+            at = pl.ds(o * span, span)
             loads[o] = [
                 start(inner.at[:, at], inner_v.at[o], sem.at[1, o]),
                 start(act.at[:, at], act_v.at[o], sem.at[2, o]),
+                start(got.at[o], got_v.at[o], sem.at[3, o]),
             ]
-            if not half:
-                loads[o].append(start(given[1].at[o], got_v.at[o], sem.at[3, o]))
-        if half:
-            d_out = outs[1]
-            d_out[...] = mm(given[0][...], given[1][...], 0, 0)
-        else:
-            d_out = given[0]
         for copy in moving:
             copy.wait()
-        for o in order:
+        for i, o in enumerate(order):
             for copy in loads[o]:
                 copy.wait()
-            d_in = mm(inner_v[o], low_v[...], 0, 0)
-            d_down = mm(act_v[o], branch_v[...], 0, 0)
-            first = place[half * n + o]
-            second = jnp.minimum(2 * n + first, head_width // 16 - 1)
-            for k in range(mp):
-                parts = [d_in[k * piece : (k + 1) * piece], d_down[k * piece : (k + 1) * piece]]
-                for p in (first, second):
-                    at = place[2 * n + k] * head_width + p * 16
-                    at = pl.ds(pl.multiple_of(at, 16), 16)
-                    parts.append(d_out[at, :])
-                row = 0
-                for part in parts:
-                    at = slice(row, row + part.shape[0])
-                    if not half:
-                        part = part.astype(BF16).astype(F32) + got_v[o, k, at].astype(F32)
-                    out_v[o, k, at] = part.astype(BF16)
-                    row += part.shape[0]
-            if half:
-                stores.append(start(out_v.at[o], outs[0].at[o], sem.at[4, o]))
-            else:
-                i = 2 * order.index(o)
-                stores += [
-                    start(out_v.at[o, :, pl.ds(0, cut)], outs[i], sem.at[4, o]),
-                    start(out_v.at[o, :, pl.ds(cut, size - cut)], outs[i + 1], sem.at[5, o]),
-                ]
+            fill_block(
+                out_v, o, mm(inner_v[o], low_v[...], 0, 0), mm(act_v[o], branch_v[...], 0, 0),
+                d_out, piece, place[o], 2 * n + place[o], lambda k: place[2 * n + k], got_v,
+            )
+            stores += [
+                start(out_v.at[o, :, pl.ds(0, cut)], outs[2 * i], sem.at[4, o]),
+                start(out_v.at[o, :, pl.ds(cut, size - cut)], outs[2 * i + 1], sem.at[5, o]),
+            ]
         for copy in stores:
             copy.wait()
 
-    last = (ctx.shape[1], width)
-    args = [place, act, branch, inner, low]
-    if half:
-        args += [ctx, att]
-        given_specs = [VMEM, VMEM]
-        out_specs = [ANY, VMEM]
-        out_shape = [
-            jax.ShapeDtypeStruct((n, mp, size, width), BF16), jax.ShapeDtypeStruct(last, F32)
-        ]
-    else:
-        args += [d_out, got]
-        given_specs = [VMEM, ANY]
-        out_specs = [ANY] * (2 * n)
-        out_shape = [
-            jax.ShapeDtypeStruct((mp, r, width), BF16) for _ in range(n) for r in (cut, size - cut)
-        ]
     wide = pltpu.VMEM((n, rows, span), BF16)
     flat = pltpu.VMEM((rows, width), BF16)
     whole = pltpu.VMEM((n, mp, size, width), BF16)
     return pl.pallas_call(
         kernel,
-        in_specs=[SMEM] + [ANY] * 4 + given_specs,
-        out_specs=out_specs,
-        out_shape=out_shape,
+        in_specs=[SMEM] + [ANY] * 4 + [VMEM, ANY],
+        out_specs=[ANY] * (2 * n),
+        out_shape=[
+            jax.ShapeDtypeStruct((mp, r, width), BF16) for _ in range(n) for r in (cut, size - cut)
+        ],
         scratch_shapes=[wide, wide, flat, flat, whole, whole, pltpu.SemaphoreType.DMA((6, n))],
         compiler_params=pltpu.CompilerParams(vmem_limit_bytes=VMEM_LIMIT),
         cost_estimate=cost(2 * rows * width * 5 * width, n * mp * width * 500),
         name="weight_grad",
-    )(*args)
+    )(place, act, branch, inner, low, d_out, got)
 
 
 def joined(body, shapes, *args, name):
@@ -839,8 +840,9 @@
             for group in (firsts, seconds):
                 weights += group + [lax.ppermute(a, "dp", swap) for a in group]
     blocks = lax.optimization_barrier(blocks)
-    joint, small, unit_sums, d_ctx = feed_forward(
-        blocks, own_tokens, own_cot, vectors, ff_place, weights, intake, block
+    grads = [(chips, mp, 2 * piece + 32, width)] if packed else []
+    joint, small, unit_sums, d_ctx, other_grads = feed_forward(
+        blocks, own_tokens, own_cot, vectors, ff_place, weights, intake, block, grads
     )
     d_blocks = to_heads(d_ctx)
     layer, act, branch, inner, low, att, ctx_all, residual = joint
@@ -867,20 +869,24 @@
         return tie(jnp.concatenate([acc, bias_acc, vector], 0), *after)
 
     if packed:
-        pairs = [act, branch, inner, low, ctx_all, att]
-        other, d_out = weight_grad(1, mp, piece, ff_place, *pairs, None, None)
+        other, d_out = other_grads
         got = lax.ppermute(other, "dp", swap)
-        sums = weight_grad(0, mp, piece, ff_place, *pairs, d_out, got)
+        sums = weight_grad(mp, piece, ff_place, act, branch, inner, low, d_out, got)
         prev_grad, acc, bias_acc, *backs = back_through(sums)
         cut = 2 * piece + 32 >> 1
         x, y = flip_pairs(dp, 2), flip_pairs(dp, 4)
         a3, b3, a2, b2, a1, b1, a0, b0 = sums
         a3, b3 = lax.ppermute(a3, "dp", y), lax.ppermute(b3, "dp", x)
         a2, b1 = lax.ppermute(a2, "dp", y), lax.ppermute(b1, "dp", x)
-        a1, a2, b1, prev_grad = lax.optimization_barrier((a1, a2, b1, prev_grad))
+        a1, a2, a3, b1, b3, prev_grad, backs[0] = lax.optimization_barrier(
+            (a1, a2, a3, b1, b3, prev_grad, backs[0])
+        )
         a1, b2 = hop_sums(a1, a3, b2, b3)
-        backs[0] = tie(backs[0], a1)
+        vector = tie(vector, a1)
         a1, b2 = lax.ppermute(a1, "dp", x), lax.ppermute(b2, "dp", y)
+        for bit in (1, 2):
+            vector += lax.ppermute(vector, "mp", flip_pairs(mp, bit))
+        a0, vector = lax.optimization_barrier((a0, vector))
         total = plane_sums(((mine - k_of) % mp).astype(jnp.int32), a0, a1, a2, b0, b1, b2)
         backs[0] = scatter_tokens(backs[0])
         backs[0], total = lax.optimization_barrier((backs[0], total))
@@ -905,9 +911,6 @@
             me % 2 == 0, jnp.concatenate([keep, other], 0), jnp.concatenate([other, keep], 0)
         )
         vector = summed[at:]
-        for bit in (1, 2):
-            vector += lax.ppermute(vector, "mp", flip_pairs(mp, bit))
-        firsts[-1], vector = lax.optimization_barrier((firsts[-1], vector))
         d_in, d_down, d_out = gather_grads(ff_place, units, piece, head_width, firsts, seconds)
         backs[-1] = tie(backs[-1], d_in)
         inner_weight_grad = d_in

time: 372 us -> 352 us (0.946); the launches traced: 365 us -> 351 us
  waiting for transfers between devices: 151 us -> 123 us
  starting transfers between devices: 51.5 us -> 69.1 us
  Pallas kernels: 108 us -> 103 us
    ppermute x2, waiting for transfers between devices: 15.5 us -> 0.01 us  [on_device(): a1, b2 = (lax.ppermute(a1, 'dp', x), lax.ppermute(b2, 'dp', y))]
    ppermute x9, starting transfers between devices: 11.7 us -> 26.5 us  [shifted(): return lax.ppermute(array, 'mp', shift_pairs(mp, k)) if k else array]
    ppermute x9, waiting for transfers between devices: 26.1 us -> 13.8 us  [shifted(): return lax.ppermute(array, 'mp', shift_pairs(mp, k)) if k else array]
    pallas_call x2 -> x1, Pallas kernels: 17.6 us -> 8.52 us  [weight_grad(): pl.pallas_call(kernel, in_specs=[SMEM] + [ANY] * 4 + [VMEM, ANY], out_spe...]
    ppermute x2, waiting for transfers between devices: 11.7 us -> 15.9 us  [on_device(): vector += lax.ppermute(vector, 'mp', flip_pairs(mp, bit))]
    pallas_call x1, Pallas kernels: 29.4 us -> 33.4 us  [feed_forward(): pl.pallas_call(kernel, in_specs=in_specs, out_specs=[ANY] * len(joint_col...]
    unnamed x117 -> x113, local copies, waits for them, and re-layouts: 12.9 us -> 13.1 us
  transfers between devices with their start and end apart: 63 -> 63, of which waited for: 27 -> 27; matrix products, arithmetic and copies ran while one was open for 7% -> 8% of each run, Pallas kernels for 18% -> 20%
where the time goes in v4:
time: 352 us; the launch traced here: 351 us
  waiting for transfers between devices  123 us (35%)
  Pallas kernels  103 us (29%)
  starting transfers between devices  69.1 us (20%)
  local copies, waits for them, and re-layouts  30.6 us (9%)
  between operations  14.8 us (4%)
  other arithmetic  9.86 us (3%)
    ppermute x3, waiting for transfers between devices, relay(): lax.ppermute(above[-1], 'mp', [(mp - 1 - i, mp - 1 - j) for i, j in pairs])  47.4 us
    pallas_call x1, Pallas kernels, feed_forward(): pl.pallas_call(kernel, in_specs=in_specs, out_specs=[ANY] * len(joint_col...  33.4 us
    ppermute x9, starting transfers between devices, shifted(): return lax.ppermute(array, 'mp', shift_pairs(mp, k)) if k else array  26.5 us
    pallas_call x2, Pallas kernels, attend(): pl.pallas_call(functools.partial(attend_kernel, b, slots, heads, size), i...  25.8 us
    pallas_call x1, Pallas kernels, attend_back(): pl.pallas_call(functools.partial(attend_back_kernel, micro, slots, heads,...  23.5 us
    ppermute x2, waiting for transfers between devices, on_device(): vector += lax.ppermute(vector, 'mp', flip_pairs(mp, bit))  15.9 us
    ppermute x9, waiting for transfers between devices, shifted(): return lax.ppermute(array, 'mp', shift_pairs(mp, k)) if k else array  13.8 us
    unnamed x113, local copies, waits for them, and re-layouts  13.1 us
  transfers between devices with their start and end apart: 63, of which 27 were waited for; matrix products, arithmetic and copies ran while one was open for 8% of the time, Pallas kernels for 20%

profile of v4, /device:TPU:0, one launch (start us, length us, event | category | flops | bytes accessed | tf_op | source)
XLA Modules:
  0.0 350.8 jit_solution(4915213309920679494)
XLA Ops:
  7.3 2.1 slice_bitcast_fusion
  16.1 5.6 %collective-permute-start = (bf16[240,768]{1,0:T(8,128)(2,1)S(1)}, bf16[240,768]{1,0:T(8,128)(2,1)S(1)}, u32[]{:S(2)}, u32[]{:S(2)}) collective-permute-start(bf16[240,768]{1,0:T(8,128)(2,1)S(1)} %dynamic-slice_bitcast_fusion), channel_id=1, source_target_pairs={{0,1},{1,2},{2,3},{4,5},{5,6},{6,7},{8,9},{9,10},{10,11},{12,13},{... | collective-permute-start | bytes 1105928 | tf_op jit(solution)/shard_map/ppermute | solution.py:685
  21.7 18.0 %collective-permute-done.1 = bf16[240,768]{1,0:T(8,128)(2,1)S(1)} collective-permute-done((bf16[240,768]{1,0:T(8,128)(2,1)S(1)}, bf16[240,768]{1,0:T(8,128)(2,1)S(1)}, u32[]{:S(2)}, u32[]{:S(2)}) %collective-permute-start.1) | collective-permute-done | bytes 368672 | tf_op jit(solution)/shard_map/ppermute | solution.py:686
  41.7 19.8 %collective-permute-done.2 = bf16[240,768]{1,0:T(8,128)(2,1)S(1)} collective-permute-done((bf16[240,768]{1,0:T(8,128)(2,1)S(1)}, bf16[240,768]{1,0:T(8,128)(2,1)S(1)}, u32[]{:S(2)}, u32[]{:S(2)}) %collective-permute-start.2) | collective-permute-done | bytes 368672 | tf_op jit(solution)/shard_map/ppermute | solution.py:686
  63.6 9.6 %collective-permute-done.3 = bf16[240,768]{1,0:T(8,128)(2,1)S(1)} collective-permute-done((bf16[240,768]{1,0:T(8,128)(2,1)S(1)}, bf16[240,768]{1,0:T(8,128)(2,1)S(1)}, u32[]{:S(2)}, u32[]{:S(2)}) %collective-permute-start.3) | collective-permute-done | bytes 368672 | tf_op jit(solution)/shard_map/ppermute | solution.py:686
  73.6 2.1 collective-permute-start.6
  80.9 12.9 %attend.2 = (bf16[2,2,3,512,512]{4,3,2,1,0:T(8,128)(2,1)}, bf16[2,3,512,512]{3,2,1,0:T(8,128)(2,1)}, bf16[2,512,576]{2,1,0:T(8,128)(2,1)}, bf16[2,512,192]{2,1,0:T(8,128)(2,1)}) custom-call(bf16[2,512,768]{2,1,0:T(8,128)(2,1)} %all-gather.3.cloned.1.call-done.tok.refs_0_, bf16[768,576]{1,0:T(8,128)(2,1)} %pad_maximum_fusion.3.w.refs_8_, ...), custom_call_target="tpu_custom_call" | custom-call | flops 2516582400 | bytes 9437184 | tf_op jit(solution)/shard_map/attend/pallas_call | solution.py:109
  97.7 14.6 %collective-permute-start.12 = (bf16[2,128,192]{2,1,0:T(8,128)(2,1)S(1)}, bf16[2,128,192]{2,1,0:T(8,128)(2,1)S(1)}, u32[]{:S(2)}, u32[]{:S(2)}) collective-permute-start(bf16[2,128,192]{2,1,0:T(8,128)(2,1)S(1)} %get-tuple-element.222), channel_id=1, source_target_pairs={{0,3},{1,0},{2,1},{3,2},{4,7},{5,4},{6,5},{7,6},{8,11},{9,8},{10,9... | collective-permute-start | bytes 294920 | tf_op jit(solution)/shard_map/ppermute | solution.py:748
  115.9 12.9 %attend.3 = (bf16[2,2,3,512,512]{4,3,2,1,0:T(8,128)(2,1)}, bf16[2,3,512,512]{3,2,1,0:T(8,128)(2,1)}, bf16[2,512,576]{2,1,0:T(8,128)(2,1)}, bf16[2,512,192]{2,1,0:T(8,128)(2,1)}) custom-call(bf16[2,512,768]{2,1,0:T(8,128)(2,1)} %all-gather.5.cloned.1.call-done.tok.refs_1_, ...), custom_call_target="tpu_custom_call", output_to_operand_aliasing={{0}: (5, {})} | custom-call | flops 2516582400 | bytes 9437184 | tf_op jit(solution)/shard_map/attend/pallas_call | solution.py:109
  128.8 3.9 %collective-permute-start.10 = (bf16[2,128,192]{2,1,0:T(8,128)(2,1)S(1)}, bf16[2,128,192]{2,1,0:T(8,128)(2,1)S(1)}, u32[]{:S(2)}, u32[]{:S(2)}) collective-permute-start(bf16[2,128,192]{2,1,0:T(8,128)(2,1)S(1)} %get-tuple-element.224), channel_id=1, source_target_pairs={{0,1},{1,2},{2,3},{3,0},{4,5},{5,6},{6,7},{7,4},{8,9},{9,10},{10,1... | collective-permute-start | bytes 294920 | tf_op jit(solution)/shard_map/ppermute | solution.py:748
  137.2 2.7 collective-permute-start.14
  140.6 2.7 collective-permute-done.15
  143.3 4.2 %collective-permute-done.14 = bf16[2,128,192]{2,1,0:T(8,128)(2,1)S(1)} collective-permute-done((bf16[2,128,192]{2,1,0:T(8,128)(2,1)S(1)}, bf16[2,128,192]{2,1,0:T(8,128)(2,1)S(1)}, u32[]{:S(2)}, u32[]{:S(2)}) %collective-permute-start.14) | collective-permute-done | bytes 98336 | tf_op jit(solution)/shard_map/ppermute | solution.py:748
  150.6 33.4 %feed_forward.1 = (bf16[512,768]{1,0:T(8,128)(2,1)}, bf16[512,3072]{1,0:T(8,128)(2,1)}, bf16[512,768]{1,0:T(8,128)(2,1)}, bf16[512,3072]{1,0:T(8,128)(2,1)}, bf1...) custom-call(s32[12]{0:T(128)} %pad_add_fusion.place, ...), custom_call_target="tpu_custom_call" | custom-call | flops 10871635968 | bytes 17301504 | tf_op jit(solution)/shard_map/feed_forward/pallas_call | solution.py:505
  188.0 5.4 %collective-permute-done.26.got = bf16[4,4,224,768]{3,2,1,0:T(8,128)(2,1)} collective-permute-done((bf16[4,4,224,768]{3,2,1,0:T(8,128)(2,1)}, bf16[4,4,224,768]{3,2,1,0:T(8,128)(2,1)}, u32[]{:S(2)}, u32[]{:S(2)}) %collective-permute-start.26) | collective-permute-done | bytes 5505056 | tf_op jit(solution)/shard_map/ppermute | solution.py:873
  193.5 8.5 %weight_grad.1 = (bf16[4,112,768]{2,1,0:T(8,128)(2,1)}, bf16[4,112,768]{2,1,0:T(8,128)(2,1)}, bf16[4,112,768]{2,1,0:T(8,128)(2,1)}, bf16[4,112,768]{2,1,0:T(8,12...) custom-call(s32[12]{0:T(128)} %pad_add_fusion.place, ...), custom_call_target="tpu_custom_call" | custom-call | flops 3019898880 | bytes 6144000 | tf_op jit(solution)/shard_map/weight_grad/pallas_call | solution.py:587
  205.6 4.4 %collective-permute-done.32 = bf16[512,192]{1,0:T(8,128)(2,1)S(1)} collective-permute-done((bf16[512,192]{1,0:T(8,128)(2,1)}, bf16[512,192]{1,0:T(8,128)(2,1)S(1)}, u32[]{:S(2)}, u32[]{:S(2)}) %collective-permute-start.32) | collective-permute-done | bytes 196640 | tf_op jit(solution)/shard_map/ppermute | solution.py:748
  212.3 23.5 %attend_back.1 = (f32[2,2,3,512,512]{4,3,2,1,0:T(8,128)}, f32[768,576]{1,0:T(8,128)}, f32[8,576]{1,0:T(8,128)}, bf16[2,512,768]{2,1,0:T(8,128)(2,1)}, bf16[2,512,768]{2,1,0:T(8,128)(2,1)}) custom-call(s32[4]{0:T(128)} %pad_add_fusion.1.place, bf16[2,512,768]{2,1,0:T(8,128)(2,1)} %all-gather.3.cloned.1.call-done.tok.refs_0_, ...), custom_call_target="tpu_custom_call" | custom-call | flops 10066329600 | bytes 25165824 | tf_op jit(solution)/shard_map/attend_back/pallas_call | solution.py:235
  237.7 3.0 hop_sum.1
  244.2 6.8 %collective-permute-done.34 = f32[24,576]{1,0:T(8,128)S(1)} collective-permute-done((f32[24,576]{1,0:T(8,128)S(1)}, f32[24,576]{1,0:T(8,128)S(1)}, u32[]{:S(2)}, u32[]{:S(2)}) %collective-permute-start.34) | collective-permute-done | bytes 55328 | tf_op jit(solution)/shard_map/ppermute | solution.py:888
  251.6 9.1 %collective-permute-done.35 = f32[24,576]{1,0:T(8,128)S(1)} collective-permute-done((f32[24,576]{1,0:T(8,128)S(1)}, f32[24,576]{1,0:T(8,128)S(1)}, u32[]{:S(2)}, u32[]{:S(2)}) %collective-permute-start.35) | collective-permute-done | bytes 55328 | tf_op jit(solution)/shard_map/ppermute | solution.py:888
  262.4 3.7 %plane_sum.1 = bf16[4,224,768]{2,1,0:T(8,128)(2,1)} custom-call(s32[4]{0:T(128)} %fusion.19.here, bf16[4,112,768]{2,1,0:T(8,128)(2,1)} %get-tuple-element.147.a0, bf16[4,112,768]{2,1,0:T(8,128)(2,1)} %copy-done.13, bf16[4,112,768]{2,1,0:T(8,128)(2,1)} %copy-done.10, bf16[4,112,768]{2,1,0:T(8,128)(2,1)} %get-tuple-element.132.b0, ...), custom_call_target="tpu_custom_call" | custom-call | tf_op jit(solution)/shard_map/plane_sum/pallas_call | solution.py:629
  266.1 6.0 %reduce-scatter.4.cloned.1.call-done = bf16[2,128,768]{2,1,0:T(8,128)(2,1)} async-done(((bf16[2,512,768]{2,1,0:T(8,128)(2,1)}), bf16[2,128,768]{2,1,0:T(8,128)(2,1)}) %reduce-scatter.4.cloned.1.call-update) | async-done | bytes 393232 | tf_op jit(solution)/shard_map/reduce_scatter | solution.py:866
  274.9 2.8 collective-permute-done.52
  281.0 10.8 %collective-permute-done.53 = f32[200,576]{1,0:T(8,128)S(1)} collective-permute-done((f32[200,576]{1,0:T(8,128)S(1)}, f32[200,576]{1,0:T(8,128)S(1)}, u32[]{:S(2)}, u32[]{:S(2)}) %collective-permute-start.53) | collective-permute-done | bytes 460832 | tf_op jit(solution)/shard_map/ppermute | solution.py:900
  295.2 10.6 %collective-permute-done.54 = f32[200,576]{1,0:T(8,128)S(1)} collective-permute-done((f32[200,576]{1,0:T(8,128)S(1)}, f32[200,576]{1,0:T(8,128)S(1)}, u32[]{:S(2)}, u32[]{:S(2)}) %collective-permute-start.54) | collective-permute-done | bytes 460832 | tf_op jit(solution)/shard_map/ppermute | solution.py:903
  319.3 2.5 collective-permute-start.40
  323.4 2.2 copy.56
  325.6 2.2 copy.55
  333.9 5.1 %gather_grads.1 = (f32[768,768]{1,0:T(8,128)}, f32[8,96,768]{2,1,0:T(8,128)}, f32[12,16,768]{2,1,0:T(8,128)}) custom-call(s32[12]{0:T(128)} %pad_add_fusion.place, bf16[112,768]{1,0:T(8,128)(2,1)} %copy-done.9, bf16[112,768]{1,0:T(8,128)(2,1)} %collective-permute-done.38.refs_1_, bf16[112,768]{1,0:T(8,128)(2,1)} %copy-done.21, ...), custom_call_target="tpu_custom_call" | custom-call | tf_op jit(solution)/shard_map/gather_grads/pallas_call | solution.py:667
  339.0 2.9 reduce-scatter.6.cloned.1.call-done
  342.0 2.3 convert_add_fusion
  (303 shorter events, 79.5 us)
Async XLA Ops:
  7.2 73.7 %all-gather.3.cloned.1.call-start = ((), (), s32[]{:S(2)}) async-start(), calls=%async_computation.3 | async-start | bytes 1966080 | tf_op jit(solution)/shard_map/all_gather | solution.py:794
  9.4 106.4 %all-gather.5.cloned.1.call-start = ((), (), s32[]{:S(2)}) async-start(), calls=%async_computation.4 | async-start | bytes 1966080 | tf_op jit(solution)/shard_map/all_gather | solution.py:794
  14.8 24.9 %collective-permute-start.1 = (bf16[240,768]{1,0:T(8,128)(2,1)S(1)}, bf16[240,768]{1,0:T(8,128)(2,1)S(1)}, u32[]{:S(2)}, u32[]{:S(2)}) collective-permute-start(bf16[240,768]{1,0:T(8,128)(2,1)S(1)} %dynamic-slice_bitcast_fusion), channel_id=1, source_target_pairs={{3,2},{2,1},{1,0},{7,6},{6,5},{5,4},{11,10},{10,9},{9,8},{15,14},{... | collective-permute-start | bytes 1105928 | tf_op jit(solution)/shard_map/ppermute | solution.py:686
  16.1 24.9 %collective-permute-start = (bf16[240,768]{1,0:T(8,128)(2,1)S(1)}, bf16[240,768]{1,0:T(8,128)(2,1)S(1)}, u32[]{:S(2)}, u32[]{:S(2)}) collective-permute-start(bf16[240,768]{1,0:T(8,128)(2,1)S(1)} %dynamic-slice_bitcast_fusion), channel_id=1, source_target_pairs={{0,1},{1,2},{2,3},{4,5},{5,6},{6,7},{8,9},{9,10},{10,11},{12,13},{... | collective-permute-start | bytes 1105928 | tf_op jit(solution)/shard_map/ppermute | solution.py:685
  39.7 21.8 %collective-permute-start.2 = (bf16[240,768]{1,0:T(8,128)(2,1)S(1)}, bf16[240,768]{1,0:T(8,128)(2,1)S(1)}, u32[]{:S(2)}, u32[]{:S(2)}) collective-permute-start(bf16[240,768]{1,0:T(8,128)(2,1)S(1)} %collective-permute-done.1), channel_id=1, source_target_pairs={{2,1},{1,0},{6,5},{5,4},{10,9},{9,8},{14,13},{13,12},{18,17},{17,1... | collective-permute-start | bytes 1105928 | tf_op jit(solution)/shard_map/ppermute | solution.py:686
  41.0 20.5 %collective-permute-start.4 = (bf16[240,768]{1,0:T(8,128)(2,1)S(1)}, bf16[240,768]{1,0:T(8,128)(2,1)S(1)}, u32[]{:S(2)}, u32[]{:S(2)}) collective-permute-start(bf16[240,768]{1,0:T(8,128)(2,1)S(1)} %collective-permute-done), channel_id=1, source_target_pairs={{1,2},{2,3},{5,6},{6,7},{9,10},{10,11},{13,14},{14,15},{17,18},{18... | collective-permute-start | bytes 1105928 | tf_op jit(solution)/shard_map/ppermute | solution.py:685
  61.5 210.6 %reduce-scatter.4.cloned.1.call-start = ((), (), s32[]{:S(2)}) async-start(), calls=%async_computation.5 | async-start | bytes 1966080 | tf_op jit(solution)/shard_map/reduce_scatter | solution.py:866
  73.6 20.4 %collective-permute-start.6 = (bf16[3,128,768]{2,1,0:T(8,128)(2,1)S(1)}, bf16[3,128,768]{2,1,0:T(8,128)(2,1)S(1)}, u32[]{:S(2)}, u32[]{:S(2)}) collective-permute-start(bf16[3,128,768]{2,1,0:T(8,128)(2,1)S(1)} %slice.132.refs_12_), channel_id=1, source_target_pairs={{0,8},{4,12},{8,0},{12,4},{16,24},{20,28},{24,16},{28,20},{1,9},{5... | collective-permute-start | bytes 1769480 | tf_op jit(solution)/shard_map/ppermute | solution.py:640
  75.7 18.1 %collective-permute-start.7 = (bf16[3,112,768]{2,1,0:T(8,128)(2,1)S(1)}, bf16[3,112,768]{2,1,0:T(8,128)(2,1)}, u32[]{:S(2)}, u32[]{:S(2)}) collective-permute-start(bf16[3,112,768]{2,1,0:T(8,128)(2,1)S(1)} %pad_maximum_fusion.4.refs_20_), channel_id=1, source_target_pairs={{0,16},{4,20},{8,24},{12,28},{16,0},{20,4},{24,8},{28,12},{1,17},{... | collective-permute-start | bytes 1548296 | tf_op jit(solution)/shard_map/ppermute | solution.py:640
  77.3 20.5 %collective-permute-start.22 = (bf16[3,112,768]{2,1,0:T(8,128)(2,1)S(1)}, bf16[3,112,768]{2,1,0:T(8,128)(2,1)}, u32[]{:S(2)}, u32[]{:S(2)}) collective-permute-start(bf16[3,112,768]{2,1,0:T(8,128)(2,1)S(1)} %pad_maximum_fusion.4.refs_20_), channel_id=1, source_target_pairs={{0,4},{4,0},{8,12},{12,8},{16,20},{20,16},{24,28},{28,24},{1,5},{5... | collective-permute-start | bytes 1548296 | tf_op jit(solution)/shard_map/ppermute | solution.py:841
  77.3 36.6 %collective-permute-start.17 = (bf16[3,128,768]{2,1,0:T(8,128)(2,1)S(1)}, bf16[3,128,768]{2,1,0:T(8,128)(2,1)}, u32[]{:S(2)}, u32[]{:S(2)}) collective-permute-start(bf16[3,128,768]{2,1,0:T(8,128)(2,1)S(1)} %slice.132.refs_12_), channel_id=1, source_target_pairs={{0,4},{4,0},{8,12},{12,8},{16,20},{20,16},{24,28},{28,24},{1,5},{5... | collective-permute-start | bytes 1769480 | tf_op jit(solution)/shard_map/ppermute | solution.py:841
  79.0 33.4 %collective-permute-start.21 = (bf16[3,112,768]{2,1,0:T(8,128)(2,1)S(1)}, bf16[3,112,768]{2,1,0:T(8,128)(2,1)}, u32[]{:S(2)}, u32[]{:S(2)}) collective-permute-start(bf16[3,112,768]{2,1,0:T(8,128)(2,1)S(1)} %pad_maximum_fusion.4.refs_20_), channel_id=1, source_target_pairs={{0,8},{4,12},{8,0},{12,4},{16,24},{20,28},{24,16},{28,20},{1,9},{5... | collective-permute-start | bytes 1548296 | tf_op jit(solution)/shard_map/ppermute | solution.py:641
  93.8 46.1 %collective-permute-start.16 = (bf16[3,128,768]{2,1,0:T(8,128)(2,1)S(1)}, bf16[3,128,768]{2,1,0:T(8,128)(2,1)S(1)}, u32[]{:S(2)}, u32[]{:S(2)}) collective-permute-start(bf16[3,128,768]{2,1,0:T(8,128)(2,1)S(1)} %slice.132.refs_12_), channel_id=1, source_target_pairs={{0,16},{4,20},{8,24},{12,28},{16,0},{20,4},{24,8},{28,12},{1,17},{... | collective-permute-start | bytes 1769480 | tf_op jit(solution)/shard_map/ppermute | solution.py:641
  94.0 46.0 %collective-permute-start.8 = (bf16[3,128,768]{2,1,0:T(8,128)(2,1)S(1)}, bf16[3,128,768]{2,1,0:T(8,128)(2,1)}, u32[]{:S(2)}, u32[]{:S(2)}) collective-permute-start(bf16[3,128,768]{2,1,0:T(8,128)(2,1)S(1)} %collective-permute-done.6.refs_13_), channel_id=1, source_target_pairs={{0,16},{4,20},{8,24},{12,28},{16,0},{20,4},{24,8},{28,12},{1,17},{... | collective-permute-start | bytes 1769480 | tf_op jit(solution)/shard_map/ppermute | solution.py:643
  97.7 17.2 %collective-permute-start.12 = (bf16[2,128,192]{2,1,0:T(8,128)(2,1)S(1)}, bf16[2,128,192]{2,1,0:T(8,128)(2,1)S(1)}, u32[]{:S(2)}, u32[]{:S(2)}) collective-permute-start(bf16[2,128,192]{2,1,0:T(8,128)(2,1)S(1)} %get-tuple-element.222), channel_id=1, source_target_pairs={{0,3},{1,0},{2,1},{3,2},{4,7},{5,4},{6,5},{7,6},{8,11},{9,8},{10,9... | collective-permute-start | bytes 294920 | tf_op jit(solution)/shard_map/ppermute | solution.py:748
  112.3 24.9 %collective-permute-start.9 = (bf16[3,112,768]{2,1,0:T(8,128)(2,1)}, bf16[3,112,768]{2,1,0:T(8,128)(2,1)S(1)}, u32[]{:S(2)}, u32[]{:S(2)}) collective-permute-start(bf16[3,112,768]{2,1,0:T(8,128)(2,1)} %collective-permute-done.7.refs_22_), channel_id=1, source_target_pairs={{0,8},{4,12},{8,0},{12,4},{16,24},{20,28},{24,16},{28,20},{1,9},{5... | collective-permute-start | bytes 1548296 | tf_op jit(solution)/shard_map/ppermute | solution.py:643
  113.8 26.2 %collective-permute-start.23 = (bf16[3,112,768]{2,1,0:T(8,128)(2,1)}, bf16[3,112,768]{2,1,0:T(8,128)(2,1)}, u32[]{:S(2)}, u32[]{:S(2)}) collective-permute-start(bf16[3,112,768]{2,1,0:T(8,128)(2,1)} %collective-permute-done.21.refs_21_), channel_id=1, source_target_pairs={{0,4},{4,0},{8,12},{12,8},{16,20},{20,16},{24,28},{28,24},{1,5},{5... | collective-permute-start | bytes 1548296 | tf_op jit(solution)/shard_map/ppermute | solution.py:841
  185.0 19.1 %collective-permute-start.31 = (bf16[512,192]{1,0:T(8,128)(2,1)}, bf16[512,192]{1,0:T(8,128)(2,1)S(1)}, u32[]{:S(2)}, u32[]{:S(2)}) collective-permute-start(bf16[512,192]{1,0:T(8,128)(2,1)} %get-tuple-element.134), channel_id=1, source_target_pairs={{0,3},{1,0},{2,1},{3,2},{4,7},{5,4},{6,5},{7,6},{8,11},{9,8},{10,9... | collective-permute-start | bytes 589832 | tf_op jit(solution)/shard_map/ppermute | solution.py:748
  186.0 24.0 %collective-permute-start.32 = (bf16[512,192]{1,0:T(8,128)(2,1)}, bf16[512,192]{1,0:T(8,128)(2,1)S(1)}, u32[]{:S(2)}, u32[]{:S(2)}) collective-permute-start(bf16[512,192]{1,0:T(8,128)(2,1)} %get-tuple-element.135), channel_id=1, source_target_pairs={{0,2},{1,3},{2,0},{3,1},{4,6},{5,7},{6,4},{7,5},{8,10},{9,11},{10,... | collective-permute-start | bytes 589832 | tf_op jit(solution)/shard_map/ppermute | solution.py:748
  186.0 25.5 %collective-permute-start.33 = (bf16[512,192]{1,0:T(8,128)(2,1)}, bf16[512,192]{1,0:T(8,128)(2,1)S(1)}, u32[]{:S(2)}, u32[]{:S(2)}) collective-permute-start(bf16[512,192]{1,0:T(8,128)(2,1)} %get-tuple-element.136), channel_id=1, source_target_pairs={{0,1},{1,2},{2,3},{3,0},{4,5},{5,6},{6,7},{7,4},{8,9},{9,10},{10,1... | collective-permute-start | bytes 589832 | tf_op jit(solution)/shard_map/ppermute | solution.py:748
  202.0 33.8 %collective-permute-start.27 = (bf16[4,112,768]{2,1,0:T(8,128)(2,1)}, bf16[4,112,768]{2,1,0:T(8,128)(2,1)S(1)}, u32[]{:S(2)}, u32[]{:S(2)}) collective-permute-start(bf16[4,112,768]{2,1,0:T(8,128)(2,1)} %get-tuple-element.121), channel_id=1, source_target_pairs={{0,16},{4,20},{8,24},{12,28},{16,0},{20,4},{24,8},{28,12},{1,17},{... | collective-permute-start | bytes 2064392 | tf_op jit(solution)/shard_map/ppermute | solution.py:880
  202.6 33.2 %collective-permute-start.28 = (bf16[4,112,768]{2,1,0:T(8,128)(2,1)}, bf16[4,112,768]{2,1,0:T(8,128)(2,1)S(1)}, u32[]{:S(2)}, u32[]{:S(2)}) collective-permute-start(bf16[4,112,768]{2,1,0:T(8,128)(2,1)} %get-tuple-element.122), channel_id=1, source_target_pairs={{0,16},{4,20},{8,24},{12,28},{16,0},{20,4},{24,8},{28,12},{1,17},{... | collective-permute-start | bytes 2064392 | tf_op jit(solution)/shard_map/ppermute | solution.py:879
  204.1 31.7 %collective-permute-start.29 = (bf16[4,112,768]{2,1,0:T(8,128)(2,1)}, bf16[4,112,768]{2,1,0:T(8,128)(2,1)S(1)}, u32[]{:S(2)}, u32[]{:S(2)}) collective-permute-start(bf16[4,112,768]{2,1,0:T(8,128)(2,1)} %get-tuple-element.123), channel_id=1, source_target_pairs={{0,8},{4,12},{8,0},{12,4},{16,24},{20,28},{24,16},{28,20},{1,9},{5... | collective-permute-start | bytes 2064392 | tf_op jit(solution)/shard_map/ppermute | solution.py:880
  210.0 26.2 %collective-permute-start.30 = (bf16[4,112,768]{2,1,0:T(8,128)(2,1)}, bf16[4,112,768]{2,1,0:T(8,128)(2,1)S(1)}, u32[]{:S(2)}, u32[]{:S(2)}) collective-permute-start(bf16[4,112,768]{2,1,0:T(8,128)(2,1)} %get-tuple-element.124), channel_id=1, source_target_pairs={{0,8},{4,12},{8,0},{12,4},{16,24},{20,28},{24,16},{28,20},{1,9},{5... | collective-permute-start | bytes 2064392 | tf_op jit(solution)/shard_map/ppermute | solution.py:879
  236.2 71.1 %reduce-scatter.8.cloned.1.call-start = ((), (), s32[]{:S(2)}) async-start(), calls=%async_computation.7 | async-start | bytes 1720320 | tf_op jit(solution)/shard_map/reduce_scatter | solution.py:893
  240.7 20.0 %collective-permute-start.37 = (bf16[4,112,768]{2,1,0:T(8,128)(2,1)}, bf16[4,112,768]{2,1,0:T(8,128)(2,1)S(1)}, u32[]{:S(2)}, u32[]{:S(2)}) collective-permute-start(bf16[4,112,768]{2,1,0:T(8,128)(2,1)} %get-tuple-element.150), channel_id=1, source_target_pairs={{0,16},{4,20},{8,24},{12,28},{16,0},{20,4},{24,8},{28,12},{1,17},{... | collective-permute-start | bytes 2064392 | tf_op jit(solution)/shard_map/ppermute | solution.py:886
  241.3 19.4 %collective-permute-start.36 = (bf16[4,112,768]{2,1,0:T(8,128)(2,1)}, bf16[4,112,768]{2,1,0:T(8,128)(2,1)S(1)}, u32[]{:S(2)}, u32[]{:S(2)}) collective-permute-start(bf16[4,112,768]{2,1,0:T(8,128)(2,1)} %get-tuple-element.145), channel_id=1, source_target_pairs={{0,8},{4,12},{8,0},{12,4},{16,24},{20,28},{24,16},{28,20},{1,9},{5... | collective-permute-start | bytes 2064392 | tf_op jit(solution)/shard_map/ppermute | solution.py:886
  272.1 69.8 %reduce-scatter.6.cloned.1.call-start = ((), (), s32[]{:S(2)}) async-start(), calls=%async_computation.6 | async-start | bytes 1966080 | tf_op jit(solution)/shard_map/reduce_scatter | solution.py:866
  312.4 17.8 %collective-permute-start.41 = (bf16[112,768]{1,0:T(8,128)(2,1)S(1)}, bf16[112,768]{1,0:T(8,128)(2,1)}, u32[]{:S(2)}, u32[]{:S(2)}) collective-permute-start(bf16[112,768]{1,0:T(8,128)(2,1)S(1)} %get-tuple-element.227.refs_0_), channel_id=1, source_target_pairs={{0,4},{4,0},{8,12},{12,8},{16,20},{20,16},{24,28},{28,24},{1,5},{5... | collective-permute-start | bytes 516104 | tf_op jit(solution)/shard_map/ppermute | solution.py:907
  314.2 16.0 %collective-permute-start.39 = (bf16[112,768]{1,0:T(8,128)(2,1)S(1)}, bf16[112,768]{1,0:T(8,128)(2,1)S(1)}, u32[]{:S(2)}, u32[]{:S(2)}) collective-permute-start(bf16[112,768]{1,0:T(8,128)(2,1)S(1)} %get-tuple-element.227.refs_0_), channel_id=1, source_target_pairs={{0,16},{4,20},{8,24},{12,28},{16,0},{20,4},{24,8},{28,12},{1,17},{... | collective-permute-start | bytes 516104 | tf_op jit(solution)/shard_map/ppermute | solution.py:641
  315.8 14.8 %collective-permute-start.50 = (bf16[112,768]{1,0:T(8,128)(2,1)}, bf16[112,768]{1,0:T(8,128)(2,1)}, u32[]{:S(2)}, u32[]{:S(2)}) collective-permute-start(bf16[112,768]{1,0:T(8,128)(2,1)} %collective-permute-done.46.refs_10_), channel_id=1, source_target_pairs={{0,4},{4,0},{8,12},{12,8},{16,20},{20,16},{24,28},{28,24},{1,5},{5... | collective-permute-start | bytes 516104 | tf_op jit(solution)/shard_map/ppermute | solution.py:908
  316.8 14.0 %collective-permute-start.47 = (bf16[112,768]{1,0:T(8,128)(2,1)}, bf16[112,768]{1,0:T(8,128)(2,1)}, u32[]{:S(2)}, u32[]{:S(2)}) collective-permute-start(bf16[112,768]{1,0:T(8,128)(2,1)} %collective-permute-done.46.refs_10_), channel_id=1, source_target_pairs={{0,8},{4,12},{8,0},{12,4},{16,24},{20,28},{24,16},{28,20},{1,9},{5... | collective-permute-start | bytes 516104 | tf_op jit(solution)/shard_map/ppermute | solution.py:643
  (84 other events, 729.5 us)
Sparse Core Ops, SparseCore 0:
  10.2 50.6 all-gather.2
  63.0 38.3 all-gather.4
  236.3 35.7 reduce-scatter.3
  274.3 31.2 reduce-scatter.7
  307.8 34.1 reduce-scatter.5

commit v5 on v4

--- a/solution.py
+++ b/solution.py
@@ -33,8 +33,8 @@
     return copy
 
 def attend_kernel(b, slots, heads, size, tok, w, bias, prev, seg, *refs):
-    logits, probs, qkv, ctx = refs[-17:-13]
-    tok_v, prev_v, logits_v, probs_v, qkv_v, ctx_v, w_v, qs, ks, vs = refs[-13:-3]
+    logits, probs, qkv, ctx = refs[-15:-11]
+    tok_v, prev_v, logits_v, probs_v, ctx_v, w_v, parts, cs = refs[-11:-3]
     sem_in, sem_out, sem_w = refs[-3:]
     length = tok_v.shape[1]
     width = heads * size
@@ -52,13 +52,12 @@
 
     def project(s, _):
         rows = (mm(tok_v[s], w_v[...], 1, 0) + bias[...]).astype(BF16)
-        qkv_v[s] = rows
-        start(qkv_v.at[s], qkv.at[s], sem_out.at[s, 2 * heads])
         for h in range(heads):
             at = h * size
-            qs[s, h] = rows[:, at : at + size] * (1.0 / math.sqrt(size))
-            ks[s, h] = rows[:, width + at : width + at + size]
-            vs[s, h] = rows[:, 2 * width + at : 2 * width + at + size]
+            parts[s, 0, h] = rows[:, at : at + size] * (1.0 / math.sqrt(size))
+            parts[s, 1, h] = rows[:, width + at : width + at + size]
+            parts[s, 2, h] = rows[:, 2 * width + at : 2 * width + at + size]
+        start(parts.at[s], qkv.at[s], sem_out.at[s, 2 * heads])
         return _
 
     lax.fori_loop(0, slots, project, 0)
@@ -68,7 +67,7 @@
         seg_k = seg[b, pl.ds(s, 1), :]
         seg_q = jnp.broadcast_to(seg_k, (8, length)).T[:, :1]
         pltpu.make_async_copy(prev.at[b, s, h], prev_v.at[s, h], sem_in.at[s, h]).wait()
-        q, k, v = qs[s, h], ks[s, h], vs[s, h]
+        q, k, v = (parts[s, j, h] for j in range(3))
         scores = mm(q, k, 1, 1) + prev_v[s, h].astype(F32)
         logits_v[s, h] = scores.astype(BF16)
         start(logits_v.at[s, h], logits.at[b, s, h], sem_out.at[s, h])
@@ -77,18 +76,18 @@
         p = (exponent * (1.0 / jnp.sum(exponent, -1, keepdims=True))).astype(BF16)
         probs_v[s, h] = p
         start(probs_v.at[s, h], probs.at[s, h], sem_out.at[s, heads + h])
-        qs[s, h] = mm(p, v, 1, 0).astype(BF16)
+        cs[s, h] = mm(p, v, 1, 0).astype(BF16)
         return _
 
     lax.fori_loop(0, slots * heads, one_head, 0)
     for s in range(slots):
-        ctx_v[s] = jnp.concatenate([qs[s, h] for h in range(heads)], -1)
+        ctx_v[s] = jnp.concatenate([cs[s, h] for h in range(heads)], -1)
         start(ctx_v.at[s], ctx.at[s], sem_out.at[s, 2 * heads + 1])
     for s in range(slots):
         for h in range(heads):
             pltpu.make_async_copy(logits_v.at[s, h], logits.at[b, s, h], sem_out.at[s, h]).wait()
             pltpu.make_async_copy(probs_v.at[s, h], probs.at[s, h], sem_out.at[s, heads + h]).wait()
-        pltpu.make_async_copy(qkv_v.at[s], qkv.at[s], sem_out.at[s, 2 * heads]).wait()
+        pltpu.make_async_copy(parts.at[s], qkv.at[s], sem_out.at[s, 2 * heads]).wait()
         pltpu.make_async_copy(ctx_v.at[s], ctx.at[s], sem_out.at[s, 2 * heads + 1]).wait()
 
 
@@ -113,14 +112,14 @@
         out_shape=[
             jax.ShapeDtypeStruct(prev_logits.shape, BF16),
             jax.ShapeDtypeStruct((slots, heads, length, length), BF16),
-            jax.ShapeDtypeStruct((slots, length, cols), BF16),
+            jax.ShapeDtypeStruct((slots, 3, heads, length, size), BF16),
             jax.ShapeDtypeStruct((slots, length, cols // 3), BF16),
         ],
         scratch_shapes=[
             pltpu.VMEM((slots, length, width), BF16), square, square, square,
-            pltpu.VMEM((slots, length, cols), BF16), pltpu.VMEM((slots, length, cols // 3), BF16),
-            pltpu.VMEM((width, cols), BF16),
-            *[pltpu.VMEM((slots, heads, length, size), BF16)] * 3,
+            pltpu.VMEM((slots, length, cols // 3), BF16), pltpu.VMEM((width, cols), BF16),
+            pltpu.VMEM((slots, 3, heads, length, size), BF16),
+            pltpu.VMEM((slots, heads, length, size), BF16),
             pltpu.SemaphoreType.DMA((slots, heads + 1)),
             pltpu.SemaphoreType.DMA((slots, 2 * heads + 2)), pltpu.SemaphoreType.DMA,
         ],
@@ -134,8 +133,8 @@
 def attend_back_kernel(micro, slots, heads, size, n_blocks, place, *refs):
     tok, qkv, ctx, probs = (refs[i * micro : (i + 1) * micro] for i in range(4))
     w, cot, *blocks = refs[4 * micro : 4 * micro + 2 + n_blocks]
-    prev_grad, acc, bias_acc, *backs = refs[-16 - micro : -13]
-    tok_v, qkv_v, ctx_v, dctx_v, probs_v, cot_v, grad_v, back_v, w_v, parts, deltas = refs[-13:-2]
+    prev_grad, acc, bias_acc, *backs = refs[-15 - micro : -12]
+    tok_v, ctx_v, dctx_v, probs_v, cot_v, grad_v, back_v, w_v, parts, deltas = refs[-12:-2]
     sem_in, sem_out = refs[-2:]
     length = tok_v.shape[1]
     width = heads * size
@@ -145,7 +144,7 @@
     for s in range(total):
         b, t = divmod(s, slots)
         first += [
-            start(qkv[b].at[t], qkv_v.at[s], sem_in.at[s, 0]),
+            start(qkv[b].at[t], parts.at[s, pl.ds(0, 3)], sem_in.at[s, 0]),
             start(ctx[b].at[t], ctx_v.at[s], sem_in.at[s, 1]),
         ]
         for j in range(n_blocks):
@@ -164,14 +163,11 @@
         copy.wait()
 
     def split(s, _):
-        rows, d_all = qkv_v[s], dctx_v[s]
+        d_all = dctx_v[s]
         product = d_all.astype(F32) * ctx_v[s].astype(F32)
         for h in range(heads):
             at = h * size
-            parts[0, s, h] = rows[:, at : at + size]
-            parts[1, s, h] = rows[:, width + at : width + at + size]
-            parts[2, s, h] = rows[:, 2 * width + at : 2 * width + at + size]
-            parts[3, s, h] = d_all[:, at : at + size]
+            parts[s, 3, h] = d_all[:, at : at + size]
             deltas[s, h] = jnp.sum(product[:, at : at + size], -1, keepdims=True)
         return _
 
@@ -191,15 +187,15 @@
             probs[0].at[0, h], probs_v.at[s, h], sem_in.at[s, 3 + n_blocks + h]).wait()
         pltpu.make_async_copy(
             cot.at[0, 0, h], cot_v.at[s, h], sem_in.at[s, 3 + n_blocks + heads + h]).wait()
-        q, k, v, d_context = (parts[j, s, h] for j in range(4))
+        q, k, v, d_context = (parts[s, j, h] for j in range(4))
         p = probs_v[s, h]
         d_scores = p.astype(F32) * (mm(d_context, v, 1, 1) - deltas[s, h]) + cot_v[s, h].astype(F32)
         grad_v[s, h] = d_scores
         leave(s, h).start()
         d_dots = (d_scores * (1.0 / math.sqrt(size))).astype(BF16)
-        parts[0, s, h] = mm(d_dots, k, 1, 0).astype(BF16)
-        parts[1, s, h] = mm(q, d_dots, 0, 0).T.astype(BF16)
-        parts[2, s, h] = mm(d_context, p, 0, 0).T.astype(BF16)
+        parts[s, 0, h] = mm(d_dots, k, 1, 0).astype(BF16)
+        parts[s, 1, h] = (mm(q, d_dots, 0, 0) * math.sqrt(size)).T.astype(BF16)
+        parts[s, 2, h] = mm(d_context, p, 0, 0).T.astype(BF16)
         return _
 
     lax.fori_loop(0, total * heads, one_head, 0)
@@ -209,7 +205,7 @@
     bias_acc[...] = jnp.zeros_like(bias_acc)
 
     def finish(s, _):
-        d_qkv = jnp.concatenate([parts[j, s, h] for j in range(3) for h in range(heads)], -1)
+        d_qkv = jnp.concatenate([parts[s, j, h] for j in range(3) for h in range(heads)], -1)
         back_v[s] = mm(d_qkv, w_v[...], 1, 1).astype(BF16)
         for b in range(micro):
             pl.when(s // slots == b)(leave_back(s, b).start)
@@ -243,12 +239,11 @@
         ]
         + [jax.ShapeDtypeStruct((slots, length, width), BF16)] * micro,
         scratch_shapes=[
-            pltpu.VMEM((total, length, width), BF16), pltpu.VMEM((total, length, cols), BF16),
-            pltpu.VMEM((total, length, cols // 3), BF16),
+            pltpu.VMEM((total, length, width), BF16), pltpu.VMEM((total, length, cols // 3), BF16),
             pltpu.VMEM((total, length, cols // 3), BF16),
             pltpu.VMEM(square, BF16), pltpu.VMEM(square, BF16), pltpu.VMEM(square, F32),
             pltpu.VMEM((total, length, width), BF16), pltpu.VMEM((width, cols), BF16),
-            pltpu.VMEM((4, total, heads, length, size), BF16),
+            pltpu.VMEM((total, 4, heads, length, size), BF16),
             pltpu.VMEM((total, heads, length, 1), F32),
             pltpu.SemaphoreType.DMA((total, 3 + len(blocks) + 2 * heads)),
             pltpu.SemaphoreType.DMA((total, heads + 2)),
@@ -896,12 +891,9 @@
         keep = keep + lax.ppermute(send, "dp", swap)
         quarter = keep.shape[0] // 2
         top, low_part = keep[:quarter], keep[quarter:]
-        top, low_part = (
-            top + lax.ppermute(top, "dp", x), low_part + lax.ppermute(low_part, "dp", y)
-        )
-        top, low_part = (
-            top + lax.ppermute(top, "dp", y), low_part + lax.ppermute(low_part, "dp", x)
-        )
+        for one, two in ((x, y), (y, x)):
+            top = top + lax.ppermute(top.astype(BF16), "dp", one).astype(F32)
+            low_part = low_part + lax.ppermute(low_part.astype(BF16), "dp", two).astype(F32)
         keep = jnp.concatenate([top, low_part], 0)
         firsts, seconds = plane_gather(scattered[:cut], scattered[cut:], dp)
         firsts += [lax.ppermute(a, "dp", swap) for a in firsts]

time: 352 us -> 352 us (level)
  waiting for transfers between devices: 123 us -> 127 us
    ppermute x4, waiting for transfers between devices: 23.8 us -> 12.8 us  [the longest x2 10.4 us: on_device(): top = top + lax.ppermute(top.astype(BF16), 'dp', one).astype(F32)]
    reduce_scatter x1, waiting for transfers between devices: 0.02 us -> 9.73 us  [on_device(): scattered = lax.psum_scatter(total, 'mp', scatter_dimension=0)]
    unnamed x113 -> x109, local copies, waits for them, and re-layouts: 13.1 us -> 12.2 us
  transfers between devices with their start and end apart: 63 -> 63, of which waited for: 27 -> 29; matrix products, arithmetic and copies ran while one was open for 8% -> 8% of each run, Pallas kernels for 20% -> 20%
where the time goes in v5:
time: 352 us; the launch traced here: 351 us
  waiting for transfers between devices  127 us (36%)
  Pallas kernels  103 us (29%)
  starting transfers between devices  67.2 us (19%)
  local copies, waits for them, and re-layouts  29.6 us (8%)
  between operations  14.8 us (4%)
  other arithmetic  9.91 us (3%)
    ppermute x3, waiting for transfers between devices, relay(): lax.ppermute(above[-1], 'mp', [(mp - 1 - i, mp - 1 - j) for i, j in pairs])  47.4 us
    pallas_call x1, Pallas kernels, feed_forward(): pl.pallas_call(kernel, in_specs=in_specs, out_specs=[ANY] * len(joint_col...  33.4 us
    ppermute x9, starting transfers between devices, shifted(): return lax.ppermute(array, 'mp', shift_pairs(mp, k)) if k else array  26.5 us
    pallas_call x2, Pallas kernels, attend(): pl.pallas_call(functools.partial(attend_kernel, b, slots, heads, size), i...  25.8 us
    pallas_call x1, Pallas kernels, attend_back(): pl.pallas_call(functools.partial(attend_back_kernel, micro, slots, heads,...  23.5 us
    ppermute x2, waiting for transfers between devices, on_device(): vector += lax.ppermute(vector, 'mp', flip_pairs(mp, bit))  15.9 us
    ppermute x9, waiting for transfers between devices, shifted(): return lax.ppermute(array, 'mp', shift_pairs(mp, k)) if k else array  13.9 us
    unnamed x109, local copies, waits for them, and re-layouts  12.2 us
  transfers between devices with their start and end apart: 63, of which 29 were waited for; matrix products, arithmetic and copies ran while one was open for 8% of the time, Pallas kernels for 20%

profile of v5, /device:TPU:0, one launch (start us, length us, event | category | flops | bytes accessed | tf_op | source)
XLA Modules:
  0.0 351.4 jit_solution(8176156365168625996)
XLA Ops:
  7.3 2.1 slice_bitcast_fusion
  16.2 5.6 %collective-permute-start = (bf16[240,768]{1,0:T(8,128)(2,1)S(1)}, bf16[240,768]{1,0:T(8,128)(2,1)S(1)}, u32[]{:S(2)}, u32[]{:S(2)}) collective-permute-start(bf16[240,768]{1,0:T(8,128)(2,1)S(1)} %dynamic-slice_bitcast_fusion), channel_id=1, source_target_pairs={{0,1},{1,2},{2,3},{4,5},{5,6},{6,7},{8,9},{9,10},{10,11},{12,13},{... | collective-permute-start | bytes 1105928 | tf_op jit(solution)/shard_map/ppermute | solution.py:680
  21.8 18.1 %collective-permute-done.1 = bf16[240,768]{1,0:T(8,128)(2,1)S(1)} collective-permute-done((bf16[240,768]{1,0:T(8,128)(2,1)S(1)}, bf16[240,768]{1,0:T(8,128)(2,1)S(1)}, u32[]{:S(2)}, u32[]{:S(2)}) %collective-permute-start.1) | collective-permute-done | bytes 368672 | tf_op jit(solution)/shard_map/ppermute | solution.py:681
  41.8 19.7 %collective-permute-done.2 = bf16[240,768]{1,0:T(8,128)(2,1)S(1)} collective-permute-done((bf16[240,768]{1,0:T(8,128)(2,1)S(1)}, bf16[240,768]{1,0:T(8,128)(2,1)S(1)}, u32[]{:S(2)}, u32[]{:S(2)}) %collective-permute-start.2) | collective-permute-done | bytes 368672 | tf_op jit(solution)/shard_map/ppermute | solution.py:681
  63.7 9.6 %collective-permute-done.3 = bf16[240,768]{1,0:T(8,128)(2,1)S(1)} collective-permute-done((bf16[240,768]{1,0:T(8,128)(2,1)S(1)}, bf16[240,768]{1,0:T(8,128)(2,1)S(1)}, u32[]{:S(2)}, u32[]{:S(2)}) %collective-permute-start.3) | collective-permute-done | bytes 368672 | tf_op jit(solution)/shard_map/ppermute | solution.py:681
  81.0 12.9 %attend.2 = (bf16[2,2,3,512,512]{4,3,2,1,0:T(8,128)(2,1)}, bf16[2,3,512,512]{3,2,1,0:T(8,128)(2,1)}, bf16[2,3,3,512,64]{4,3,2,1,0:T(8,128)(2,1)}, bf16[2,512,192]{2,1,0:T(8,128)(2,1)}) custom-call(bf16[2,512,768]{2,1,0:T(8,128)(2,1)} %all-gather.3.cloned.1.call-done.tok.refs_0_, bf16[768,576]{1,0:T(8,128)(2,1)} %pad_maximum_fusion.3.w.refs_8_, ...), custom_call_target="tpu_custom_call" | custom-call | flops 2516582400 | bytes 9437184 | tf_op jit(solution)/shard_map/attend/pallas_call | solution.py:108
  97.7 14.7 %collective-permute-start.12 = (bf16[2,128,192]{2,1,0:T(8,128)(2,1)S(1)}, bf16[2,128,192]{2,1,0:T(8,128)(2,1)S(1)}, u32[]{:S(2)}, u32[]{:S(2)}) collective-permute-start(bf16[2,128,192]{2,1,0:T(8,128)(2,1)S(1)} %get-tuple-element.224), channel_id=1, source_target_pairs={{0,3},{1,0},{2,1},{3,2},{4,7},{5,4},{6,5},{7,6},{8,11},{9,8},{10,9... | collective-permute-start | bytes 294920 | tf_op jit(solution)/shard_map/ppermute | solution.py:743
  115.9 12.9 %attend.3 = (bf16[2,2,3,512,512]{4,3,2,1,0:T(8,128)(2,1)}, bf16[2,3,512,512]{3,2,1,0:T(8,128)(2,1)}, bf16[2,3,3,512,64]{4,3,2,1,0:T(8,128)(2,1)}, bf16[2,512,192]{2,1,0:T(8,128)(2,1)}) custom-call(bf16[2,512,768]{2,1,0:T(8,128)(2,1)} %all-gather.5.cloned.1.call-done.tok.refs_1_, ...), custom_call_target="tpu_custom_call", output_to_operand_aliasing={{0}: (5, {})} | custom-call | flops 2516582400 | bytes 9437184 | tf_op jit(solution)/shard_map/attend/pallas_call | solution.py:108
  128.9 3.9 %collective-permute-start.10 = (bf16[2,128,192]{2,1,0:T(8,128)(2,1)S(1)}, bf16[2,128,192]{2,1,0:T(8,128)(2,1)S(1)}, u32[]{:S(2)}, u32[]{:S(2)}) collective-permute-start(bf16[2,128,192]{2,1,0:T(8,128)(2,1)S(1)} %get-tuple-element.226), channel_id=1, source_target_pairs={{0,1},{1,2},{2,3},{3,0},{4,5},{5,6},{6,7},{7,4},{8,9},{9,10},{10,1... | collective-permute-start | bytes 294920 | tf_op jit(solution)/shard_map/ppermute | solution.py:743
  137.3 2.7 collective-permute-start.14
  140.7 2.7 collective-permute-done.15
  143.4 4.2 %collective-permute-done.14 = bf16[2,128,192]{2,1,0:T(8,128)(2,1)S(1)} collective-permute-done((bf16[2,128,192]{2,1,0:T(8,128)(2,1)S(1)}, bf16[2,128,192]{2,1,0:T(8,128)(2,1)S(1)}, u32[]{:S(2)}, u32[]{:S(2)}) %collective-permute-start.14) | collective-permute-done | bytes 98336 | tf_op jit(solution)/shard_map/ppermute | solution.py:743
  150.7 33.4 %feed_forward.1 = (bf16[512,768]{1,0:T(8,128)(2,1)}, bf16[512,3072]{1,0:T(8,128)(2,1)}, bf16[512,768]{1,0:T(8,128)(2,1)}, bf16[512,3072]{1,0:T(8,128)(2,1)}, bf1...) custom-call(s32[12]{0:T(128)} %pad_add_fusion.place, ...), custom_call_target="tpu_custom_call" | custom-call | flops 10871635968 | bytes 17301504 | tf_op jit(solution)/shard_map/feed_forward/pallas_call | solution.py:500
  188.1 5.4 %collective-permute-done.26.got = bf16[4,4,224,768]{3,2,1,0:T(8,128)(2,1)} collective-permute-done((bf16[4,4,224,768]{3,2,1,0:T(8,128)(2,1)}, bf16[4,4,224,768]{3,2,1,0:T(8,128)(2,1)}, u32[]{:S(2)}, u32[]{:S(2)}) %collective-permute-start.26) | collective-permute-done | bytes 5505056 | tf_op jit(solution)/shard_map/ppermute | solution.py:868
  193.6 8.5 %weight_grad.1 = (bf16[4,112,768]{2,1,0:T(8,128)(2,1)}, bf16[4,112,768]{2,1,0:T(8,128)(2,1)}, bf16[4,112,768]{2,1,0:T(8,128)(2,1)}, bf16[4,112,768]{2,1,0:T(8,12...) custom-call(s32[12]{0:T(128)} %pad_add_fusion.place, ...), custom_call_target="tpu_custom_call" | custom-call | flops 3019898880 | bytes 6144000 | tf_op jit(solution)/shard_map/weight_grad/pallas_call | solution.py:582
  205.7 4.5 %collective-permute-done.32 = bf16[512,192]{1,0:T(8,128)(2,1)S(1)} collective-permute-done((bf16[512,192]{1,0:T(8,128)(2,1)}, bf16[512,192]{1,0:T(8,128)(2,1)S(1)}, u32[]{:S(2)}, u32[]{:S(2)}) %collective-permute-start.32) | collective-permute-done | bytes 196640 | tf_op jit(solution)/shard_map/ppermute | solution.py:743
  212.4 23.5 %attend_back.1 = (f32[2,2,3,512,512]{4,3,2,1,0:T(8,128)}, f32[768,576]{1,0:T(8,128)}, f32[8,576]{1,0:T(8,128)}, bf16[2,512,768]{2,1,0:T(8,128)(2,1)}, bf16[2,512,768]{2,1,0:T(8,128)(2,1)}) custom-call(s32[4]{0:T(128)} %pad_add_fusion.1.place, bf16[2,512,768]{2,1,0:T(8,128)(2,1)} %all-gather.3.cloned.1.call-done.tok.refs_0_, ...), custom_call_target="tpu_custom_call" | custom-call | flops 10066329600 | bytes 25165824 | tf_op jit(solution)/shard_map/attend_back/pallas_call | solution.py:231
  237.8 3.0 hop_sum.1
  244.2 6.8 %collective-permute-done.34 = f32[24,576]{1,0:T(8,128)S(1)} collective-permute-done((f32[24,576]{1,0:T(8,128)S(1)}, f32[24,576]{1,0:T(8,128)S(1)}, u32[]{:S(2)}, u32[]{:S(2)}) %collective-permute-start.34) | collective-permute-done | bytes 55328 | tf_op jit(solution)/shard_map/ppermute | solution.py:883
  251.6 9.1 %collective-permute-done.35 = f32[24,576]{1,0:T(8,128)S(1)} collective-permute-done((f32[24,576]{1,0:T(8,128)S(1)}, f32[24,576]{1,0:T(8,128)S(1)}, u32[]{:S(2)}, u32[]{:S(2)}) %collective-permute-start.35) | collective-permute-done | bytes 55328 | tf_op jit(solution)/shard_map/ppermute | solution.py:883
  262.4 3.7 %plane_sum.1 = bf16[4,224,768]{2,1,0:T(8,128)(2,1)} custom-call(s32[4]{0:T(128)} %fusion.21.here, bf16[4,112,768]{2,1,0:T(8,128)(2,1)} %get-tuple-element.147.a0, bf16[4,112,768]{2,1,0:T(8,128)(2,1)} %copy-done.12, bf16[4,112,768]{2,1,0:T(8,128)(2,1)} %copy-done.9, bf16[4,112,768]{2,1,0:T(8,128)(2,1)} %get-tuple-element.132.b0, ...), custom_call_target="tpu_custom_call" | custom-call | tf_op jit(solution)/shard_map/plane_sum/pallas_call | solution.py:624
  266.2 6.0 %reduce-scatter.4.cloned.1.call-done = bf16[2,128,768]{2,1,0:T(8,128)(2,1)} async-done(((bf16[2,512,768]{2,1,0:T(8,128)(2,1)}), bf16[2,128,768]{2,1,0:T(8,128)(2,1)}) %reduce-scatter.4.cloned.1.call-update) | async-done | bytes 393232 | tf_op jit(solution)/shard_map/reduce_scatter | solution.py:861
  275.0 2.8 collective-permute-done.52
  281.0 5.3 %collective-permute-done.53 = bf16[200,576]{1,0:T(8,128)(2,1)S(1)} collective-permute-done((bf16[200,576]{1,0:T(8,128)(2,1)S(1)}, bf16[200,576]{1,0:T(8,128)(2,1)S(1)}, u32[]{:S(2)}, u32[]{:S(2)}) %collective-permute-start.53) | collective-permute-done | bytes 230432 | tf_op jit(solution)/shard_map/ppermute | solution.py:895
  289.8 5.1 %collective-permute-done.54 = bf16[200,576]{1,0:T(8,128)(2,1)S(1)} collective-permute-done((bf16[200,576]{1,0:T(8,128)(2,1)S(1)}, bf16[200,576]{1,0:T(8,128)(2,1)S(1)}, u32[]{:S(2)}, u32[]{:S(2)}) %collective-permute-start.54) | collective-permute-done | bytes 230432 | tf_op jit(solution)/shard_map/ppermute | solution.py:895
  296.5 9.7 %reduce-scatter.8.cloned.1.call-done = bf16[1,224,768]{2,1,0:T(8,128)(2,1)} async-done(((bf16[4,224,768]{2,1,0:T(8,128)(2,1)}), bf16[1,224,768]{2,1,0:T(8,128)(2,1)}) %reduce-scatter.8.cloned.1.call-update) | async-done | bytes 344080 | tf_op jit(solution)/shard_map/reduce_scatter | solution.py:888
  317.6 2.2 collective-permute-done.38.refs_1_
  321.8 2.2 copy.56
  324.0 2.2 copy.55
  332.2 5.1 %gather_grads.1 = (f32[768,768]{1,0:T(8,128)}, f32[8,96,768]{2,1,0:T(8,128)}, f32[12,16,768]{2,1,0:T(8,128)}) custom-call(s32[12]{0:T(128)} %pad_add_fusion.place, bf16[112,768]{1,0:T(8,128)(2,1)} %copy-done.8, bf16[112,768]{1,0:T(8,128)(2,1)} %collective-permute-done.38.refs_1_, bf16[112,768]{1,0:T(8,128)(2,1)} %collective-permute-done.39.refs_2_, ...), custom_call_target="tpu_custom_call" | custom-call | tf_op jit(solution)/shard_map/gather_grads/pallas_call | solution.py:662
  337.4 5.2 %reduce-scatter.6.cloned.1.call-done = bf16[2,128,768]{2,1,0:T(8,128)(2,1)} async-done(((bf16[2,512,768]{2,1,0:T(8,128)(2,1)}), bf16[2,128,768]{2,1,0:T(8,128)(2,1)}) %reduce-scatter.6.cloned.1.call-update) | async-done | bytes 393232 | tf_op jit(solution)/shard_map/reduce_scatter | solution.py:861
  342.6 2.3 convert_add_fusion
  (298 shorter events, 81.4 us)
Async XLA Ops:
  7.2 73.7 %all-gather.3.cloned.1.call-start = ((), (), s32[]{:S(2)}) async-start(), calls=%async_computation.3 | async-start | bytes 1966080 | tf_op jit(solution)/shard_map/all_gather | solution.py:789
  9.4 106.5 %all-gather.5.cloned.1.call-start = ((), (), s32[]{:S(2)}) async-start(), calls=%async_computation.4 | async-start | bytes 1966080 | tf_op jit(solution)/shard_map/all_gather | solution.py:789
  14.9 25.0 %collective-permute-start.1 = (bf16[240,768]{1,0:T(8,128)(2,1)S(1)}, bf16[240,768]{1,0:T(8,128)(2,1)S(1)}, u32[]{:S(2)}, u32[]{:S(2)}) collective-permute-start(bf16[240,768]{1,0:T(8,128)(2,1)S(1)} %dynamic-slice_bitcast_fusion), channel_id=1, source_target_pairs={{3,2},{2,1},{1,0},{7,6},{6,5},{5,4},{11,10},{10,9},{9,8},{15,14},{... | collective-permute-start | bytes 1105928 | tf_op jit(solution)/shard_map/ppermute | solution.py:681
  16.2 25.0 %collective-permute-start = (bf16[240,768]{1,0:T(8,128)(2,1)S(1)}, bf16[240,768]{1,0:T(8,128)(2,1)S(1)}, u32[]{:S(2)}, u32[]{:S(2)}) collective-permute-start(bf16[240,768]{1,0:T(8,128)(2,1)S(1)} %dynamic-slice_bitcast_fusion), channel_id=1, source_target_pairs={{0,1},{1,2},{2,3},{4,5},{5,6},{6,7},{8,9},{9,10},{10,11},{12,13},{... | collective-permute-start | bytes 1105928 | tf_op jit(solution)/shard_map/ppermute | solution.py:680
  39.9 21.7 %collective-permute-start.2 = (bf16[240,768]{1,0:T(8,128)(2,1)S(1)}, bf16[240,768]{1,0:T(8,128)(2,1)S(1)}, u32[]{:S(2)}, u32[]{:S(2)}) collective-permute-start(bf16[240,768]{1,0:T(8,128)(2,1)S(1)} %collective-permute-done.1), channel_id=1, source_target_pairs={{2,1},{1,0},{6,5},{5,4},{10,9},{9,8},{14,13},{13,12},{18,17},{17,1... | collective-permute-start | bytes 1105928 | tf_op jit(solution)/shard_map/ppermute | solution.py:681
  41.2 20.4 %collective-permute-start.4 = (bf16[240,768]{1,0:T(8,128)(2,1)S(1)}, bf16[240,768]{1,0:T(8,128)(2,1)S(1)}, u32[]{:S(2)}, u32[]{:S(2)}) collective-permute-start(bf16[240,768]{1,0:T(8,128)(2,1)S(1)} %collective-permute-done), channel_id=1, source_target_pairs={{1,2},{2,3},{5,6},{6,7},{9,10},{10,11},{13,14},{14,15},{17,18},{18... | collective-permute-start | bytes 1105928 | tf_op jit(solution)/shard_map/ppermute | solution.py:680
  61.6 210.6 %reduce-scatter.4.cloned.1.call-start = ((), (), s32[]{:S(2)}) async-start(), calls=%async_computation.5 | async-start | bytes 1966080 | tf_op jit(solution)/shard_map/reduce_scatter | solution.py:861
  73.6 20.4 %collective-permute-start.6 = (bf16[3,128,768]{2,1,0:T(8,128)(2,1)S(1)}, bf16[3,128,768]{2,1,0:T(8,128)(2,1)S(1)}, u32[]{:S(2)}, u32[]{:S(2)}) collective-permute-start(bf16[3,128,768]{2,1,0:T(8,128)(2,1)S(1)} %slice.132.refs_12_), channel_id=1, source_target_pairs={{0,8},{4,12},{8,0},{12,4},{16,24},{20,28},{24,16},{28,20},{1,9},{5... | collective-permute-start | bytes 1769480 | tf_op jit(solution)/shard_map/ppermute | solution.py:635
  75.7 18.1 %collective-permute-start.7 = (bf16[3,112,768]{2,1,0:T(8,128)(2,1)S(1)}, bf16[3,112,768]{2,1,0:T(8,128)(2,1)}, u32[]{:S(2)}, u32[]{:S(2)}) collective-permute-start(bf16[3,112,768]{2,1,0:T(8,128)(2,1)S(1)} %pad_maximum_fusion.4.refs_20_), channel_id=1, source_target_pairs={{0,16},{4,20},{8,24},{12,28},{16,0},{20,4},{24,8},{28,12},{1,17},{... | collective-permute-start | bytes 1548296 | tf_op jit(solution)/shard_map/ppermute | solution.py:635
  77.0 20.7 %collective-permute-start.22 = (bf16[3,112,768]{2,1,0:T(8,128)(2,1)S(1)}, bf16[3,112,768]{2,1,0:T(8,128)(2,1)}, u32[]{:S(2)}, u32[]{:S(2)}) collective-permute-start(bf16[3,112,768]{2,1,0:T(8,128)(2,1)S(1)} %pad_maximum_fusion.4.refs_20_), channel_id=1, source_target_pairs={{0,4},{4,0},{8,12},{12,8},{16,20},{20,16},{24,28},{28,24},{1,5},{5... | collective-permute-start | bytes 1548296 | tf_op jit(solution)/shard_map/ppermute | solution.py:836
  77.0 36.8 %collective-permute-start.17 = (bf16[3,128,768]{2,1,0:T(8,128)(2,1)S(1)}, bf16[3,128,768]{2,1,0:T(8,128)(2,1)}, u32[]{:S(2)}, u32[]{:S(2)}) collective-permute-start(bf16[3,128,768]{2,1,0:T(8,128)(2,1)S(1)} %slice.132.refs_12_), channel_id=1, source_target_pairs={{0,4},{4,0},{8,12},{12,8},{16,20},{20,16},{24,28},{28,24},{1,5},{5... | collective-permute-start | bytes 1769480 | tf_op jit(solution)/shard_map/ppermute | solution.py:836
  78.8 33.6 %collective-permute-start.21 = (bf16[3,112,768]{2,1,0:T(8,128)(2,1)S(1)}, bf16[3,112,768]{2,1,0:T(8,128)(2,1)}, u32[]{:S(2)}, u32[]{:S(2)}) collective-permute-start(bf16[3,112,768]{2,1,0:T(8,128)(2,1)S(1)} %pad_maximum_fusion.4.refs_20_), channel_id=1, source_target_pairs={{0,8},{4,12},{8,0},{12,4},{16,24},{20,28},{24,16},{28,20},{1,9},{5... | collective-permute-start | bytes 1548296 | tf_op jit(solution)/shard_map/ppermute | solution.py:636
  93.8 46.2 %collective-permute-start.16 = (bf16[3,128,768]{2,1,0:T(8,128)(2,1)S(1)}, bf16[3,128,768]{2,1,0:T(8,128)(2,1)S(1)}, u32[]{:S(2)}, u32[]{:S(2)}) collective-permute-start(bf16[3,128,768]{2,1,0:T(8,128)(2,1)S(1)} %slice.132.refs_12_), channel_id=1, source_target_pairs={{0,16},{4,20},{8,24},{12,28},{16,0},{20,4},{24,8},{28,12},{1,17},{... | collective-permute-start | bytes 1769480 | tf_op jit(solution)/shard_map/ppermute | solution.py:636
  94.0 46.0 %collective-permute-start.8 = (bf16[3,128,768]{2,1,0:T(8,128)(2,1)S(1)}, bf16[3,128,768]{2,1,0:T(8,128)(2,1)}, u32[]{:S(2)}, u32[]{:S(2)}) collective-permute-start(bf16[3,128,768]{2,1,0:T(8,128)(2,1)S(1)} %collective-permute-done.6.refs_13_), channel_id=1, source_target_pairs={{0,16},{4,20},{8,24},{12,28},{16,0},{20,4},{24,8},{28,12},{1,17},{... | collective-permute-start | bytes 1769480 | tf_op jit(solution)/shard_map/ppermute | solution.py:638
  97.7 17.2 %collective-permute-start.12 = (bf16[2,128,192]{2,1,0:T(8,128)(2,1)S(1)}, bf16[2,128,192]{2,1,0:T(8,128)(2,1)S(1)}, u32[]{:S(2)}, u32[]{:S(2)}) collective-permute-start(bf16[2,128,192]{2,1,0:T(8,128)(2,1)S(1)} %get-tuple-element.224), channel_id=1, source_target_pairs={{0,3},{1,0},{2,1},{3,2},{4,7},{5,4},{6,5},{7,6},{8,11},{9,8},{10,9... | collective-permute-start | bytes 294920 | tf_op jit(solution)/shard_map/ppermute | solution.py:743
  112.4 24.9 %collective-permute-start.9 = (bf16[3,112,768]{2,1,0:T(8,128)(2,1)}, bf16[3,112,768]{2,1,0:T(8,128)(2,1)S(1)}, u32[]{:S(2)}, u32[]{:S(2)}) collective-permute-start(bf16[3,112,768]{2,1,0:T(8,128)(2,1)} %collective-permute-done.7.refs_22_), channel_id=1, source_target_pairs={{0,8},{4,12},{8,0},{12,4},{16,24},{20,28},{24,16},{28,20},{1,9},{5... | collective-permute-start | bytes 1548296 | tf_op jit(solution)/shard_map/ppermute | solution.py:638
  113.9 26.2 %collective-permute-start.23 = (bf16[3,112,768]{2,1,0:T(8,128)(2,1)}, bf16[3,112,768]{2,1,0:T(8,128)(2,1)}, u32[]{:S(2)}, u32[]{:S(2)}) collective-permute-start(bf16[3,112,768]{2,1,0:T(8,128)(2,1)} %collective-permute-done.21.refs_21_), channel_id=1, source_target_pairs={{0,4},{4,0},{8,12},{12,8},{16,20},{20,16},{24,28},{28,24},{1,5},{5... | collective-permute-start | bytes 1548296 | tf_op jit(solution)/shard_map/ppermute | solution.py:836
  185.2 19.0 %collective-permute-start.31 = (bf16[512,192]{1,0:T(8,128)(2,1)}, bf16[512,192]{1,0:T(8,128)(2,1)S(1)}, u32[]{:S(2)}, u32[]{:S(2)}) collective-permute-start(bf16[512,192]{1,0:T(8,128)(2,1)} %get-tuple-element.134), channel_id=1, source_target_pairs={{0,3},{1,0},{2,1},{3,2},{4,7},{5,4},{6,5},{7,6},{8,11},{9,8},{10,9... | collective-permute-start | bytes 589832 | tf_op jit(solution)/shard_map/ppermute | solution.py:743
  186.1 24.0 %collective-permute-start.32 = (bf16[512,192]{1,0:T(8,128)(2,1)}, bf16[512,192]{1,0:T(8,128)(2,1)S(1)}, u32[]{:S(2)}, u32[]{:S(2)}) collective-permute-start(bf16[512,192]{1,0:T(8,128)(2,1)} %get-tuple-element.135), channel_id=1, source_target_pairs={{0,2},{1,3},{2,0},{3,1},{4,6},{5,7},{6,4},{7,5},{8,10},{9,11},{10,... | collective-permute-start | bytes 589832 | tf_op jit(solution)/shard_map/ppermute | solution.py:743
  186.1 25.5 %collective-permute-start.33 = (bf16[512,192]{1,0:T(8,128)(2,1)}, bf16[512,192]{1,0:T(8,128)(2,1)S(1)}, u32[]{:S(2)}, u32[]{:S(2)}) collective-permute-start(bf16[512,192]{1,0:T(8,128)(2,1)} %get-tuple-element.136), channel_id=1, source_target_pairs={{0,1},{1,2},{2,3},{3,0},{4,5},{5,6},{6,7},{7,4},{8,9},{9,10},{10,1... | collective-permute-start | bytes 589832 | tf_op jit(solution)/shard_map/ppermute | solution.py:743
  202.1 33.9 %collective-permute-start.27 = (bf16[4,112,768]{2,1,0:T(8,128)(2,1)}, bf16[4,112,768]{2,1,0:T(8,128)(2,1)S(1)}, u32[]{:S(2)}, u32[]{:S(2)}) collective-permute-start(bf16[4,112,768]{2,1,0:T(8,128)(2,1)} %get-tuple-element.121), channel_id=1, source_target_pairs={{0,16},{4,20},{8,24},{12,28},{16,0},{20,4},{24,8},{28,12},{1,17},{... | collective-permute-start | bytes 2064392 | tf_op jit(solution)/shard_map/ppermute | solution.py:875
  202.7 33.2 %collective-permute-start.28 = (bf16[4,112,768]{2,1,0:T(8,128)(2,1)}, bf16[4,112,768]{2,1,0:T(8,128)(2,1)S(1)}, u32[]{:S(2)}, u32[]{:S(2)}) collective-permute-start(bf16[4,112,768]{2,1,0:T(8,128)(2,1)} %get-tuple-element.122), channel_id=1, source_target_pairs={{0,16},{4,20},{8,24},{12,28},{16,0},{20,4},{24,8},{28,12},{1,17},{... | collective-permute-start | bytes 2064392 | tf_op jit(solution)/shard_map/ppermute | solution.py:874
  204.2 31.8 %collective-permute-start.29 = (bf16[4,112,768]{2,1,0:T(8,128)(2,1)}, bf16[4,112,768]{2,1,0:T(8,128)(2,1)S(1)}, u32[]{:S(2)}, u32[]{:S(2)}) collective-permute-start(bf16[4,112,768]{2,1,0:T(8,128)(2,1)} %get-tuple-element.123), channel_id=1, source_target_pairs={{0,8},{4,12},{8,0},{12,4},{16,24},{20,28},{24,16},{28,20},{1,9},{5... | collective-permute-start | bytes 2064392 | tf_op jit(solution)/shard_map/ppermute | solution.py:875
  210.1 26.1 %collective-permute-start.30 = (bf16[4,112,768]{2,1,0:T(8,128)(2,1)}, bf16[4,112,768]{2,1,0:T(8,128)(2,1)S(1)}, u32[]{:S(2)}, u32[]{:S(2)}) collective-permute-start(bf16[4,112,768]{2,1,0:T(8,128)(2,1)} %get-tuple-element.124), channel_id=1, source_target_pairs={{0,8},{4,12},{8,0},{12,4},{16,24},{20,28},{24,16},{28,20},{1,9},{5... | collective-permute-start | bytes 2064392 | tf_op jit(solution)/shard_map/ppermute | solution.py:874
  236.3 69.9 %reduce-scatter.8.cloned.1.call-start = ((), (), s32[]{:S(2)}) async-start(), calls=%async_computation.7 | async-start | bytes 1720320 | tf_op jit(solution)/shard_map/reduce_scatter | solution.py:888
  240.8 20.0 %collective-permute-start.37 = (bf16[4,112,768]{2,1,0:T(8,128)(2,1)}, bf16[4,112,768]{2,1,0:T(8,128)(2,1)S(1)}, u32[]{:S(2)}, u32[]{:S(2)}) collective-permute-start(bf16[4,112,768]{2,1,0:T(8,128)(2,1)} %get-tuple-element.150), channel_id=1, source_target_pairs={{0,16},{4,20},{8,24},{12,28},{16,0},{20,4},{24,8},{28,12},{1,17},{... | collective-permute-start | bytes 2064392 | tf_op jit(solution)/shard_map/ppermute | solution.py:881
  241.3 19.4 %collective-permute-start.36 = (bf16[4,112,768]{2,1,0:T(8,128)(2,1)}, bf16[4,112,768]{2,1,0:T(8,128)(2,1)S(1)}, u32[]{:S(2)}, u32[]{:S(2)}) collective-permute-start(bf16[4,112,768]{2,1,0:T(8,128)(2,1)} %get-tuple-element.145), channel_id=1, source_target_pairs={{0,8},{4,12},{8,0},{12,4},{16,24},{20,28},{24,16},{28,20},{1,9},{5... | collective-permute-start | bytes 2064392 | tf_op jit(solution)/shard_map/ppermute | solution.py:881
  272.2 70.4 %reduce-scatter.6.cloned.1.call-start = ((), (), s32[]{:S(2)}) async-start(), calls=%async_computation.6 | async-start | bytes 1966080 | tf_op jit(solution)/shard_map/reduce_scatter | solution.py:861
  296.4 14.5 %collective-permute-start.57 = (f32[400,576]{1,0:T(8,128)S(1)}, f32[400,576]{1,0:T(8,128)}, u32[]{:S(2)}, u32[]{:S(2)}) collective-permute-start(f32[400,576]{1,0:T(8,128)S(1)} %pad_maximum_fusion.2), channel_id=1, source_target_pairs={{0,4},{4,0},{8,12},{12,8},{16,20},{20,16},{24,28},{28,24},{1,5},{5... | collective-permute-start | bytes 2764808 | tf_op jit(solution)/shard_map/ppermute | solution.py:901
  312.6 15.9 %collective-permute-start.41 = (bf16[112,768]{1,0:T(8,128)(2,1)S(1)}, bf16[112,768]{1,0:T(8,128)(2,1)}, u32[]{:S(2)}, u32[]{:S(2)}) collective-permute-start(bf16[112,768]{1,0:T(8,128)(2,1)S(1)} %get-tuple-element.229.refs_0_), channel_id=1, source_target_pairs={{0,4},{4,0},{8,12},{12,8},{16,20},{20,16},{24,28},{28,24},{1,5},{5... | collective-permute-start | bytes 516104 | tf_op jit(solution)/shard_map/ppermute | solution.py:899
  312.7 15.8 %collective-permute-start.39 = (bf16[112,768]{1,0:T(8,128)(2,1)S(1)}, bf16[112,768]{1,0:T(8,128)(2,1)}, u32[]{:S(2)}, u32[]{:S(2)}) collective-permute-start(bf16[112,768]{1,0:T(8,128)(2,1)S(1)} %get-tuple-element.229.refs_0_), channel_id=1, source_target_pairs={{0,16},{4,20},{8,24},{12,28},{16,0},{20,4},{24,8},{28,12},{1,17},{... | collective-permute-start | bytes 516104 | tf_op jit(solution)/shard_map/ppermute | solution.py:636
  314.2 14.8 %collective-permute-start.50 = (bf16[112,768]{1,0:T(8,128)(2,1)}, bf16[112,768]{1,0:T(8,128)(2,1)}, u32[]{:S(2)}, u32[]{:S(2)}) collective-permute-start(bf16[112,768]{1,0:T(8,128)(2,1)} %collective-permute-done.46.refs_10_), channel_id=1, source_target_pairs={{0,4},{4,0},{8,12},{12,8},{16,20},{20,16},{24,28},{28,24},{1,5},{5... | collective-permute-start | bytes 516104 | tf_op jit(solution)/shard_map/ppermute | solution.py:900
  (82 other events, 685.1 us)
Sparse Core Ops, SparseCore 0:
  10.2 50.6 all-gather.2
  63.0 38.2 all-gather.4
  236.4 35.7 reduce-scatter.3
  274.9 31.2 reduce-scatter.7
  308.4 34.1 reduce-scatter.5
